TPU v7x, 32 devices: a whole 2x2x4 slice. The times are simulated.
32 devices in a mesh: dp: 8 (over z, x), mp: 4 (over y, core).
Axes of the slice: x: 2, y: 2, z: 4, core: 2. Of those that a mesh axis runs over, the one named last changes fastest.
Arguments:
- tokens: bfloat16 [4096, 1024], P('dp'), may hold values from -6 to 6
- memory: bfloat16 [8192, 1024], P('dp'), may hold values from -6 to 6
- segment_ids: int32 [8, 512], P('dp'), may hold values from 0 to 7, never falling along the last dimension, each value on 1 to 256 neighbouring positions
- answer_ids: int32 [8, 512], P('dp'), may hold values from 0 to 50264
- loss_mask: int32 [8, 512], P('dp'), may hold values 0 or 1
- doc_scores: float32 [16, 4], replicated, may hold values from -5 to 5
- slot_place: int32 [64], replicated, may hold values from 0 to 63, each once
- self_query: bfloat16 [1024, 1024], P(None, 'mp'), may hold values from -0.25 to 0.25
- self_key: bfloat16 [1024, 1024], P(None, 'mp'), may hold values from -0.25 to 0.25
- self_value: bfloat16 [1024, 1024], P(None, 'mp'), may hold values from -0.1875 to 0.1875
- self_out: bfloat16 [1024, 1024], P('mp'), may hold values from -0.75 to 0.75
- cross_query: bfloat16 [1024, 1024], P(None, 'mp'), may hold values from -0.25 to 0.25
- cross_key: bfloat16 [1024, 1024], P(None, 'mp'), may hold values from -0.25 to 0.25
- cross_value: bfloat16 [1024, 1024], P(None, 'mp'), may hold values from -0.1875 to 0.1875
- cross_out: bfloat16 [1024, 1024], P('mp'), may hold values from -1 to 1
- feed_up: bfloat16 [1024, 4096], P(None, 'mp'), may hold values from -0.1875 to 0.1875
- feed_down: bfloat16 [4096, 1024], P('mp'), may hold values from -0.09375 to 0.09375
- gain_self: float32 [1024], replicated, may hold values from 0.5 to 1.5
- shift_self: float32 [1024], replicated, may hold values from -1.5 to 1.5
- gain_cross: float32 [1024], replicated, may hold values from 0.5 to 1.5
- shift_cross: float32 [1024], replicated, may hold values from -1.5 to 1.5
- gain_feed: float32 [1024], replicated, may hold values from 0.5 to 1.5
- shift_feed: float32 [1024], replicated, may hold values from -1.5 to 1.5
- embedding: bfloat16 [51200, 1024], P('mp', 'dp'), may hold values from -0.5 to 0.5
Outputs:
- loss: float32 [], replicated
- tokens_grad: float32 [4096, 1024], P('dp', 'mp')
- memory_grad: float32 [8192, 1024], P('dp', 'mp')
- self_query_grad: float32 [1024, 1024], P(None, 'mp')
- self_key_grad: float32 [1024, 1024], P(None, 'mp')
- self_value_grad: float32 [1024, 1024], P(None, 'mp')
- self_out_grad: float32 [1024, 1024], P('mp')
- cross_query_grad: float32 [1024, 1024], P(None, 'mp')
- cross_key_grad: float32 [1024, 1024], P(None, 'mp')
- cross_value_grad: float32 [1024, 1024], P(None, 'mp')
- cross_out_grad: float32 [1024, 1024], P('mp')
- feed_up_grad: float32 [1024, 4096], P(None, 'mp')
- feed_down_grad: float32 [4096, 1024], P('mp')
- gain_self_grad: float32 [1024], replicated
- shift_self_grad: float32 [1024], replicated
- gain_cross_grad: float32 [1024], replicated
- shift_cross_grad: float32 [1024], replicated
- gain_feed_grad: float32 [1024], replicated
- shift_feed_grad: float32 [1024], replicated
- embedding_grad: float32 [51200, 1024], P('mp', 'dp')
- scores_grad: float32 [16, 4], replicated
Inputs may be any that keep to these rules, and one draw needn't show every extreme that they name: `segment_ids`: segment numbers never fall along a row and every number of 0 to 7 occurs in every row. `slot_place`: every number of 0 to 63 occurs exactly once; entry q * 4 + k names the global segment r * 8 + s that decodes passage slot k of question q.
All inputs are finite; a program needn't handle non-finite values. No bound on the sum of `loss_mask` on one device may be relied on, other than what follows from the above.
Results may differ from a plain program's by a relative error of at most 0.03.
The roundings to bfloat16 on the way count: a program that leaves them out, or rounds other values in their place, can miss the bound.
Values may be sent and summed in bfloat16 or wider, within the bound.
A program may use at most 256 MiB of HBM per device.

v0:
```python
import jax
import jax.numpy as jnp
from jax import lax
from jax.sharding import PartitionSpec as P

HEAD_DIM = 64
SEG_ROW = 8
MEM = 128


masked_score = -1e30
norm_eps = 1e-05
highest = lax.Precision.HIGHEST


def product(left_side, right_side):
    return jnp.dot(left_side, right_side, preferred_element_type=jnp.float32)


def product_tn(left_side, right_side):
    return lax.dot_general(
        left_side, right_side, (((0,), (0,)), ((), ())), preferred_element_type=jnp.float32
    )


def product_nt(left_side, right_side):
    return lax.dot_general(
        left_side, right_side, (((1,), (1,)), ((), ())), preferred_element_type=jnp.float32
    )


def layer_norm(inputs, gain_vec, shift_vec):
    center = inputs - jnp.mean(inputs, axis=-1, keepdims=True)
    spread = jnp.mean(center * center, axis=-1, keepdims=True)
    return center * lax.rsqrt(spread + norm_eps) * gain_vec + shift_vec


def norm_back(residual, gain_vec, shift_vec, grad_out):
    outputs, pullback = jax.vjp(layer_norm, residual, gain_vec, shift_vec)
    return pullback(grad_out)


def gelu_exact(inputs):
    return jax.nn.gelu(inputs, approximate=False)


def split_heads(matrix):
    return matrix.reshape(matrix.shape[0], matrix.shape[1] // HEAD_DIM, HEAD_DIM)


def attention_scores(queries, keys, allowed):
    scores = jnp.einsum(
        "qhd,khd->hqk", split_heads(queries), split_heads(keys), preferred_element_type=jnp.float32
    ) * HEAD_DIM ** (-0.5)
    return jnp.where(allowed[None], scores, masked_score)


def attend_forward(queries, keys, values, allowed):
    scores = attention_scores(queries, keys, allowed)
    largest = jnp.max(scores, axis=-1, keepdims=True)
    weights = jnp.exp(scores - largest)
    total = jnp.sum(weights, axis=-1, keepdims=True)
    probabilities = (weights / total).astype(jnp.bfloat16)
    mixed_out = jnp.einsum(
        "hqk,khd->qhd", probabilities, split_heads(values), preferred_element_type=jnp.float32
    )
    return (mixed_out.reshape(queries.shape[0], queries.shape[1]), largest + jnp.log(total))


def attend_backward(queries, keys, values, allowed, log_total, grad_out):
    scores = attention_scores(queries, keys, allowed)
    probabilities = jnp.exp(scores - log_total)
    heads_grad = split_heads(grad_out)
    grad_prob = jnp.einsum(
        "qhd,khd->hqk", heads_grad, split_heads(values), preferred_element_type=jnp.float32
    )
    grad_values = jnp.einsum(
        "hqk,qhd->khd",
        probabilities.astype(jnp.bfloat16),
        heads_grad,
        preferred_element_type=jnp.float32,
    )
    row_dot = jnp.sum(grad_prob * probabilities, axis=-1, keepdims=True)
    grad_scores = (probabilities * (grad_prob - row_dot)).astype(jnp.bfloat16)
    grad_queries = jnp.einsum(
        "hqk,khd->qhd", grad_scores, split_heads(keys), preferred_element_type=jnp.float32
    ) * HEAD_DIM ** (-0.5)
    grad_keys = jnp.einsum(
        "hqk,qhd->khd", grad_scores, split_heads(queries), preferred_element_type=jnp.float32
    ) * HEAD_DIM ** (-0.5)
    width = queries.shape[1]
    return (
        grad_queries.reshape(-1, width).astype(jnp.bfloat16),
        grad_keys.reshape(-1, width).astype(jnp.bfloat16),
        grad_values.reshape(-1, width).astype(jnp.bfloat16),
    )


def run_rows(queries, keys, values, masks):
    mixed_out, log_total = attend_forward(queries, keys, values, masks[0])
    totals = [log_total]
    return (mixed_out.astype(jnp.bfloat16), totals)


def back_rows(queries, keys, values, masks, totals, grad_mix):
    parts_query, parts_key, parts_value = ([], [], [])
    grad_query, grad_key, grad_value = attend_backward(
        queries, keys, values, masks[0], totals[0], grad_mix
    )
    parts_query.append(grad_query)
    parts_key.append(grad_key)
    parts_value.append(grad_value)
    return (parts_query[0], parts_key[0], parts_value[0])


def join_heads(partial_value):
    return lax.psum(partial_value, "mp")


def join_grads(partial_value):
    return lax.psum(partial_value, "mp")


def local(
    tokens,
    memory,
    segment_ids,
    answer_ids,
    loss_mask,
    doc_scores,
    slot_place,
    self_query,
    self_key,
    self_value,
    self_out,
    cross_query,
    cross_key,
    cross_value,
    cross_out,
    feed_up,
    feed_down,
    gain_self,
    shift_self,
    gain_cross,
    shift_cross,
    gain_feed,
    shift_feed,
    embedding,
):
    row_count, row_len = segment_ids.shape
    span = SEG_ROW * MEM
    inputs = tokens.astype(jnp.float32)
    keeper = loss_mask.astype(jnp.float32).reshape(-1)
    places = jnp.arange(row_len, dtype=jnp.int32)
    owners = jnp.arange(span, dtype=jnp.int32) // MEM
    self_masks = [
        (segment_ids[0][:, None] == segment_ids[0][None, :]) & (places[None, :] <= places[:, None])
    ]
    cross_masks = [segment_ids[0][:, None] == owners[None, :]]
    query_self = product(tokens, self_query).astype(jnp.bfloat16)
    key_self = product(tokens, self_key).astype(jnp.bfloat16)
    value_self = product(tokens, self_value).astype(jnp.bfloat16)
    self_mix, self_totals = run_rows(query_self, key_self, value_self, self_masks)
    branch_self = join_heads(product(self_mix, self_out))
    first_norm = layer_norm(inputs + branch_self, gain_self, shift_self)
    first_low = first_norm.astype(jnp.bfloat16)
    query_cross = product(first_low, cross_query).astype(jnp.bfloat16)
    key_cross = product(memory, cross_key).astype(jnp.bfloat16)
    value_cross = product(memory, cross_value).astype(jnp.bfloat16)
    cross_mix, cross_totals = run_rows(query_cross, key_cross, value_cross, cross_masks)
    branch_cross = join_heads(product(cross_mix, cross_out))
    second_norm = layer_norm(first_norm + branch_cross, gain_cross, shift_cross)
    second_low = second_norm.astype(jnp.bfloat16)
    feed_pre = product(second_low, feed_up)
    feed_act = gelu_exact(feed_pre).astype(jnp.bfloat16)
    branch_feed = join_heads(product(feed_act, feed_down))
    third_norm = layer_norm(second_norm + branch_feed, gain_feed, shift_feed)
    third_low = third_norm.astype(jnp.bfloat16)
    vocab_local = embedding.shape[0]
    logits = product_nt(third_low, lax.all_gather(embedding, "dp", axis=1, tiled=True))
    offset = lax.axis_index("mp") * vocab_local
    local_target = answer_ids.reshape(-1) - offset
    inside = (local_target >= 0) & (local_target < vocab_local)
    clipped = jnp.clip(local_target, 0, vocab_local - 1)
    picked_part = jnp.where(
        inside, jnp.take_along_axis(logits, clipped[:, None], axis=1)[:, 0], 0.0
    )
    local_top = jnp.max(logits, axis=1)
    global_top = lax.pmax(local_top, "mp")
    global_sum, picked = lax.psum(
        (jnp.sum(jnp.exp(logits - global_top[:, None]), axis=1), picked_part), "mp"
    )
    log_total = global_top + jnp.log(global_sum)
    token_logp = (picked - log_total) * keeper
    seg_local = row_count * SEG_ROW
    local_ids = (segment_ids + (jnp.arange(row_count, dtype=jnp.int32) * SEG_ROW)[:, None]).reshape(
        -1
    )
    seg_hot = (local_ids[:, None] == jnp.arange(seg_local, dtype=jnp.int32)[None, :]).astype(
        jnp.float32
    )
    seg_sums = jnp.sum(seg_hot * token_logp[:, None], axis=0)
    counts = jnp.sum(seg_hot * keeper[:, None], axis=0)
    likely_local = seg_sums / jnp.maximum(counts, 1.0)
    likely_all = lax.all_gather(likely_local, "dp", axis=0, tiled=True)
    place_hot = (
        slot_place[:, None] == jnp.arange(likely_all.shape[0], dtype=jnp.int32)[None, :]
    ).astype(jnp.float32)

    def marginal(scores, likely):
        joint_score = jax.nn.log_softmax(scores, axis=1) + jnp.dot(
            place_hot, likely, precision=highest
        ).reshape(scores.shape)
        return -jnp.sum(jax.nn.logsumexp(joint_score, axis=1))

    loss, pullback = jax.vjp(marginal, doc_scores, likely_all)
    grad_scores, grad_likely = pullback(jnp.ones_like(loss))
    per_segment = lax.dynamic_slice_in_dim(
        grad_likely, lax.axis_index("dp") * seg_local, seg_local
    ) / jnp.maximum(counts, 1.0)
    grad_logp = jnp.dot(seg_hot, per_segment, precision=highest) * keeper
    probabilities = jnp.exp(logits - log_total[:, None])
    vocab_ids = jnp.arange(vocab_local, dtype=jnp.int32)
    grad_logits = (
        grad_logp[:, None]
        * ((local_target[:, None] == vocab_ids[None, :]).astype(jnp.float32) - probabilities)
    ).astype(jnp.bfloat16)
    grad_third = join_grads(
        product(grad_logits, lax.all_gather(embedding, "dp", axis=1, tiled=True))
    )
    grad_table = (
        lax.psum_scatter(
            product_tn(third_low, grad_logits).astype(jnp.bfloat16),
            "dp",
            scatter_dimension=0,
            tiled=True,
        )
        .astype(jnp.float32)
        .T
    )
    grad_res3, grad_gain_feed, grad_shift_feed = norm_back(
        second_norm + branch_feed, gain_feed, shift_feed, grad_third
    )
    grad_branch = grad_res3.astype(jnp.bfloat16)
    grad_feed_down = product_tn(feed_act, grad_branch)
    grad_act = product_nt(grad_branch, feed_down)
    act_value, act_pull = jax.vjp(gelu_exact, feed_pre)
    grad_pre = act_pull(grad_act)[0].astype(jnp.bfloat16)
    grad_feed_up = product_tn(second_low, grad_pre)
    grad_second = grad_res3 + join_grads(product_nt(grad_pre, feed_up))
    grad_res2, grad_gain_cross, grad_shift_cross = norm_back(
        first_norm + branch_cross, gain_cross, shift_cross, grad_second
    )
    grad_branch = grad_res2.astype(jnp.bfloat16)
    grad_cross_out = product_tn(cross_mix, grad_branch)
    grad_mix = product_nt(grad_branch, cross_out).astype(jnp.bfloat16)
    cross_gq, cross_gk, cross_gv = back_rows(
        query_cross, key_cross, value_cross, cross_masks, cross_totals, grad_mix
    )
    grad_cross_query = product_tn(first_low, cross_gq)
    grad_cross_key = product_tn(memory, cross_gk)
    grad_cross_value = product_tn(memory, cross_gv)
    grad_memory_part = product_nt(cross_gk, cross_key) + product_nt(cross_gv, cross_value)
    grad_first = grad_res2 + join_grads(product_nt(cross_gq, cross_query))
    grad_res1, grad_gain_self, grad_shift_self = norm_back(
        inputs + branch_self, gain_self, shift_self, grad_first
    )
    grad_branch = grad_res1.astype(jnp.bfloat16)
    grad_self_out = product_tn(self_mix, grad_branch)
    grad_mix = product_nt(grad_branch, self_out).astype(jnp.bfloat16)
    self_gq, self_gk, self_gv = back_rows(
        query_self, key_self, value_self, self_masks, self_totals, grad_mix
    )
    grad_self_query = product_tn(tokens, self_gq)
    grad_self_key = product_tn(tokens, self_gk)
    grad_self_value = product_tn(tokens, self_gv)
    grad_input_part = (
        product_nt(self_gq, self_query)
        + product_nt(self_gk, self_key)
        + product_nt(self_gv, self_value)
    )
    input_share, memory_share = (
        lax.psum_scatter(
            grad_input_part.astype(jnp.bfloat16), "mp", scatter_dimension=1, tiled=True
        ).astype(jnp.float32),
        lax.psum_scatter(
            grad_memory_part.astype(jnp.bfloat16), "mp", scatter_dimension=1, tiled=True
        ).astype(jnp.float32),
    )
    column_start = lax.axis_index("mp") * input_share.shape[1]
    grad_tokens = input_share + lax.dynamic_slice_in_dim(
        grad_res1, column_start, input_share.shape[1], 1
    )
    (
        sum_sq,
        sum_sk,
        sum_sv,
        sum_so,
        sum_cq,
        sum_ck,
        sum_cv,
        sum_co,
        sum_up,
        sum_down,
        sum_gs,
        sum_ss,
        sum_gc,
        sum_sc,
        sum_gf,
        sum_sf,
    ) = (
        lax.psum(grad_self_query.astype(jnp.bfloat16), "dp").astype(jnp.float32),
        lax.psum(grad_self_key.astype(jnp.bfloat16), "dp").astype(jnp.float32),
        lax.psum(grad_self_value.astype(jnp.bfloat16), "dp").astype(jnp.float32),
        lax.psum(grad_self_out.astype(jnp.bfloat16), "dp").astype(jnp.float32),
        lax.psum(grad_cross_query.astype(jnp.bfloat16), "dp").astype(jnp.float32),
        lax.psum(grad_cross_key.astype(jnp.bfloat16), "dp").astype(jnp.float32),
        lax.psum(grad_cross_value.astype(jnp.bfloat16), "dp").astype(jnp.float32),
        lax.psum(grad_cross_out.astype(jnp.bfloat16), "dp").astype(jnp.float32),
        lax.psum(grad_feed_up.astype(jnp.bfloat16), "dp").astype(jnp.float32),
        lax.psum(grad_feed_down.astype(jnp.bfloat16), "dp").astype(jnp.float32),
        lax.psum(grad_gain_self.astype(jnp.bfloat16), "dp").astype(jnp.float32),
        lax.psum(grad_shift_self.astype(jnp.bfloat16), "dp").astype(jnp.float32),
        lax.psum(grad_gain_cross.astype(jnp.bfloat16), "dp").astype(jnp.float32),
        lax.psum(grad_shift_cross.astype(jnp.bfloat16), "dp").astype(jnp.float32),
        lax.psum(grad_gain_feed.astype(jnp.bfloat16), "dp").astype(jnp.float32),
        lax.psum(grad_shift_feed.astype(jnp.bfloat16), "dp").astype(jnp.float32),
    )
    return (
        loss,
        grad_tokens,
        memory_share,
        sum_sq,
        sum_sk,
        sum_sv,
        sum_so,
        sum_cq,
        sum_ck,
        sum_cv,
        sum_co,
        sum_up,
        sum_down,
        sum_gs,
        sum_ss,
        sum_gc,
        sum_sc,
        sum_gf,
        sum_sf,
        grad_table,
        grad_scores,
    )


def solution(mesh):
    return jax.shard_map(
        local,
        mesh=mesh,
        in_specs=(
            P("dp", None),
            P("dp", None),
            P("dp", None),
            P("dp", None),
            P("dp", None),
            P(),
            P(),
            P(None, "mp"),
            P(None, "mp"),
            P(None, "mp"),
            P("mp", None),
            P(None, "mp"),
            P(None, "mp"),
            P(None, "mp"),
            P("mp", None),
            P(None, "mp"),
            P("mp", None),
            P(),
            P(),
            P(),
            P(),
            P(),
            P(),
            P("mp", "dp"),
        ),
        out_specs=(
            P(),
            P("dp", "mp"),
            P("dp", "mp"),
            P(None, "mp"),
            P(None, "mp"),
            P(None, "mp"),
            P("mp", None),
            P(None, "mp"),
            P(None, "mp"),
            P(None, "mp"),
            P("mp", None),
            P(None, "mp"),
            P("mp", None),
            P(),
            P(),
            P(),
            P(),
            P(),
            P(),
            P("mp", "dp"),
            P(),
        ),
        check_vma=False,
    )
```

profile of v0, /device:TPU:0, one launch (start us, length us, event | category | flops | bytes accessed | tf_op | source)
XLA Modules:
  0.0 1602.5 jit_solution(9922767284052008243)
XLA Ops:
  24.5 48.2 %all-reduce.12.cloned.1.call-done = f32[512,1024]{1,0:T(8,128)} async-done(((f32[512,1024]{1,0:T(8,128)}), f32[512,1024]{1,0:T(8,128)}) %all-reduce.12.cloned.1.call-update) | async-done | bytes 2097168 | tf_op jit(solution)/shard_map/psum | solution.py:117
  87.4 51.4 %all-reduce.14.cloned.1.call-done = f32[512,1024]{1,0:T(8,128)} async-done(((f32[512,1024]{1,0:T(8,128)}), f32[512,1024]{1,0:T(8,128)}) %all-reduce.14.cloned.1.call-update) | async-done | bytes 2097168 | tf_op jit(solution)/shard_map/psum | solution.py:117
  142.4 6.9 multiply_convert_fusion.3
  155.3 49.3 %all-reduce.16.cloned.1.call-done = f32[512,1024]{1,0:T(8,128)} async-done(((f32[512,1024]{1,0:T(8,128)}), f32[512,1024]{1,0:T(8,128)}) %all-reduce.16.cloned.1.call-update) | async-done | bytes 2097168 | tf_op jit(solution)/shard_map/psum | solution.py:117
  209.1 447.2 %all-gather.2.cloned.1.call-done = bf16[12800,1024]{1,0:T(8,128)(2,1)} async-done(((bf16[12800,128]{1,0:T(8,128)(2,1)}), bf16[12800,1024]{1,0:T(8,128)(2,1)}) %all-gather.2.cloned.1.call-update) | async-done | bytes 26214416 | tf_op jit(solution)/shard_map/all_gather | solution.py:180
  656.4 25.5 %fusion.84 = (f32[512]{0:T(512)S(1)}, f32[512,12800]{1,0:T(8,128)}) fusion(bf16[12800,1024]{1,0:T(8,128)(2,1)} %all-gather.2.cloned.1.call-done, f32[512,1024]{1,0:T(8,128)} %copy-done.13, f32[1024]{0:T(1024)S(1)} %copy-done.91, f32[1024]{0:T(1024)S(1)} %copy-done.80, f32[512]{0:T(512)S(1)} %fusion.56, f32[512]{0:T(512)S(1)} %broadcast_multiply_fusion), kind=kOutput, calls=%fused_computation.192 | convolution fusion | flops 13430947840 | bytes 54540288 | tf_op jit(solution)/shard_map/dot_general | solution.py:27
  681.9 5.6 pmax.7
  687.5 7.9 gather_fusion
  695.5 10.8 exponential_reduce_fusion
  706.3 6.8 all-reduce.1
  713.4 19.8 %all-reduce = f32[64]{0:T(128)S(1)} all-reduce(f32[64]{0:T(128)S(1)} %divide_dynamic-update-slice_fusion), channel_id=1, replica_groups=mesh['dp'=8,'mp'=4] {'dp'}, use_global_device_ids=true, to_apply=%add | all-reduce | flops 64 | bytes 512
  735.2 17.0 %multiply_convert_fusion = bf16[512,12800]{1,0:T(8,128)(2,1)} fusion(f32[512,12800]{1,0:T(8,128)} %get-tuple-element.145, f32[512]{0:T(512)S(1)} %get-tuple-element.126, s32[512]{0:T(512)S(1)} %bitcast.184, f32[512]{0:T(512)S(1)} %mul.319), kind=kLoop, calls=%fused_computation.1 | loop fusion | flops 39321600 | bytes 39327744 | tf_op jit(solution)/shard_map/convert_element_type | solution.py:227
  752.2 21.8 %fusion.88 = f32[512,1024]{1,0:T(8,128)} fusion(bf16[512,12800]{1,0:T(8,128)(2,1)} %multiply_convert_fusion, bf16[12800,1024]{1,0:T(8,128)(2,1)} %all-gather.2.cloned.1.call-done), kind=kOutput, calls=%fused_computation.196 | convolution fusion | flops 13421772800 | bytes 41418752 | tf_op jit(solution)/shard_map/dot_general | solution.py:17
  774.1 47.5 %all-reduce.18.cloned.1.call-done = f32[512,1024]{1,0:T(8,128)} async-done(((f32[512,1024]{1,0:T(8,128)}), f32[512,1024]{1,0:T(8,128)}) %all-reduce.18.cloned.1.call-update) | async-done | bytes 2097168 | tf_op jit(solution)/shard_map/psum | solution.py:121
  834.5 51.4 %all-reduce.20.cloned.1.call-done = f32[512,1024]{1,0:T(8,128)} async-done(((f32[512,1024]{1,0:T(8,128)}), f32[512,1024]{1,0:T(8,128)}) %all-reduce.20.cloned.1.call-update) | async-done | bytes 2097168 | tf_op jit(solution)/shard_map/psum | solution.py:121
  901.2 51.5 %all-reduce.22.cloned.1.call-done = f32[512,1024]{1,0:T(8,128)} async-done(((f32[512,1024]{1,0:T(8,128)}), f32[512,1024]{1,0:T(8,128)}) %all-reduce.22.cloned.1.call-update) | async-done | bytes 2097168 | tf_op jit(solution)/shard_map/psum | solution.py:121
  971.5 5.2 fusion.22
  978.9 4.7 convolution_convert_fusion.1
  998.7 23.8 %convolution_convert_fusion = bf16[1024,12800]{1,0:T(8,128)(2,1)} fusion(bf16[512,12800]{1,0:T(8,128)(2,1)} %multiply_convert_fusion, f32[512,1024]{1,0:T(8,128)S(1)} %copy-done.15, f32[1024]{0:T(1024)S(1)} %copy-done.91, f32[1024]{0:T(1024)S(1)} %copy-done.80, f32[512]{0:T(512)S(1)} %fusion.56, f32[512]{0:T(512)S(1)} %broadcast_multiply_fusion), kind=kOutput, calls=%fused_computation.4 | convolution fusion | flops 13437501440 | bytes 41431040 | tf_op jit(solution)/shard_map/dot_general | solution.py:21
  1024.0 38.7 %all-reduce.2 = (bf16[1024]{0:T(1024)(128)(2,1)S(1)}, bf16[1024]{0:T(1024)(128)(2,1)S(1)}, bf16[1024]{0:T(1024)(128)(2,1)S(1)}, bf16[1024]{0:T(1024)(128)(2,1)S(...) all-reduce(bf16[1024]{0:T(1024)(128)(2,1)S(1)} %get-tuple-element.8, ...), channel_id=1, replica_groups=mesh['dp'=8,'mp'=4] {'dp'}, use_global_device_ids=true, to_apply=%region_49.50 | all-reduce | flops 6144 | bytes 24576 | tf_op jit(solution)/shard_map/psum | solution.py:322
  1070.4 382.8 %all-reduce.24.cloned.1.call-done = (bf16[1024,256]{0,1:T(8,128)(2,1)}, bf16[1024,256]{0,1:T(8,128)(2,1)}, bf16[1024,256]{0,1:T(8,128)(2,1)}, bf16[1024,256]{0,1...) async-done(((bf16[1024,256]{0,1:T(8,128)(2,1)}, ...) | async-done | bytes 8388624 | tf_op jit(solution)/shard_map/psum | solution.py:312
  1469.5 110.8 %reduce-scatter.8.cloned.1.call-done = bf16[128,12800]{1,0:T(8,128)(2,1)} async-done(((bf16[1024,12800]{1,0:T(8,128)(2,1)}), bf16[128,12800]{1,0:T(8,128)(2,1)}) %reduce-scatter.8.cloned.1.call-update) | async-done | bytes 3276816 | tf_op jit(solution)/shard_map/reduce_scatter | solution.py:232
  1580.3 5.3 convert_bitcast_fusion
  1585.6 8.3 copy.79
  (348 shorter events, 135.0 us)
Async XLA Ops:
  8.0 134.0 %copy-start = (bf16[1024,1024]{1,0:T(8,128)(2,1)S(1)}, bf16[1024,1024]{1,0:T(8,128)(2,1)}, u32[]{:S(2)}) copy-start(bf16[1024,1024]{1,0:T(8,128)(2,1)} %param.39) | copy-start | bytes 6291460
  8.1 64.7 %all-reduce.12.cloned.1.call-start = ((), (), s32[]{:S(2)}) async-start(), calls=%async_computation.3 | async-start | bytes 4194304 | tf_op jit(solution)/shard_map/psum | solution.py:117
  18.5 120.3 %all-reduce.14.cloned.1.call-start = ((), (), s32[]{:S(2)}) async-start(), calls=%async_computation.4 | async-start | bytes 4194304 | tf_op jit(solution)/shard_map/psum | solution.py:117
  87.2 117.4 %all-reduce.16.cloned.1.call-start = ((), (), s32[]{:S(2)}) async-start(), calls=%async_computation.5 | async-start | bytes 4194304 | tf_op jit(solution)/shard_map/psum | solution.py:117
  141.6 7.7 copy-start.7
  142.4 7.9 copy-start.87
  153.0 503.4 %all-gather.2.cloned.1.call-start = ((), (), s32[]{:S(2)}) async-start(), calls=%async_computation.6 | async-start | bytes 29491200 | tf_op jit(solution)/shard_map/all_gather | solution.py:180
  153.5 668.1 %all-reduce.18.cloned.1.call-start = ((), (), s32[]{:S(2)}) async-start(), calls=%async_computation.7 | async-start | bytes 4194304 | tf_op jit(solution)/shard_map/psum | solution.py:121
  207.4 448.9 %copy-start.80 = (f32[1024]{0:T(1024)S(1)}, f32[1024]{0:T(1024)}, u32[]{:S(2)}) copy-start(f32[1024]{0:T(1024)} %param.45) | copy-start | bytes 12292
  207.5 448.9 %copy-start.91 = (f32[1024]{0:T(1024)S(1)}, f32[1024]{0:T(1024)}, u32[]{:S(2)}) copy-start(f32[1024]{0:T(1024)} %param.46) | copy-start | bytes 12292
  695.5 37.7 %copy-start.92 = (s32[64]{0:T(128)S(1)}, s32[64]{0:T(128)}, u32[]{:S(2)}) copy-start(s32[64]{0:T(128)} %param.30) | copy-start | bytes 772
  774.0 111.8 %all-reduce.20.cloned.1.call-start = ((), (), s32[]{:S(2)}) async-start(), calls=%async_computation.8 | async-start | bytes 4194304 | tf_op jit(solution)/shard_map/psum | solution.py:121
  834.2 51.6 %copy-start.8 = (f32[512,1024]{1,0:T(8,128)S(1)}, f32[512,1024]{1,0:T(8,128)}, u32[]{:S(2)}) copy-start(f32[512,1024]{1,0:T(8,128)} %copy-done.7) | copy-start | bytes 6291460
  834.3 118.5 %all-reduce.22.cloned.1.call-start = ((), (), s32[]{:S(2)}) async-start(), calls=%async_computation.9 | async-start | bytes 4194304 | tf_op jit(solution)/shard_map/psum | solution.py:121
  885.9 5.4 slice-start
  899.3 53.5 %copy-start.6 = (f32[512,1024]{1,0:T(8,128)S(1)}, f32[512,1024]{1,0:T(8,128)}, u32[]{:S(2)}) copy-start(f32[512,1024]{1,0:T(8,128)} %copy-done.5) | copy-start | bytes 6291460
  901.1 165.2 %reduce-scatter.4.cloned.1.call-start = ((), (), s32[]{:S(2)}) async-start(), calls=%async_computation.10 | async-start | bytes 1310720 | tf_op jit(solution)/shard_map/reduce_scatter | solution.py:283
  901.2 54.7 %copy-start.78 = (f32[512]{0:T(512)S(1)}, f32[512]{0:T(512)}, u32[]{:S(2)}) copy-start(f32[512]{0:T(512)} %copy-done.77) | copy-start | bytes 6148
  967.4 100.9 %reduce-scatter.6.cloned.1.call-start = ((), (), s32[]{:S(2)}) async-start(), calls=%async_computation.11 | async-start | bytes 2621440 | tf_op jit(solution)/shard_map/reduce_scatter | solution.py:286
  971.5 5.2 copy-start.60
  978.9 474.3 %all-reduce.24.cloned.1.call-start = ((), (), s32[]{:S(2)}) async-start(), calls=%async_computation.13 | async-start | bytes 16777216 | tf_op jit(solution)/shard_map/psum | solution.py:312
  997.2 583.1 %reduce-scatter.8.cloned.1.call-start = ((), (), s32[]{:S(2)}) async-start(), calls=%async_computation.12 | async-start | bytes 29491200 | tf_op jit(solution)/shard_map/reduce_scatter | solution.py:232
  1453.2 5.8 copy-start.68
  1585.6 8.3 copy-start.1
  (88 other events, 197.1 us)
Sparse Core Ops, SparseCore 0:
  18.6 54.0 all-reduce.11
  87.3 51.4 all-reduce.13
  153.0 51.4 all-reduce.15
  774.1 47.4 all-reduce.17
  834.4 51.4 all-reduce.19
  901.3 51.4 all-reduce.21
  967.5 24.9 reduce-scatter.3
  995.8 31.4 reduce-scatter.5
  1031.2 549.0 reduce-scatter.7
Sparse Core Ops, SparseCore 1:
  154.9 501.4 all-gather.1
  997.3 455.9 all-reduce.23
where the time goes:
time: 1610 us; the launch traced here: 1600 us
  waiting for transfers between devices  1240 us (77%)
  matrix products  145 us (9%)
  other arithmetic  79.3 us (5%)
  blocking collectives  71 us (4%)
  local copies, waits for them, and re-layouts  46.2 us (3%)
  between operations  19.3 us (1%)
    all_gather x1, waiting for transfers between devices, local(): lax.all_gather(embedding, 'dp', axis=1, tiled=True)  447 us
    psum x1, waiting for transfers between devices, local(): lax.psum(grad_self_query.astype(jnp.bfloat16), 'dp').astype(jnp.float32)  383 us
    psum x3, waiting for transfers between devices, join_grads(): return lax.psum(partial_value, 'mp')  150 us
    psum x3, waiting for transfers between devices, join_heads(): return lax.psum(partial_value, 'mp')  149 us
    reduce_scatter x1, waiting for transfers between devices, local(): lax.psum_scatter(product_tn(third_low, grad_logits).astype(jnp.bfloat16),...  111 us
    dot_general x11, matrix products, product(): return jnp.dot(left_side, right_side, preferred_element_type=jnp.float32)  43 us
    dot_general x11, matrix products, product_tn(): lax.dot_general(left_side, right_side, (((0,), (0,)), ((), ())), preferre...  41.9 us
    psum x1, blocking collectives, local(): lax.psum(grad_gain_self.astype(jnp.bfloat16), 'dp').astype(jnp.float32)  38.7 us
  transfers between devices with their start and end apart: 11, of which 9 were waited for; matrix products, arithmetic and copies ran while one was open for 5% of the time, Pallas kernels for 0%

commit v1 on v0

--- a/solution.py
+++ b/solution.py
@@ -119,6 +119,42 @@
 
 def join_grads(partial_value):
     return lax.psum(partial_value, "mp")
+
+
+def shift_pairs(total, step):
+    return [(index, (index + step) % total) for index in range(total)]
+
+
+def spread_rows(table):
+    total = lax.axis_size("dp")
+    place = lax.axis_index("dp")
+    width = table.shape[1]
+    part = table.shape[0] // total
+    whole = jnp.zeros((part, width * total), table.dtype)
+    for step in range(total):
+        block = lax.dynamic_slice_in_dim(table, (place + step) % total * part, part, 0)
+        if step:
+            block = lax.ppermute(block, "dp", shift_pairs(total, step))
+        whole = lax.dynamic_update_slice_in_dim(
+            whole, block, (place - step) % total * width, 1
+        )
+    return whole
+
+
+def return_rows(rows, height):
+    total = lax.axis_size("dp")
+    place = lax.axis_index("dp")
+    part = rows.shape[0]
+    width = rows.shape[1] // total
+    whole = jnp.zeros((height, width), rows.dtype)
+    for step in range(total):
+        block = lax.dynamic_slice_in_dim(rows, (place + step) % total * width, width, 1)
+        if step:
+            block = lax.ppermute(block, "dp", shift_pairs(total, step))
+        whole = lax.dynamic_update_slice_in_dim(
+            whole, block, (place - step) % total * part, 0
+        )
+    return whole
 
 
 def local(
@@ -148,9 +184,13 @@
     embedding,
 ):
     row_count, row_len = segment_ids.shape
+    table_rows = spread_rows(embedding)
+    segments_all, answers_all, kept_all = (
+        lax.all_gather(ids, "dp", axis=0, tiled=True)
+        for ids in (segment_ids, answer_ids, loss_mask)
+    )
     span = SEG_ROW * MEM
     inputs = tokens.astype(jnp.float32)
-    keeper = loss_mask.astype(jnp.float32).reshape(-1)
     places = jnp.arange(row_len, dtype=jnp.int32)
     owners = jnp.arange(span, dtype=jnp.int32) // MEM
     self_masks = [
@@ -177,32 +217,27 @@
     third_norm = layer_norm(second_norm + branch_feed, gain_feed, shift_feed)
     third_low = third_norm.astype(jnp.bfloat16)
     vocab_local = embedding.shape[0]
-    logits = product_nt(third_low, lax.all_gather(embedding, "dp", axis=1, tiled=True))
-    offset = lax.axis_index("mp") * vocab_local
-    local_target = answer_ids.reshape(-1) - offset
-    inside = (local_target >= 0) & (local_target < vocab_local)
-    clipped = jnp.clip(local_target, 0, vocab_local - 1)
-    picked_part = jnp.where(
-        inside, jnp.take_along_axis(logits, clipped[:, None], axis=1)[:, 0], 0.0
-    )
-    local_top = jnp.max(logits, axis=1)
-    global_top = lax.pmax(local_top, "mp")
+    part = table_rows.shape[0]
+    states = lax.all_gather(third_low, "dp", axis=0, tiled=True)
+    logits = product_nt(states, table_rows)
+    offset = lax.axis_index("mp") * vocab_local + lax.axis_index("dp") * part
+    local_target = answers_all.reshape(-1) - offset
+    vocab_ids = jnp.arange(part, dtype=jnp.int32)
+    answer_hot = local_target[:, None] == vocab_ids[None, :]
+    picked_part = jnp.sum(jnp.where(answer_hot, logits, 0.0), axis=1)
+    global_top = lax.pmax(jnp.max(logits, axis=1), ("dp", "mp"))
     global_sum, picked = lax.psum(
-        (jnp.sum(jnp.exp(logits - global_top[:, None]), axis=1), picked_part), "mp"
+        (jnp.sum(jnp.exp(logits - global_top[:, None]), axis=1), picked_part), ("dp", "mp")
     )
     log_total = global_top + jnp.log(global_sum)
-    token_logp = (picked - log_total) * keeper
-    seg_local = row_count * SEG_ROW
-    local_ids = (segment_ids + (jnp.arange(row_count, dtype=jnp.int32) * SEG_ROW)[:, None]).reshape(
-        -1
-    )
-    seg_hot = (local_ids[:, None] == jnp.arange(seg_local, dtype=jnp.int32)[None, :]).astype(
-        jnp.float32
-    )
-    seg_sums = jnp.sum(seg_hot * token_logp[:, None], axis=0)
-    counts = jnp.sum(seg_hot * keeper[:, None], axis=0)
-    likely_local = seg_sums / jnp.maximum(counts, 1.0)
-    likely_all = lax.all_gather(likely_local, "dp", axis=0, tiled=True)
+    keeper = kept_all.astype(jnp.float32)
+    token_logp = (picked - log_total).reshape(keeper.shape) * keeper
+    seg_hot = (
+        segments_all[:, :, None] == jnp.arange(SEG_ROW, dtype=jnp.int32)[None, None, :]
+    ).astype(jnp.float32)
+    seg_sums = jnp.sum(seg_hot * token_logp[:, :, None], axis=1)
+    counts = jnp.sum(seg_hot * keeper[:, :, None], axis=1)
+    likely_all = (seg_sums / jnp.maximum(counts, 1.0)).reshape(-1)
     place_hot = (
         slot_place[:, None] == jnp.arange(likely_all.shape[0], dtype=jnp.int32)[None, :]
     ).astype(jnp.float32)
@@ -215,29 +250,23 @@
 
     loss, pullback = jax.vjp(marginal, doc_scores, likely_all)
     grad_scores, grad_likely = pullback(jnp.ones_like(loss))
-    per_segment = lax.dynamic_slice_in_dim(
-        grad_likely, lax.axis_index("dp") * seg_local, seg_local
-    ) / jnp.maximum(counts, 1.0)
-    grad_logp = jnp.dot(seg_hot, per_segment, precision=highest) * keeper
-    probabilities = jnp.exp(logits - log_total[:, None])
-    vocab_ids = jnp.arange(vocab_local, dtype=jnp.int32)
+    per_segment = grad_likely.reshape(counts.shape) / jnp.maximum(counts, 1.0)
+    grad_logp = (jnp.sum(seg_hot * per_segment[:, None, :], axis=2) * keeper).reshape(-1)
     grad_logits = (
         grad_logp[:, None]
-        * ((local_target[:, None] == vocab_ids[None, :]).astype(jnp.float32) - probabilities)
+        * (answer_hot.astype(jnp.float32) - jnp.exp(logits - log_total[:, None]))
     ).astype(jnp.bfloat16)
     grad_third = join_grads(
-        product(grad_logits, lax.all_gather(embedding, "dp", axis=1, tiled=True))
-    )
-    grad_table = (
         lax.psum_scatter(
-            product_tn(third_low, grad_logits).astype(jnp.bfloat16),
+            product(grad_logits, table_rows).astype(jnp.bfloat16),
             "dp",
             scatter_dimension=0,
             tiled=True,
-        )
-        .astype(jnp.float32)
-        .T
-    )
+        ).astype(jnp.float32)
+    )
+    grad_table = return_rows(
+        product_tn(grad_logits, states).astype(jnp.bfloat16), vocab_local
+    ).astype(jnp.float32)
     grad_res3, grad_gain_feed, grad_shift_feed = norm_back(
         second_norm + branch_feed, gain_feed, shift_feed, grad_third
     )

time: 1610 us -> 1320 us (0.82)
  waiting for transfers between devices: 1240 us -> 650 us
  blocking collectives: 71 us -> 340 us
  starting transfers between devices: 1.31 us -> 47.1 us
    all_gather x1, waiting for transfers between devices: 447 us -> 0.01 us  [local(): states = lax.all_gather(third_low, 'dp', axis=0, tiled=True)]
    psum x1, waiting for transfers between devices: 383 us -> 143 us  [local(): lax.psum(grad_self_query.astype(jnp.bfloat16), 'dp').astype(jnp.float32)]
    all_gather x0 -> x3, blocking collectives: none -> 150 us  [local(): lax.all_gather(ids, 'dp', axis=0, tiled=True)]
    ppermute x0 -> x14, waiting for transfers between devices: none -> 107 us  [the longest x7 93.1 us: return_rows(): block = lax.ppermute(block, 'dp', shift_pairs(total, step))]
    psum x3 -> x2, waiting for transfers between devices: 150 us -> 101 us  [join_grads(): return lax.psum(partial_value, 'mp')]
    ppermute x0 -> x14, starting transfers between devices: none -> 45.9 us  [the longest x7 35.5 us: return_rows(): block = lax.ppermute(block, 'dp', shift_pairs(total, step))]
    psum x0 -> x1, blocking collectives: none -> 42.8 us  [join_grads(): return lax.psum(partial_value, 'mp')]
    pmax x1, blocking collectives: 5.63 us -> 43.8 us  [local(): global_top = lax.pmax(jnp.max(logits, axis=1), ('dp', 'mp'))]
  transfers between devices with their start and end apart: 11 -> 24, of which waited for: 9 -> 11; matrix products, arithmetic and copies ran while one was open for 5% -> 6% of each run, Pallas kernels for 0% -> 0%
where the time goes in v1:
time: 1320 us; the launch traced here: 1310 us
  waiting for transfers between devices  650 us (49%)
  blocking collectives  340 us (26%)
  matrix products  143 us (11%)
  other arithmetic  64.7 us (5%)
  starting transfers between devices  47.1 us (4%)
  local copies, waits for them, and re-layouts  46.5 us (4%)
  between operations  17.8 us (1%)
    psum x3, waiting for transfers between devices, join_heads(): return lax.psum(partial_value, 'mp')  151 us
    all_gather x3, blocking collectives, local(): lax.all_gather(ids, 'dp', axis=0, tiled=True)  150 us
    reduce_scatter x1, waiting for transfers between devices, local(): lax.psum_scatter(product(grad_logits, table_rows).astype(jnp.bfloat16), '...  149 us
    psum x1, waiting for transfers between devices, local(): lax.psum(grad_self_query.astype(jnp.bfloat16), 'dp').astype(jnp.float32)  143 us
    psum x2, waiting for transfers between devices, join_grads(): return lax.psum(partial_value, 'mp')  101 us
    ppermute x7, waiting for transfers between devices, return_rows(): block = lax.ppermute(block, 'dp', shift_pairs(total, step))  93.1 us
    psum x1, blocking collectives, local(): lax.psum(grad_gain_self.astype(jnp.bfloat16), 'dp').astype(jnp.float32)  61.3 us
    dot_general x11, matrix products, product(): return jnp.dot(left_side, right_side, preferred_element_type=jnp.float32)  46.9 us
  transfers between devices with their start and end apart: 24, of which 11 were waited for; matrix products, arithmetic and copies ran while one was open for 6% of the time, Pallas kernels for 0%

profile of v1, /device:TPU:0, one launch (start us, length us, event | category | flops | bytes accessed | tf_op | source)
XLA Modules:
  0.0 1309.7 jit_solution(13218269071357332770)
XLA Ops:
  23.7 48.2 %all-reduce.11.cloned.1.call-done = f32[512,1024]{1,0:T(8,128)} async-done(((f32[512,1024]{1,0:T(8,128)}), f32[512,1024]{1,0:T(8,128)}) %all-reduce.11.cloned.1.call-update) | async-done | bytes 2097168 | tf_op jit(solution)/shard_map/psum | solution.py:117
  86.6 51.3 %all-reduce.13.cloned.1.call-done = f32[512,1024]{1,0:T(8,128)} async-done(((f32[512,1024]{1,0:T(8,128)}), f32[512,1024]{1,0:T(8,128)}) %all-reduce.13.cloned.1.call-update) | async-done | bytes 2097168 | tf_op jit(solution)/shard_map/psum | solution.py:117
  152.1 51.5 %all-reduce.15.cloned.1.call-done = f32[512,1024]{1,0:T(8,128)} async-done(((f32[512,1024]{1,0:T(8,128)}), f32[512,1024]{1,0:T(8,128)}) %all-reduce.15.cloned.1.call-update) | async-done | bytes 2097168 | tf_op jit(solution)/shard_map/psum | solution.py:117
  224.5 97.1 %all-gather = s32[8,1,512]{2,1,0:T(1,128)S(1)} all-gather(s32[1,1,512]{2,1,0:T(1,128)S(1)} %bitcast.189), channel_id=1, replica_groups=mesh['dp'=8,'mp'=4] {'dp'}, dimensions={0}, use_global_device_ids=true | all-gather | bytes 18432 | tf_op jit(solution)/shard_map/all_gather | solution.py:189
  321.6 26.6 %all-gather.2 = s32[8,1,512]{2,1,0:T(1,128)S(1)} all-gather(s32[1,1,512]{2,1,0:T(1,128)S(1)} %bitcast.193), channel_id=1, replica_groups=mesh['dp'=8,'mp'=4] {'dp'}, dimensions={0}, use_global_device_ids=true | all-gather | bytes 18432 | tf_op jit(solution)/shard_map/all_gather | solution.py:189
  348.2 26.4 %all-gather.1 = s32[8,1,512]{2,1,0:T(1,128)S(1)} all-gather(s32[1,1,512]{2,1,0:T(1,128)S(1)} %bitcast.194), channel_id=1, replica_groups=mesh['dp'=8,'mp'=4] {'dp'}, dimensions={0}, use_global_device_ids=true | all-gather | bytes 18432 | tf_op jit(solution)/shard_map/all_gather | solution.py:189
  381.5 13.8 %collective-permute-done.2 = bf16[1600,128]{1,0:T(8,128)(2,1)S(1)} collective-permute-done((bf16[1600,128]{1,0:T(8,128)(2,1)}, bf16[1600,128]{1,0:T(8,128)(2,1)S(1)}, u32[]{:S(2)}, u32[]{:S(2)}) %collective-permute-start.2) | collective-permute-done | bytes 409632 | tf_op jit(solution)/shard_map/ppermute | solution.py:137
  402.2 21.9 %fusion.81 = (f32[4096]{0:T(1024)S(1)}, f32[4096,1600]{0,1:T(8,128)}) fusion(bf16[4096,1024]{1,0:T(8,128)(2,1)} %all-gather.5.cloned.1.call-done, bf16[1600,1024]{1,0:T(8,128)(2,1)} %constant_dynamic-update-slice_fusion.7), kind=kOutput, calls=%fused_computation.215 | convolution fusion | flops 13428322304 | bytes 37896192 | tf_op jit(solution)/shard_map/dot_general | solution.py:27
  424.2 43.8 %pmax.7 = f32[4096]{0:T(1024)S(1)} all-reduce(f32[4096]{0:T(1024)S(1)} %get-tuple-element.181), channel_id=1, replica_groups=mesh['dp'=8,'mp'=4] {'dp','mp'}, use_global_device_ids=true, to_apply=%region_18.19 | all-reduce | flops 4096 | bytes 32768 | tf_op jit(solution)/shard_map/pmax | solution.py:228
  468.0 12.1 exponential_reduce_fusion
  480.1 42.1 %all-reduce = (f32[4096]{0:T(1024)S(1)}, f32[4096]{0:T(1024)S(1)}) all-reduce(f32[4096]{0:T(1024)S(1)} %get-tuple-element.105, f32[4096]{0:T(1024)S(1)} %get-tuple-element.106), channel_id=1, replica_groups=mesh['dp'=8,'mp'=4] {'dp','mp'}, use_global_device_ids=true, to_apply=%region_20.21 | all-reduce | flops 8192 | bytes 65536 | tf_op jit(solution)/shard_map/psum | solution.py:229
  524.7 25.6 %convolution_convert_fusion = bf16[4096,1024]{1,0:T(8,128)(2,1)} fusion(bf16[1600,1024]{1,0:T(8,128)(2,1)} %constant_dynamic-update-slice_fusion.7, f32[4096,1600]{0,1:T(8,128)} %get-tuple-element.182, f32[4096]{0:T(1024)S(1)} %get-tuple-element.149, f32[4096]{0:T(1024)S(1)} %bitcast.190, s32[4096]{0:T(1024)S(1)} %bitcast.184), kind=kOutput, calls=%fused_computation.10 | convolution fusion | flops 13465288704 | bytes 37928960 | tf_op jit(solution)/shard_map/dot_general | solution.py:17
  550.4 148.9 %reduce-scatter.4.cloned.1.call-done = bf16[512,1024]{1,0:T(8,128)(2,1)} async-done(((bf16[4096,1024]{1,0:T(8,128)(2,1)}), bf16[512,1024]{1,0:T(8,128)(2,1)}) %reduce-scatter.4.cloned.1.call-update) | async-done | bytes 1048592 | tf_op jit(solution)/shard_map/reduce_scatter | solution.py:260
  699.3 42.8 %all-reduce.22 = f32[512,1024]{1,0:T(8,128)} all-reduce(bf16[512,1024]{1,0:T(8,128)(2,1)} %reduce-scatter.4.cloned.1.call-done), channel_id=1, replica_groups=mesh['dp'=8,'mp'=4] {'mp'}, use_global_device_ids=true, to_apply=%region_28.29 | all-reduce | flops 524288 | bytes 3145728 | tf_op jit(solution)/shard_map/psum | solution.py:121
  754.8 49.4 %all-reduce.17.cloned.1.call-done = f32[512,1024]{1,0:T(8,128)} async-done(((f32[512,1024]{1,0:T(8,128)}), f32[512,1024]{1,0:T(8,128)}) %all-reduce.17.cloned.1.call-update) | async-done | bytes 2097168 | tf_op jit(solution)/shard_map/psum | solution.py:121
  820.0 51.1 %all-reduce.19.cloned.1.call-done = f32[512,1024]{1,0:T(8,128)} async-done(((f32[512,1024]{1,0:T(8,128)}), f32[512,1024]{1,0:T(8,128)}) %all-reduce.19.cloned.1.call-update) | async-done | bytes 2097168 | tf_op jit(solution)/shard_map/psum | solution.py:121
  916.3 21.9 %convolution_convert_fusion.1 = bf16[1600,1024]{1,0:T(8,128)(2,1)S(1)} fusion(bf16[4096,1024]{1,0:T(8,128)(2,1)} %all-gather.5.cloned.1.call-done, f32[4096,1600]{0,1:T(8,128)} %get-tuple-element.182, f32[4096]{0:T(1024)S(1)} %get-tuple-element.149, f32[4096]{0:T(1024)S(1)} %bitcast.191, s32[4096]{0:T(1024)S(1)} %bitcast.185), kind=kOutput, calls=%fused_computation.23 | convolution fusion | flops 13462732800 | bytes 37928960 | tf_op jit(solution)/shard_map/dot_general | solution.py:21
  948.4 49.8 %collective-permute-done.7 = bf16[1600,128]{1,0:T(8,128)(2,1)S(1)} collective-permute-done((bf16[1600,128]{1,0:T(8,128)(2,1)S(1)}, bf16[1600,128]{1,0:T(8,128)(2,1)S(1)}, u32[]{:S(2)}, u32[]{:S(2)}) %collective-permute-start.7) | collective-permute-done | bytes 409632 | tf_op jit(solution)/shard_map/ppermute | solution.py:153
  998.2 17.2 %collective-permute-start.9 = (bf16[1600,128]{1,0:T(8,128)(2,1)S(1)}, bf16[1600,128]{1,0:T(8,128)(2,1)S(1)}, u32[]{:S(2)}, u32[]{:S(2)}) collective-permute-start(bf16[1600,128]{1,0:T(8,128)(2,1)S(1)} %get-tuple-element.162), channel_id=1, source_target_pairs={{0,12},{4,16},{8,20},{12,24},{16,28},{20,0},{24,4},{28,8},{1,13},{... | collective-permute-start | bytes 1228808 | tf_op jit(solution)/shard_map/ppermute | solution.py:153
  1015.5 10.2 collective-permute-start.10
  1025.7 35.4 %collective-permute-done.9 = bf16[1600,128]{1,0:T(8,128)(2,1)S(1)} collective-permute-done((bf16[1600,128]{1,0:T(8,128)(2,1)S(1)}, bf16[1600,128]{1,0:T(8,128)(2,1)S(1)}, u32[]{:S(2)}, u32[]{:S(2)}) %collective-permute-start.9) | collective-permute-done | bytes 409632 | tf_op jit(solution)/shard_map/ppermute | solution.py:153
  1061.2 7.9 collective-permute-done.10
  1072.4 61.3 %all-reduce.1 = (bf16[1024]{0:T(1024)(128)(2,1)S(1)}, bf16[1024]{0:T(1024)(128)(2,1)S(1)}, bf16[1024]{0:T(1024)(128)(2,1)S(1)}, bf16[1024]{0:T(1024)(128)(2,1)S(...) all-reduce(bf16[1024]{0:T(1024)(128)(2,1)S(1)} %get-tuple-element.1, ...), channel_id=1, replica_groups=mesh['dp'=8,'mp'=4] {'dp'}, use_global_device_ids=true, to_apply=%region_52.53 | all-reduce | flops 6144 | bytes 24576 | tf_op jit(solution)/shard_map/psum | solution.py:351
  1141.4 142.6 %all-reduce.21.cloned.1.call-done = (bf16[1024,256]{0,1:T(8,128)(2,1)}, bf16[1024,256]{0,1:T(8,128)(2,1)}, bf16[1024,256]{0,1:T(8,128)(2,1)}, bf16[1024,256]{0,1...) async-done(((bf16[1024,256]{0,1:T(8,128)(2,1)}, ...) | async-done | bytes 8388624 | tf_op jit(solution)/shard_map/psum | solution.py:341
  (427 shorter events, 192.8 us)
Async XLA Ops:
  7.2 64.6 %all-reduce.11.cloned.1.call-start = ((), (), s32[]{:S(2)}) async-start(), calls=%async_computation.3 | async-start | bytes 4194304 | tf_op jit(solution)/shard_map/psum | solution.py:117
  17.6 120.3 %all-reduce.13.cloned.1.call-start = ((), (), s32[]{:S(2)}) async-start(), calls=%async_computation.4 | async-start | bytes 4194304 | tf_op jit(solution)/shard_map/psum | solution.py:117
  86.3 117.4 %all-reduce.15.cloned.1.call-start = ((), (), s32[]{:S(2)}) async-start(), calls=%async_computation.5 | async-start | bytes 4194304 | tf_op jit(solution)/shard_map/psum | solution.py:117
  152.1 250.2 %all-gather.5.cloned.1.call-start = ((), (), s32[]{:S(2)}) async-start(), calls=%async_computation.6 | async-start | bytes 9437184 | tf_op jit(solution)/shard_map/all_gather | solution.py:221
  209.3 490.0 %reduce-scatter.4.cloned.1.call-start = ((), (), s32[]{:S(2)}) async-start(), calls=%async_computation.7 | async-start | bytes 9437184 | tf_op jit(solution)/shard_map/reduce_scatter | solution.py:260
  214.4 186.0 %collective-permute-start.6 = (bf16[1600,128]{1,0:T(8,128)(2,1)S(1)}, bf16[1600,128]{1,0:T(8,128)(2,1)}, u32[]{:S(2)}, u32[]{:S(2)}) collective-permute-start(bf16[1600,128]{1,0:T(8,128)(2,1)S(1)} %get-tuple-element.166), channel_id=1, source_target_pairs={{0,28},{4,0},{8,4},{12,8},{16,12},{20,16},{24,20},{28,24},{1,29},{... | collective-permute-start | bytes 1228808 | tf_op jit(solution)/shard_map/ppermute | solution.py:137
  218.7 179.2 %collective-permute-start.4 = (bf16[1600,128]{1,0:T(8,128)(2,1)}, bf16[1600,128]{1,0:T(8,128)(2,1)}, u32[]{:S(2)}, u32[]{:S(2)}) collective-permute-start(bf16[1600,128]{1,0:T(8,128)(2,1)} %get-tuple-element.167), channel_id=1, source_target_pairs={{0,20},{4,24},{8,28},{12,0},{16,4},{20,8},{24,12},{28,16},{1,21},{... | collective-permute-start | bytes 1228808 | tf_op jit(solution)/shard_map/ppermute | solution.py:137
  218.7 177.4 %collective-permute-start.3 = (bf16[1600,128]{1,0:T(8,128)(2,1)}, bf16[1600,128]{1,0:T(8,128)(2,1)}, u32[]{:S(2)}, u32[]{:S(2)}) collective-permute-start(bf16[1600,128]{1,0:T(8,128)(2,1)} %get-tuple-element.168), channel_id=1, source_target_pairs={{0,16},{4,20},{8,24},{12,28},{16,0},{20,4},{24,8},{28,12},{1,17},{... | collective-permute-start | bytes 1228808 | tf_op jit(solution)/shard_map/ppermute | solution.py:137
  218.8 158.3 %collective-permute-start.1 = (bf16[1600,128]{1,0:T(8,128)(2,1)}, bf16[1600,128]{1,0:T(8,128)(2,1)}, u32[]{:S(2)}, u32[]{:S(2)}) collective-permute-start(bf16[1600,128]{1,0:T(8,128)(2,1)} %get-tuple-element.170), channel_id=1, source_target_pairs={{0,8},{4,12},{8,16},{12,20},{16,24},{20,28},{24,0},{28,4},{1,9},{5... | collective-permute-start | bytes 1228808 | tf_op jit(solution)/shard_map/ppermute | solution.py:137
  220.3 154.9 %collective-permute-start = (bf16[1600,128]{1,0:T(8,128)(2,1)}, bf16[1600,128]{1,0:T(8,128)(2,1)}, u32[]{:S(2)}, u32[]{:S(2)}) collective-permute-start(bf16[1600,128]{1,0:T(8,128)(2,1)} %get-tuple-element.171), channel_id=1, source_target_pairs={{0,4},{4,8},{8,12},{12,16},{16,20},{20,24},{24,28},{28,0},{1,5},{5... | collective-permute-start | bytes 1228808 | tf_op jit(solution)/shard_map/ppermute | solution.py:137
  375.2 20.1 %collective-permute-start.2 = (bf16[1600,128]{1,0:T(8,128)(2,1)}, bf16[1600,128]{1,0:T(8,128)(2,1)S(1)}, u32[]{:S(2)}, u32[]{:S(2)}) collective-permute-start(bf16[1600,128]{1,0:T(8,128)(2,1)} %get-tuple-element.169), channel_id=1, source_target_pairs={{0,12},{4,16},{8,20},{12,24},{16,28},{20,0},{24,4},{28,8},{1,13},{... | collective-permute-start | bytes 1228808 | tf_op jit(solution)/shard_map/ppermute | solution.py:137
  377.1 22.6 %collective-permute-start.5 = (bf16[1600,128]{1,0:T(8,128)(2,1)S(1)}, bf16[1600,128]{1,0:T(8,128)(2,1)S(1)}, u32[]{:S(2)}, u32[]{:S(2)}) collective-permute-start(bf16[1600,128]{1,0:T(8,128)(2,1)S(1)} %get-tuple-element.173), channel_id=1, source_target_pairs={{0,24},{4,28},{8,0},{12,4},{16,8},{20,12},{24,16},{28,20},{1,25},{... | collective-permute-start | bytes 1228808 | tf_op jit(solution)/shard_map/ppermute | solution.py:137
  550.3 253.9 %all-reduce.17.cloned.1.call-start = ((), (), s32[]{:S(2)}) async-start(), calls=%async_computation.8 | async-start | bytes 4194304 | tf_op jit(solution)/shard_map/psum | solution.py:121
  754.7 116.4 %all-reduce.19.cloned.1.call-start = ((), (), s32[]{:S(2)}) async-start(), calls=%async_computation.9 | async-start | bytes 4194304 | tf_op jit(solution)/shard_map/psum | solution.py:121
  819.5 317.8 %reduce-scatter.6.cloned.1.call-start = ((), (), s32[]{:S(2)}) async-start(), calls=%async_computation.10 | async-start | bytes 1310720 | tf_op jit(solution)/shard_map/reduce_scatter | solution.py:312
  885.8 253.5 %reduce-scatter.8.cloned.1.call-start = ((), (), s32[]{:S(2)}) async-start(), calls=%async_computation.11 | async-start | bytes 2621440 | tf_op jit(solution)/shard_map/reduce_scatter | solution.py:315
  897.0 387.0 %all-reduce.21.cloned.1.call-start = ((), (), s32[]{:S(2)}) async-start(), calls=%async_computation.12 | async-start | bytes 16777216 | tf_op jit(solution)/shard_map/psum | solution.py:341
  939.7 129.7 %collective-permute-start.13 = (bf16[1600,128]{1,0:T(8,128)(2,1)S(1)}, bf16[1600,128]{1,0:T(8,128)(2,1)S(1)}, u32[]{:S(2)}, u32[]{:S(2)}) collective-permute-start(bf16[1600,128]{1,0:T(8,128)(2,1)S(1)} %get-tuple-element.158), channel_id=1, source_target_pairs={{0,28},{4,0},{8,4},{12,8},{16,12},{20,16},{24,20},{28,24},{1,29},{... | collective-permute-start | bytes 1228808 | tf_op jit(solution)/shard_map/ppermute | solution.py:153
  943.8 125.5 %collective-permute-start.12 = (bf16[1600,128]{1,0:T(8,128)(2,1)S(1)}, bf16[1600,128]{1,0:T(8,128)(2,1)S(1)}, u32[]{:S(2)}, u32[]{:S(2)}) collective-permute-start(bf16[1600,128]{1,0:T(8,128)(2,1)S(1)} %get-tuple-element.159), channel_id=1, source_target_pairs={{0,24},{4,28},{8,0},{12,4},{16,8},{20,12},{24,16},{28,20},{1,25},{... | collective-permute-start | bytes 1228808 | tf_op jit(solution)/shard_map/ppermute | solution.py:153
  944.3 124.9 %collective-permute-start.11 = (bf16[1600,128]{1,0:T(8,128)(2,1)S(1)}, bf16[1600,128]{1,0:T(8,128)(2,1)S(1)}, u32[]{:S(2)}, u32[]{:S(2)}) collective-permute-start(bf16[1600,128]{1,0:T(8,128)(2,1)S(1)} %get-tuple-element.160), channel_id=1, source_target_pairs={{0,20},{4,24},{8,28},{12,0},{16,4},{20,8},{24,12},{28,16},{1,21},{... | collective-permute-start | bytes 1228808 | tf_op jit(solution)/shard_map/ppermute | solution.py:153
  944.3 71.1 %collective-permute-start.8 = (bf16[1600,128]{1,0:T(8,128)(2,1)S(1)}, bf16[1600,128]{1,0:T(8,128)(2,1)S(1)}, u32[]{:S(2)}, u32[]{:S(2)}) collective-permute-start(bf16[1600,128]{1,0:T(8,128)(2,1)S(1)} %get-tuple-element.163), channel_id=1, source_target_pairs={{0,8},{4,12},{8,16},{12,20},{16,24},{20,28},{24,0},{28,4},{1,9},{5... | collective-permute-start | bytes 1228808 | tf_op jit(solution)/shard_map/ppermute | solution.py:153
  945.8 52.4 %collective-permute-start.7 = (bf16[1600,128]{1,0:T(8,128)(2,1)S(1)}, bf16[1600,128]{1,0:T(8,128)(2,1)S(1)}, u32[]{:S(2)}, u32[]{:S(2)}) collective-permute-start(bf16[1600,128]{1,0:T(8,128)(2,1)S(1)} %get-tuple-element.164), channel_id=1, source_target_pairs={{0,4},{4,8},{8,12},{12,16},{16,20},{20,24},{24,28},{28,0},{1,5},{5... | collective-permute-start | bytes 1228808 | tf_op jit(solution)/shard_map/ppermute | solution.py:153
  998.2 62.9 %collective-permute-start.9 = (bf16[1600,128]{1,0:T(8,128)(2,1)S(1)}, bf16[1600,128]{1,0:T(8,128)(2,1)S(1)}, u32[]{:S(2)}, u32[]{:S(2)}) collective-permute-start(bf16[1600,128]{1,0:T(8,128)(2,1)S(1)} %get-tuple-element.162), channel_id=1, source_target_pairs={{0,12},{4,16},{8,20},{12,24},{16,28},{20,0},{24,4},{28,8},{1,13},{... | collective-permute-start | bytes 1228808 | tf_op jit(solution)/shard_map/ppermute | solution.py:153
  1015.5 53.6 %collective-permute-start.10 = (bf16[1600,128]{1,0:T(8,128)(2,1)S(1)}, bf16[1600,128]{1,0:T(8,128)(2,1)S(1)}, u32[]{:S(2)}, u32[]{:S(2)}) collective-permute-start(bf16[1600,128]{1,0:T(8,128)(2,1)S(1)} %get-tuple-element.161), channel_id=1, source_target_pairs={{0,16},{4,20},{8,24},{12,28},{16,0},{20,4},{24,8},{28,12},{1,17},{... | collective-permute-start | bytes 1228808 | tf_op jit(solution)/shard_map/ppermute | solution.py:153
  (118 other events, 1218.0 us)
Sparse Core Ops, SparseCore 0:
  17.7 54.0 all-reduce.10
  86.4 51.4 all-reduce.12
  152.2 51.4 all-reduce.14
  209.4 177.1 all-gather.4
  550.5 148.7 reduce-scatter.3
  754.8 49.3 all-reduce.16
  819.6 51.4 all-reduce.18
  885.9 24.9 reduce-scatter.5
  914.2 31.3 reduce-scatter.7
  952.9 331.0 all-reduce.20

commit v2 on v1

--- a/solution.py
+++ b/solution.py
@@ -1,6 +1,10 @@
+import functools
+
 import jax
 import jax.numpy as jnp
 from jax import lax
+from jax.experimental import pallas as pl
+from jax.experimental.pallas import tpu as pltpu
 from jax.sharding import PartitionSpec as P
 
 HEAD_DIM = 64
@@ -27,17 +31,6 @@
     return lax.dot_general(
         left_side, right_side, (((1,), (1,)), ((), ())), preferred_element_type=jnp.float32
     )
-
-
-def layer_norm(inputs, gain_vec, shift_vec):
-    center = inputs - jnp.mean(inputs, axis=-1, keepdims=True)
-    spread = jnp.mean(center * center, axis=-1, keepdims=True)
-    return center * lax.rsqrt(spread + norm_eps) * gain_vec + shift_vec
-
-
-def norm_back(residual, gain_vec, shift_vec, grad_out):
-    outputs, pullback = jax.vjp(layer_norm, residual, gain_vec, shift_vec)
-    return pullback(grad_out)
 
 
 def gelu_exact(inputs):
@@ -113,12 +106,504 @@
     return (parts_query[0], parts_key[0], parts_value[0])
 
 
-def join_heads(partial_value):
-    return lax.psum(partial_value, "mp")
-
-
-def join_grads(partial_value):
-    return lax.psum(partial_value, "mp")
+MESH = pl.DeviceIdType.MESH
+VMEM = pl.BlockSpec(memory_space=pltpu.VMEM)
+ANY = pl.BlockSpec(memory_space=pl.ANY)
+DMA = pltpu.SemaphoreType.DMA
+QUARTERS = 4
+
+
+def flip(index, mask):
+    for bit in range(mask.bit_length()):
+        if mask >> bit & 1:
+            step = 1 << bit
+            index = index + step * (1 - 2 * lax.rem(lax.div(index, step), 2))
+    return index
+
+
+def greet(peers):
+    barrier = pltpu.get_barrier_semaphore()
+    for peer in peers:
+        pl.semaphore_signal(barrier, inc=1, device_id=peer, device_id_type=MESH)
+    pl.semaphore_wait(barrier, len(peers))
+
+
+def remote(source, target, send_sem, recv_sem, peer):
+    copy = pltpu.make_async_remote_copy(
+        src_ref=source,
+        dst_ref=target,
+        send_sem=send_sem,
+        recv_sem=recv_sem,
+        device_id=peer,
+        device_id_type=MESH,
+    )
+    copy.start()
+    return copy
+
+
+def sum_quarter(place, block_of, near, far, sib_send, sib_recv, far_send, far_recv, sems):
+    copies = []
+    for slot, mask in enumerate((3, 1)):
+        sib_send[slot] = block_of(flip(place, mask)).astype(jnp.bfloat16)
+        copies.append(
+            remote(
+                sib_send.at[slot], sib_recv.at[slot], sems.at[0, slot], sems.at[1, slot], near
+            )
+        )
+    distant = block_of(flip(place, 2))
+    own = block_of(place)
+    copies[0].wait_recv()
+    far_send[...] = (distant + sib_recv[0].astype(jnp.float32)).astype(jnp.bfloat16)
+    last = remote(far_send, far_recv, sems.at[0, 2], sems.at[1, 2], far)
+    copies[1].wait_recv()
+    own = own + sib_recv[1].astype(jnp.float32)
+    last.wait_recv()
+    own = own + far_recv[...].astype(jnp.float32)
+    return own, copies + [last]
+
+
+def share_quarter(place, quarters, near, far, sems):
+    here = quarters.at[place]
+    to_far = remote(here, here, sems.at[0, 3], sems.at[1, 3], far)
+    to_near = remote(here, here, sems.at[0, 4], sems.at[1, 4], near)
+    to_far.wait_recv()
+    there = quarters.at[flip(place, 2)]
+    passed = remote(there, there, sems.at[0, 5], sems.at[1, 5], near)
+    to_near.wait_recv()
+    passed.wait_recv()
+    return [to_far, to_near, passed]
+
+
+def norm_rows(rows, gain, shift):
+    center = rows - jnp.mean(rows, axis=-1, keepdims=True)
+    spread = jnp.mean(center * center, axis=-1, keepdims=True)
+    return center * lax.rsqrt(spread + norm_eps) * gain + shift
+
+
+def norm_rows_back(rows, gain, grad):
+    center = rows - jnp.mean(rows, axis=-1, keepdims=True)
+    scale = lax.rsqrt(jnp.mean(center * center, axis=-1, keepdims=True) + norm_eps)
+    normed = center * scale
+    inner = grad * gain
+    grad_rows = scale * (
+        inner
+        - jnp.mean(inner, axis=-1, keepdims=True)
+        - normed * jnp.mean(inner * normed, axis=-1, keepdims=True)
+    )
+    return (
+        grad_rows,
+        jnp.sum(grad * normed, axis=0, keepdims=True),
+        jnp.sum(grad, axis=0, keepdims=True),
+    )
+
+
+def rows_of(ref, height, index):
+    return ref[pl.ds(pl.multiple_of(index * height, height), height), :]
+
+
+def exchange_scratch(height, width):
+    return [
+        pltpu.VMEM((2, height, width), jnp.bfloat16),
+        pltpu.VMEM((2, height, width), jnp.bfloat16),
+        pltpu.VMEM((height, width), jnp.bfloat16),
+        pltpu.VMEM((height, width), jnp.bfloat16),
+        DMA((2, 6)),
+    ]
+
+
+def mix_norm_kernel(
+    total, left, weight, kept, gain, shift, ids, quarters, normed, rows, ids_all,
+    sib_send, sib_recv, far_send, far_recv, sems, ids_sems, ids_local,
+):
+    block, place = lax.axis_index("dp"), lax.axis_index("mp")
+    near, far = (block, flip(place, 1)), (block, flip(place, 2))
+    height = kept.shape[0]
+    peers = [near, far]
+    if ids is not None:
+        peers += [(flip(block, mask), place) for mask in range(1, total)]
+    greet(peers)
+    copies = []
+    if ids is not None:
+        own = pltpu.make_async_copy(ids, ids_all.at[block], ids_local)
+        own.start()
+        for mask in range(1, total):
+            copies.append(
+                remote(
+                    ids, ids_all.at[block], ids_sems.at[0, mask], ids_sems.at[1, mask],
+                    (flip(block, mask), place),
+                )
+            )
+
+    def block_of(index):
+        return jnp.dot(
+            rows_of(left, height, index), weight[...], preferred_element_type=jnp.float32
+        )
+
+    branch, more = sum_quarter(
+        place, block_of, near, far, sib_send, sib_recv, far_send, far_recv, sems
+    )
+    outcome = kept[...].astype(jnp.float32) + branch
+    rows[...] = outcome
+    outcome = norm_rows(outcome, gain[...], shift[...])
+    normed[...] = outcome
+    quarters[place] = outcome.astype(jnp.bfloat16)
+    more += share_quarter(place, quarters, near, far, sems)
+    for copy in copies:
+        copy.wait_recv()
+    for copy in copies + more:
+        copy.wait_send()
+    if ids is not None:
+        own.wait()
+
+
+def mix_norm(left, weight, kept, gain, shift, number, ids=None):
+    height, width = kept.shape
+    total = lax.axis_size("dp")
+    quarter = jax.ShapeDtypeStruct((height, width), jnp.float32)
+    out_shape = [
+        jax.ShapeDtypeStruct((QUARTERS, height, width), jnp.bfloat16), quarter, quarter
+    ]
+    given = [left, weight, kept, gain.reshape(1, -1), shift.reshape(1, -1)]
+    scratch = exchange_scratch(height, width)
+    if ids is None:
+        def kernel(left, weight, kept, gain, shift, quarters, normed, rows, *scratch):
+            mix_norm_kernel(
+                total, left, weight, kept, gain, shift, None, quarters, normed, rows, None,
+                *scratch, None, None,
+            )
+    else:
+        kernel = functools.partial(mix_norm_kernel, total)
+        given.append(ids)
+        out_shape.append(jax.ShapeDtypeStruct((total,) + ids.shape, ids.dtype))
+        scratch += [DMA((2, total)), DMA]
+    outcome = pl.pallas_call(
+        kernel,
+        out_shape=out_shape,
+        in_specs=[VMEM] * len(given),
+        out_specs=[VMEM] * len(out_shape),
+        scratch_shapes=scratch,
+        compiler_params=pltpu.CompilerParams(
+            collective_id=number, has_side_effects=True, vmem_limit_bytes=48 * 2**20
+        ),
+    )(*given)
+    return (outcome[0].reshape(-1, width),) + tuple(outcome[1:])
+
+
+def feed_norm_kernel(
+    total, left, weight, kept, gain, shift, states, rows,
+    low, sib_send, sib_recv, far_send, far_recv, sems, hops, own_sem,
+):
+    block, place = lax.axis_index("dp"), lax.axis_index("mp")
+    near, far = (block, flip(place, 1)), (block, flip(place, 2))
+    beside = (flip(block, 1), place)
+    height = kept.shape[0]
+    greet([near, far, beside] + [(flip(block, mask), place) for mask in range(2, total, 2)])
+
+    def block_of(index):
+        return jnp.dot(
+            rows_of(left, height, index), weight[...], preferred_element_type=jnp.float32
+        )
+
+    branch, sent = sum_quarter(
+        place, block_of, near, far, sib_send, sib_recv, far_send, far_recv, sems
+    )
+    outcome = kept[...] + branch
+    rows[...] = outcome
+    low[...] = norm_rows(outcome, gain[...], shift[...]).astype(jnp.bfloat16)
+    own = pltpu.make_async_copy(low, states.at[block, place], own_sem)
+    own.start()
+    across = flip(place, 2)
+
+    def hop(kind, mask, source, peer, row, column):
+        copy = remote(
+            source, states.at[row, column], hops.at[0, kind, mask], hops.at[1, kind, mask], peer
+        )
+        sent.append(copy)
+        return copy
+
+    first = {}
+    for mask in range(2, total, 2):
+        first[mask] = hop(0, mask, low, (flip(block, mask), place), block, place)
+    over = {}
+    ends = []
+
+    def pass_on(mask):
+        over[mask].wait_recv()
+        row = flip(block, mask)
+        ends.append(hop(3, mask, states.at[row, across], near, row, across))
+
+    for mask in range(total):
+        row = flip(block, mask)
+        if mask:
+            first[mask].wait_recv()
+        source = states.at[row, place] if mask else low
+        if mask % 2 == 0:
+            first[mask + 1] = hop(0, mask + 1, source, beside, row, place)
+        over[mask] = hop(1, mask, source, far, row, place)
+        ends.append(hop(2, mask, source, near, row, place))
+        if mask >= 2:
+            pass_on(mask - 2)
+    for mask in range(max(total - 2, 0), total):
+        pass_on(mask)
+    for copy in ends:
+        copy.wait_recv()
+    for copy in sent:
+        copy.wait_send()
+    own.wait()
+
+
+def feed_norm(left, weight, kept, gain, shift, number):
+    height, width = kept.shape
+    total = lax.axis_size("dp")
+    states, rows = pl.pallas_call(
+        functools.partial(feed_norm_kernel, total),
+        out_shape=[
+            jax.ShapeDtypeStruct((total, QUARTERS, height, width), jnp.bfloat16),
+            jax.ShapeDtypeStruct((height, width), jnp.float32),
+        ],
+        in_specs=[VMEM] * 5,
+        out_specs=[ANY, VMEM],
+        scratch_shapes=[pltpu.VMEM((height, width), jnp.bfloat16)]
+        + exchange_scratch(height, width)
+        + [DMA((2, 4, total)), DMA],
+        compiler_params=pltpu.CompilerParams(
+            collective_id=number, has_side_effects=True, vmem_limit_bytes=48 * 2**20
+        ),
+    )(left, weight, kept, gain.reshape(1, -1), shift.reshape(1, -1))
+    return states.reshape(-1, width), rows
+
+
+def back_norm_kernel(
+    left, weight, kept, rows, gain, quarters, grad_rows, grad_vecs,
+    sib_send, sib_recv, far_send, far_recv, sems,
+):
+    block, place = lax.axis_index("dp"), lax.axis_index("mp")
+    near, far = (block, flip(place, 1)), (block, flip(place, 2))
+    height = kept.shape[0]
+    greet([near, far])
+
+    def block_of(index):
+        return lax.dot_general(
+            rows_of(left, height, index),
+            weight[...],
+            (((1,), (1,)), ((), ())),
+            preferred_element_type=jnp.float32,
+        )
+
+    branch, sent = sum_quarter(
+        place, block_of, near, far, sib_send, sib_recv, far_send, far_recv, sems
+    )
+    outcome, grad_gain, grad_shift = norm_rows_back(rows[...], gain[...], kept[...] + branch)
+    grad_rows[...] = outcome
+    grad_vecs[0:1] = grad_gain
+    grad_vecs[1:2] = grad_shift
+    quarters[place] = outcome.astype(jnp.bfloat16)
+    sent += share_quarter(place, quarters, near, far, sems)
+    for copy in sent:
+        copy.wait_send()
+
+
+def back_norm(left, weight, kept, rows, gain, number):
+    height, width = kept.shape
+    quarters, grad_rows, grad_vecs = pl.pallas_call(
+        back_norm_kernel,
+        out_shape=[
+            jax.ShapeDtypeStruct((QUARTERS, height, width), jnp.bfloat16),
+            jax.ShapeDtypeStruct((height, width), jnp.float32),
+            jax.ShapeDtypeStruct((2, width), jnp.float32),
+        ],
+        in_specs=[VMEM] * 5,
+        out_specs=[VMEM] * 3,
+        scratch_shapes=exchange_scratch(height, width),
+        compiler_params=pltpu.CompilerParams(
+            collective_id=number, has_side_effects=True, vmem_limit_bytes=48 * 2**20
+        ),
+    )(left, weight, kept, rows, gain.reshape(1, -1))
+    return quarters.reshape(-1, width), grad_rows, grad_vecs
+
+
+def join_totals_kernel(total, given, outcome, sends, recvs, sems):
+    block, place = lax.axis_index("dp"), lax.axis_index("mp")
+    peers = [((block, flip(place, 1)), lax.rem(place, 2))]
+    peers.append(((block, flip(place, 2)), lax.div(place, 2)))
+    step = 1
+    while step < total:
+        peers.append(((flip(block, step), place), lax.rem(lax.div(block, step), 2)))
+        step *= 2
+    greet([peer for peer, _ in peers])
+    values = [given[0], given[1], given[2]]
+    copies = []
+    for stage, (peer, side) in enumerate(peers):
+        for index in range(3):
+            sends[stage, index] = values[index]
+        copy = remote(
+            sends.at[stage], recvs.at[stage], sems.at[0, stage], sems.at[1, stage], peer
+        )
+        copy.wait_recv()
+        copies.append(copy)
+        ahead = side == 0
+        theirs = [recvs[stage, index] for index in range(3)]
+        early = [jnp.where(ahead, mine, other) for mine, other in zip(values, theirs)]
+        late = [jnp.where(ahead, other, mine) for mine, other in zip(values, theirs)]
+        top = jnp.maximum(early[0], late[0])
+        values = [
+            top,
+            early[1] * jnp.exp(early[0] - top) + late[1] * jnp.exp(late[0] - top),
+            early[2] + late[2],
+        ]
+    for index in range(3):
+        outcome[index] = values[index]
+    for copy in copies:
+        copy.wait_send()
+
+
+def join_totals(top, amount, picked, number):
+    total = lax.axis_size("dp")
+    stages = 2 + (total - 1).bit_length()
+    given = jnp.stack([top, amount, picked]).reshape(3, -1, 128)
+    outcome = pl.pallas_call(
+        functools.partial(join_totals_kernel, total),
+        out_shape=jax.ShapeDtypeStruct(given.shape, jnp.float32),
+        in_specs=[VMEM],
+        out_specs=VMEM,
+        scratch_shapes=[
+            pltpu.VMEM((stages,) + given.shape, jnp.float32),
+            pltpu.VMEM((stages,) + given.shape, jnp.float32),
+            DMA((2, stages)),
+        ],
+        compiler_params=pltpu.CompilerParams(collective_id=number, has_side_effects=True),
+    )(given)
+    return outcome.reshape(3, -1)
+
+
+def head_back_kernel(
+    total, parts, rows, gain, quarters, grad_rows, grad_vecs,
+    mine, sib_recv, far_recv, beside_recv, end_recv, sems, sib_sems, far_sems, beside_sems,
+    end_sems, load_sems,
+):
+    block, place = lax.axis_index("dp"), lax.axis_index("mp")
+    near, far = (block, flip(place, 1)), (block, flip(place, 2))
+    beside = (flip(block, 1), place)
+    greet([near, far, beside] + [(flip(block, mask), place) for mask in range(2, total, 2)])
+    order = [mask for mask in range(total - 1, -1, -1) if mask % 2]
+    order += [mask for mask in range(total - 1, -1, -1) if mask % 2 == 0]
+    sent, loads, sib, across, over, ends = [], {}, {}, {}, {}, {}
+    for mask in order:
+        row = flip(block, mask)
+        for slot, turn in enumerate((2, 0)):
+            loads[mask, slot] = pltpu.make_async_copy(
+                parts.at[row, flip(place, turn)], mine.at[mask, slot], load_sems.at[mask, slot]
+            )
+            loads[mask, slot].start()
+            sib[mask, slot] = remote(
+                parts.at[row, flip(place, turn + 1)],
+                sib_recv.at[mask, slot],
+                sib_sems.at[0, mask, slot],
+                sib_sems.at[1, mask, slot],
+                near,
+            )
+            sent.append(sib[mask, slot])
+
+    def join(mask, slot, *others):
+        value = mine[mask, slot].astype(jnp.float32)
+        for other in others:
+            value = value + other.astype(jnp.float32)
+        return value
+
+    def to_far(mask):
+        for slot in (0, 1):
+            loads[mask, slot].wait()
+            sib[mask, slot].wait_recv()
+        mine[mask, 0] = join(mask, 0, sib_recv[mask, 0]).astype(jnp.bfloat16)
+        across[mask] = remote(
+            mine.at[mask, 0], far_recv.at[mask], far_sems.at[0, mask], far_sems.at[1, mask], far
+        )
+        sent.append(across[mask])
+
+    def to_beside(mask):
+        across[mask].wait_recv()
+        mine[mask, 1] = join(mask, 1, sib_recv[mask, 1], far_recv[mask]).astype(jnp.bfloat16)
+        over[mask] = remote(
+            mine.at[mask, 1],
+            beside_recv.at[mask // 2],
+            beside_sems.at[0, mask // 2],
+            beside_sems.at[1, mask // 2],
+            beside,
+        )
+        sent.append(over[mask])
+
+    def to_end(mask):
+        across[mask].wait_recv()
+        over[mask + 1].wait_recv()
+        value = join(mask, 1, sib_recv[mask, 1], far_recv[mask], beside_recv[mask // 2])
+        if mask == 0:
+            return value
+        mine[mask, 1] = value.astype(jnp.bfloat16)
+        ends[mask] = remote(
+            mine.at[mask, 1],
+            end_recv.at[mask // 2],
+            end_sems.at[0, mask // 2],
+            end_sems.at[1, mask // 2],
+            (flip(block, mask), place),
+        )
+        sent.append(ends[mask])
+        return None
+
+    outcome = None
+    for step in range(len(order) + 2):
+        if step < len(order):
+            to_far(order[step])
+        if step >= 2:
+            mask = order[step - 2]
+            if mask % 2:
+                to_beside(mask)
+            else:
+                outcome = to_end(mask)
+    for mask in range(total - 2, 0, -2):
+        ends[mask].wait_recv()
+        outcome = outcome + end_recv[mask // 2].astype(jnp.float32)
+    outcome, grad_gain, grad_shift = norm_rows_back(rows[...], gain[...], outcome)
+    grad_rows[...] = outcome
+    grad_vecs[0:1] = grad_gain
+    grad_vecs[1:2] = grad_shift
+    quarters[place] = outcome.astype(jnp.bfloat16)
+    sent += share_quarter(place, quarters, near, far, sems)
+    for copy in sent:
+        copy.wait_send()
+
+
+def head_back(parts, rows, gain, number):
+    height, width = rows.shape
+    total = lax.axis_size("dp")
+    half = total // 2
+    block = (height, width)
+    quarters, grad_rows, grad_vecs = pl.pallas_call(
+        functools.partial(head_back_kernel, total),
+        out_shape=[
+            jax.ShapeDtypeStruct((QUARTERS,) + block, jnp.bfloat16),
+            jax.ShapeDtypeStruct(block, jnp.float32),
+            jax.ShapeDtypeStruct((2, width), jnp.float32),
+        ],
+        in_specs=[ANY, VMEM, VMEM],
+        out_specs=[VMEM] * 3,
+        scratch_shapes=[
+            pltpu.VMEM((total, 2) + block, jnp.bfloat16),
+            pltpu.VMEM((total, 2) + block, jnp.bfloat16),
+            pltpu.VMEM((total,) + block, jnp.bfloat16),
+            pltpu.VMEM((half,) + block, jnp.bfloat16),
+            pltpu.VMEM((half,) + block, jnp.bfloat16),
+            DMA((2, 6)),
+            DMA((2, total, 2)),
+            DMA((2, total)),
+            DMA((2, half)),
+            DMA((2, half)),
+            DMA((total, 2)),
+        ],
+        compiler_params=pltpu.CompilerParams(
+            collective_id=number, has_side_effects=True, vmem_limit_bytes=60 * 2**20
+        ),
+    )(parts.reshape((total, QUARTERS) + block), rows, gain.reshape(1, -1))
+    return quarters.reshape(-1, width), grad_rows, grad_vecs
 
 
 def shift_pairs(total, step):
@@ -185,12 +670,9 @@
 ):
     row_count, row_len = segment_ids.shape
     table_rows = spread_rows(embedding)
-    segments_all, answers_all, kept_all = (
-        lax.all_gather(ids, "dp", axis=0, tiled=True)
-        for ids in (segment_ids, answer_ids, loss_mask)
-    )
     span = SEG_ROW * MEM
-    inputs = tokens.astype(jnp.float32)
+    quarter = tokens.shape[0] // QUARTERS
+    inputs = lax.dynamic_slice_in_dim(tokens, lax.axis_index("mp") * quarter, quarter, 0)
     places = jnp.arange(row_len, dtype=jnp.int32)
     owners = jnp.arange(span, dtype=jnp.int32) // MEM
     self_masks = [
@@ -201,33 +683,37 @@
     key_self = product(tokens, self_key).astype(jnp.bfloat16)
     value_self = product(tokens, self_value).astype(jnp.bfloat16)
     self_mix, self_totals = run_rows(query_self, key_self, value_self, self_masks)
-    branch_self = join_heads(product(self_mix, self_out))
-    first_norm = layer_norm(inputs + branch_self, gain_self, shift_self)
-    first_low = first_norm.astype(jnp.bfloat16)
+    first_low, first_norm, rows_self, ids_all = mix_norm(
+        self_mix, self_out, inputs, gain_self, shift_self, 0,
+        jnp.concatenate([segment_ids, answer_ids, loss_mask], axis=0),
+    )
+    segments_all, answers_all, kept_all = (
+        ids_all[:, kind * row_count : (kind + 1) * row_count].reshape(-1, row_len)
+        for kind in range(3)
+    )
     query_cross = product(first_low, cross_query).astype(jnp.bfloat16)
     key_cross = product(memory, cross_key).astype(jnp.bfloat16)
     value_cross = product(memory, cross_value).astype(jnp.bfloat16)
     cross_mix, cross_totals = run_rows(query_cross, key_cross, value_cross, cross_masks)
-    branch_cross = join_heads(product(cross_mix, cross_out))
-    second_norm = layer_norm(first_norm + branch_cross, gain_cross, shift_cross)
-    second_low = second_norm.astype(jnp.bfloat16)
+    second_low, second_norm, rows_cross = mix_norm(
+        cross_mix, cross_out, first_norm, gain_cross, shift_cross, 1
+    )
     feed_pre = product(second_low, feed_up)
     feed_act = gelu_exact(feed_pre).astype(jnp.bfloat16)
-    branch_feed = join_heads(product(feed_act, feed_down))
-    third_norm = layer_norm(second_norm + branch_feed, gain_feed, shift_feed)
-    third_low = third_norm.astype(jnp.bfloat16)
+    states, rows_feed = feed_norm(
+        feed_act, feed_down, second_norm, gain_feed, shift_feed, 2
+    )
     vocab_local = embedding.shape[0]
     part = table_rows.shape[0]
-    states = lax.all_gather(third_low, "dp", axis=0, tiled=True)
     logits = product_nt(states, table_rows)
     offset = lax.axis_index("mp") * vocab_local + lax.axis_index("dp") * part
     local_target = answers_all.reshape(-1) - offset
     vocab_ids = jnp.arange(part, dtype=jnp.int32)
     answer_hot = local_target[:, None] == vocab_ids[None, :]
     picked_part = jnp.sum(jnp.where(answer_hot, logits, 0.0), axis=1)
-    global_top = lax.pmax(jnp.max(logits, axis=1), ("dp", "mp"))
-    global_sum, picked = lax.psum(
-        (jnp.sum(jnp.exp(logits - global_top[:, None]), axis=1), picked_part), ("dp", "mp")
+    local_top = jnp.max(logits, axis=1)
+    global_top, global_sum, picked = join_totals(
+        local_top, jnp.sum(jnp.exp(logits - local_top[:, None]), axis=1), picked_part, 3
     )
     log_total = global_top + jnp.log(global_sum)
     keeper = kept_all.astype(jnp.float32)
@@ -256,31 +742,20 @@
         grad_logp[:, None]
         * (answer_hot.astype(jnp.float32) - jnp.exp(logits - log_total[:, None]))
     ).astype(jnp.bfloat16)
-    grad_third = join_grads(
-        lax.psum_scatter(
-            product(grad_logits, table_rows).astype(jnp.bfloat16),
-            "dp",
-            scatter_dimension=0,
-            tiled=True,
-        ).astype(jnp.float32)
+    grad_branch, grad_res3, grad_vecs_feed = head_back(
+        product(grad_logits, table_rows).astype(jnp.bfloat16), rows_feed, gain_feed, 4
     )
     grad_table = return_rows(
         product_tn(grad_logits, states).astype(jnp.bfloat16), vocab_local
     ).astype(jnp.float32)
-    grad_res3, grad_gain_feed, grad_shift_feed = norm_back(
-        second_norm + branch_feed, gain_feed, shift_feed, grad_third
-    )
-    grad_branch = grad_res3.astype(jnp.bfloat16)
     grad_feed_down = product_tn(feed_act, grad_branch)
     grad_act = product_nt(grad_branch, feed_down)
     act_value, act_pull = jax.vjp(gelu_exact, feed_pre)
     grad_pre = act_pull(grad_act)[0].astype(jnp.bfloat16)
     grad_feed_up = product_tn(second_low, grad_pre)
-    grad_second = grad_res3 + join_grads(product_nt(grad_pre, feed_up))
-    grad_res2, grad_gain_cross, grad_shift_cross = norm_back(
-        first_norm + branch_cross, gain_cross, shift_cross, grad_second
-    )
-    grad_branch = grad_res2.astype(jnp.bfloat16)
+    grad_branch, grad_res2, grad_vecs_cross = back_norm(
+        grad_pre, feed_up, grad_res3, rows_cross, gain_cross, 5
+    )
     grad_cross_out = product_tn(cross_mix, grad_branch)
     grad_mix = product_nt(grad_branch, cross_out).astype(jnp.bfloat16)
     cross_gq, cross_gk, cross_gv = back_rows(
@@ -290,11 +765,9 @@
     grad_cross_key = product_tn(memory, cross_gk)
     grad_cross_value = product_tn(memory, cross_gv)
     grad_memory_part = product_nt(cross_gk, cross_key) + product_nt(cross_gv, cross_value)
-    grad_first = grad_res2 + join_grads(product_nt(cross_gq, cross_query))
-    grad_res1, grad_gain_self, grad_shift_self = norm_back(
-        inputs + branch_self, gain_self, shift_self, grad_first
-    )
-    grad_branch = grad_res1.astype(jnp.bfloat16)
+    grad_branch, _, grad_vecs_self = back_norm(
+        cross_gq, cross_query, grad_res2, rows_self, gain_self, 6
+    )
     grad_self_out = product_tn(self_mix, grad_branch)
     grad_mix = product_nt(grad_branch, self_out).astype(jnp.bfloat16)
     self_gq, self_gk, self_gv = back_rows(
@@ -318,7 +791,10 @@
     )
     column_start = lax.axis_index("mp") * input_share.shape[1]
     grad_tokens = input_share + lax.dynamic_slice_in_dim(
-        grad_res1, column_start, input_share.shape[1], 1
+        grad_branch, column_start, input_share.shape[1], 1
+    ).astype(jnp.float32)
+    grad_vecs = lax.psum(
+        jnp.concatenate([grad_vecs_self, grad_vecs_cross, grad_vecs_feed], axis=0), ("dp", "mp")
     )
     (
         sum_sq,
@@ -331,12 +807,6 @@
         sum_co,
         sum_up,
         sum_down,
-        sum_gs,
-        sum_ss,
-        sum_gc,
-        sum_sc,
-        sum_gf,
-        sum_sf,
     ) = (
         lax.psum(grad_self_query.astype(jnp.bfloat16), "dp").astype(jnp.float32),
         lax.psum(grad_self_key.astype(jnp.bfloat16), "dp").astype(jnp.float32),
@@ -348,12 +818,6 @@
         lax.psum(grad_cross_out.astype(jnp.bfloat16), "dp").astype(jnp.float32),
         lax.psum(grad_feed_up.astype(jnp.bfloat16), "dp").astype(jnp.float32),
         lax.psum(grad_feed_down.astype(jnp.bfloat16), "dp").astype(jnp.float32),
-        lax.psum(grad_gain_self.astype(jnp.bfloat16), "dp").astype(jnp.float32),
-        lax.psum(grad_shift_self.astype(jnp.bfloat16), "dp").astype(jnp.float32),
-        lax.psum(grad_gain_cross.astype(jnp.bfloat16), "dp").astype(jnp.float32),
-        lax.psum(grad_shift_cross.astype(jnp.bfloat16), "dp").astype(jnp.float32),
-        lax.psum(grad_gain_feed.astype(jnp.bfloat16), "dp").astype(jnp.float32),
-        lax.psum(grad_shift_feed.astype(jnp.bfloat16), "dp").astype(jnp.float32),
     )
     return (
         loss,
@@ -369,12 +833,7 @@
         sum_co,
         sum_up,
         sum_down,
-        sum_gs,
-        sum_ss,
-        sum_gc,
-        sum_sc,
-        sum_gf,
-        sum_sf,
+        *grad_vecs,
         grad_table,
         grad_scores,
     )

time: 1320 us -> 843 us (0.64)
  waiting for transfers between devices: 650 us -> 187 us
  Pallas kernels: 0 us -> 257 us
  blocking collectives: 340 us -> 112 us
  other arithmetic: 64.7 us -> 40.5 us
  starting transfers between devices: 47.1 us -> 23.9 us
    pallas_call x0 -> x7, Pallas kernels: none -> 257 us  [the longest x1 70.7 us: head_back(): pl.pallas_call(functools.partial(head_back_kernel, total), out_shape=[jax...]
    psum x5 -> x0, waiting for transfers between devices: 252 us -> none  [the longest x3 151 us: join_heads(): return lax.psum(partial_value, 'mp')]
    all_gather x3 -> x0, blocking collectives: 150 us -> none  [local(): lax.all_gather(ids, 'dp', axis=0, tiled=True)]
    reduce_scatter x1 -> x0, waiting for transfers between devices: 149 us -> none  [local(): lax.psum_scatter(product(grad_logits, table_rows).astype(jnp.bfloat16), '...]
    ppermute x7, waiting for transfers between devices: 93.1 us -> 42.4 us  [return_rows(): block = lax.ppermute(block, 'dp', shift_pairs(total, step))]
    pmax x1 -> x0, blocking collectives: 43.8 us -> none  [local(): global_top = lax.pmax(jnp.max(logits, axis=1), ('dp', 'mp'))]
    psum x3 -> x1, blocking collectives: 146 us -> 112 us  [local(): lax.psum(jnp.concatenate([grad_vecs_self, grad_vecs_cross, grad_vecs_feed...]
    ppermute x7, starting transfers between devices: 35.5 us -> 10.7 us  [return_rows(): block = lax.ppermute(block, 'dp', shift_pairs(total, step))]
  transfers between devices with their start and end apart: 24 -> 17, of which waited for: 11 -> 4; matrix products, arithmetic and copies ran while one was open for 6% -> 13% of each run, Pallas kernels for 0% -> 14%
where the time goes in v2:
time: 843 us; the launch traced here: 837 us
  Pallas kernels  257 us (30%)
  waiting for transfers between devices  187 us (22%)
  matrix products  147 us (17%)
  blocking collectives  112 us (13%)
  local copies, waits for them, and re-layouts  49.2 us (6%)
  other arithmetic  40.5 us (5%)
  starting transfers between devices  23.9 us (3%)
  between operations  19.5 us (2%)
    psum x1, waiting for transfers between devices, local(): lax.psum(grad_self_query.astype(jnp.bfloat16), 'dp').astype(jnp.float32)  130 us
    psum x1, blocking collectives, local(): lax.psum(jnp.concatenate([grad_vecs_self, grad_vecs_cross, grad_vecs_feed...  112 us
    pallas_call x1, Pallas kernels, head_back(): pl.pallas_call(functools.partial(head_back_kernel, total), out_shape=[jax...  70.7 us
    pallas_call x1, Pallas kernels, feed_norm(): pl.pallas_call(functools.partial(feed_norm_kernel, total), out_shape=[jax...  66.8 us
    pallas_call x2, Pallas kernels, mix_norm(): pl.pallas_call(kernel, out_shape=out_shape, in_specs=[VMEM] * len(given),...  53.2 us
    dot_general x8, matrix products, product(): return jnp.dot(left_side, right_side, preferred_element_type=jnp.float32)  44.2 us
    ppermute x7, waiting for transfers between devices, return_rows(): block = lax.ppermute(block, 'dp', shift_pairs(total, step))  42.4 us
    pallas_call x2, Pallas kernels, back_norm(): pl.pallas_call(back_norm_kernel, out_shape=[jax.ShapeDtypeStruct((QUARTER...  41.3 us
  transfers between devices with their start and end apart: 17, of which 4 were waited for; matrix products, arithmetic and copies ran while one was open for 13% of the time, Pallas kernels for 14%

profile of v2, /device:TPU:0, one launch (start us, length us, event | category | flops | bytes accessed | tf_op | source)
XLA Modules:
  0.0 836.7 jit_solution(8899020883387389492)
XLA Ops:
  13.6 6.0 collective-permute-start.6
  39.8 34.0 %shard_map.391 = (bf16[4,128,1024]{2,1,0:T(8,128)(2,1)S(1)}, f32[128,1024]{1,0:T(8,128)S(1)}, f32[128,1024]{1,0:T(8,128)S(1)}, s32[8,3,512]{2,1,0:T(4,128)S(1)}) custom-call(bf16[512,256]{1,0:T(8,128)(2,1)S(1)} %copy.74.left, bf16[256,1024]{1,0:T(8,128)(2,1)S(1)} %copy-done.21, bf16[128,1024]{1,0:T(8,128)(2,1)S(1)} %constant_dynamic-slice_fusion.14.kept, ...), custom_call_target="tpu_custom_call" | custom-call | tf_op jit(solution)/shard_map/pallas_call | solution.py:279
  84.3 19.3 %shard_map.392 = (bf16[4,128,1024]{2,1,0:T(8,128)(2,1)S(1)}, f32[128,1024]{1,0:T(8,128)S(1)}, f32[128,1024]{1,0:T(8,128)S(1)}) custom-call(bf16[512,256]{1,0:T(8,128)(2,1)S(1)} %copy.75.left, bf16[256,1024]{1,0:T(8,128)(2,1)S(1)} %copy-done.19, f32[128,1024]{1,0:T(8,128)S(1)} %copy-done.23, f32[1,1024]{1,0:T(1,128)S(1)} %bitcast.172, f32[1,1024]{1,0:T(1,128)S(1)} %bitcast.177), custom_call_target="tpu_custom_call" | custom-call | tf_op jit(solution)/shard_map/pallas_call | solution.py:279
  103.6 8.9 %multiply_convert_fusion.3 = (bf16[512,1024]{1,0:T(8,128)(2,1)S(1)}, f32[512,1024]{1,0:T(8,128)}, f32[512,1024]{1,0:T(8,128)}) fusion(bf16[512,1024]{1,0:T(8,128)(2,1)S(1)} %bitcast.179, bf16[1024,1024]{1,0:T(8,128)(2,1)} %weight.8), kind=kOutput, calls=%fused_computation.32 | convolution fusion | flops 1107820544 | bytes 8388608 | tf_op jit(solution)/shard_map/dot_general | solution.py:21
  112.6 66.8 %shard_map.393 = (bf16[8,4,128,1024]{3,2,1,0:T(8,128)(2,1)}, f32[128,1024]{1,0:T(8,128)S(1)}) custom-call(bf16[512,1024]{1,0:T(8,128)(2,1)S(1)} %get-tuple-element.136.left, bf16[1024,1024]{1,0:T(8,128)(2,1)S(1)} %copy-done.4, f32[128,1024]{1,0:T(8,128)S(1)} %get-tuple-element.42.kept, f32[1,1024]{1,0:T(1,128)S(1)} %bitcast.171, f32[1,1024]{1,0:T(1,128)S(1)} %bitcast.178), custom_call_target="tpu_custom_call" | custom-call | tf_op jit(solution)/shard_map/pallas_call | solution.py:358
  180.8 3.3 collective-permute-start.5
  185.3 15.0 %collective-permute-done.2 = bf16[1600,128]{1,0:T(8,128)(2,1)S(1)} collective-permute-done((bf16[1600,128]{1,0:T(8,128)(2,1)S(1)}, bf16[1600,128]{1,0:T(8,128)(2,1)S(1)}, u32[]{:S(2)}, u32[]{:S(2)}) %collective-permute-start.2) | collective-permute-done | bytes 409632 | tf_op jit(solution)/shard_map/ppermute | solution.py:622
  204.1 22.2 %fusion.60 = (f32[4096]{0:T(1024)S(1)}, f32[4096,1600]{0,1:T(8,128)}) fusion(bf16[4096,1024]{1,0:T(8,128)(2,1)} %bitcast.238, bf16[1600,1024]{1,0:T(8,128)(2,1)S(1)} %constant_dynamic-update-slice_fusion.7), kind=kOutput, calls=%fused_computation.170 | convolution fusion | flops 13428322304 | bytes 37896192 | tf_op jit(solution)/shard_map/dot_general | solution.py:31
  226.3 12.0 %exponential_reduce_fusion = (f32[4096]{0:T(1024)S(1)}, f32[4096]{0:T(1024)S(1)}) fusion(f32[4096,1600]{0,1:T(8,128)} %get-tuple-element.173, f32[4096]{0:T(1024)S(1)} %get-tuple-element.172, s32[4096]{0:T(1024)S(1)} %bitcast.219), kind=kLoop, calls=%fused_computation.3 | loop fusion | flops 32759808 | bytes 26279936 | tf_op jit(solution)/shard_map/reduce_sum | solution.py:716
  239.0 24.9 %shard_map.394 = f32[3,32,128]{2,1,0:T(8,128)} custom-call(f32[3,32,128]{2,1,0:T(8,128)} %pad_maximum_fusion.given), custom_call_target="tpu_custom_call" | custom-call | tf_op jit(solution)/shard_map/pallas_call | solution.py:464
  266.7 26.2 %convolution_convert_fusion = bf16[4096,1024]{1,0:T(8,128)(2,1)} fusion(bf16[1600,1024]{1,0:T(8,128)(2,1)} %copy-done.42, f32[4096,1600]{0,1:T(8,128)} %get-tuple-element.173, f32[4096]{0:T(1024)S(1)} %get-tuple-element.157, f32[4096]{0:T(1024)S(1)} %mul.260, s32[4096]{0:T(1024)S(1)} %bitcast.220), kind=kOutput, calls=%fused_computation.10 | convolution fusion | flops 13465288704 | bytes 37928960 | tf_op jit(solution)/shard_map/dot_general | solution.py:21
  292.9 70.7 %shard_map.395 = (bf16[4,128,1024]{2,1,0:T(8,128)(2,1)}, f32[128,1024]{1,0:T(8,128)}, f32[2,1024]{1,0:T(2,128)}) custom-call(bf16[8,4,128,1024]{3,2,1,0:T(8,128)(2,1)} %bitcast.183, f32[128,1024]{1,0:T(8,128)} %copy-done.15, f32[1,1024]{1,0:T(1,128)} %bitcast.170), custom_call_target="tpu_custom_call" | custom-call | tf_op jit(solution)/shard_map/pallas_call | solution.py:580
  363.6 5.1 add_convert_fusion.2.left
  368.8 20.6 %shard_map.396 = (bf16[4,128,1024]{2,1,0:T(8,128)(2,1)S(1)}, f32[128,1024]{1,0:T(8,128)S(1)}, f32[2,1024]{1,0:T(2,128)S(1)}) custom-call(bf16[512,1024]{1,0:T(8,128)(2,1)S(1)} %add_convert_fusion.2.left, bf16[1024,1024]{1,0:T(8,128)(2,1)S(1)} %copy-done.5, f32[128,1024]{1,0:T(8,128)S(1)} %copy-done.18, f32[128,1024]{1,0:T(8,128)S(1)} %get-tuple-element.47.rows, ...), custom_call_target="tpu_custom_call" | custom-call | tf_op jit(solution)/shard_map/pallas_call | solution.py:408
  390.0 5.5 multiply_reduce_fusion
  402.2 20.7 %shard_map.397 = (bf16[4,128,1024]{2,1,0:T(8,128)(2,1)S(1)}, f32[128,1024]{1,0:T(8,128)}, f32[2,1024]{1,0:T(2,128)S(1)}) custom-call(bf16[512,256]{1,0:T(8,128)(2,1)S(1)} %copy.77.left, bf16[1024,256]{1,0:T(8,128)(2,1)S(1)} %copy-done.3, f32[128,1024]{1,0:T(8,128)S(1)} %copy-done.17, f32[128,1024]{1,0:T(8,128)S(1)} %copy-done.14, f32[1,1024]{1,0:T(1,128)S(1)} %bitcast.175), custom_call_target="tpu_custom_call" | custom-call | tf_op jit(solution)/shard_map/pallas_call | solution.py:408
  434.1 3.1 fusion.21
  438.8 5.3 fusion.18
  466.4 22.7 %convolution_convert_fusion.1 = bf16[1600,1024]{1,0:T(8,128)(2,1)S(1)} fusion(bf16[4096,1024]{1,0:T(8,128)(2,1)} %bitcast.239, f32[4096,1600]{0,1:T(8,128)} %get-tuple-element.173, f32[4096]{0:T(1024)S(1)} %get-tuple-element.157, f32[4096]{0:T(1024)S(1)} %mul.260, s32[4096]{0:T(1024)S(1)} %bitcast.221), kind=kOutput, calls=%fused_computation.23 | convolution fusion | flops 13462732800 | bytes 37928960 | tf_op jit(solution)/shard_map/dot_general | solution.py:25
  499.1 111.7 %psum.87 = f32[6,1024]{1,0:T(8,128)S(1)} all-reduce(f32[6,1024]{1,0:T(8,128)S(1)} %pad_maximum_fusion.1), channel_id=1, replica_groups=mesh['dp'=8,'mp'=4] {'dp','mp'}, use_global_device_ids=true, to_apply=%region_29.30 | all-reduce | flops 6144 | bytes 49152 | tf_op jit(solution)/shard_map/psum | solution.py:796
  615.4 3.1 collective-permute-start.10
  620.3 39.7 %collective-permute-done.9 = bf16[1600,128]{1,0:T(8,128)(2,1)S(1)} collective-permute-done((bf16[1600,128]{1,0:T(8,128)(2,1)}, bf16[1600,128]{1,0:T(8,128)(2,1)S(1)}, u32[]{:S(2)}, u32[]{:S(2)}) %collective-permute-start.9) | collective-permute-done | bytes 409632 | tf_op jit(solution)/shard_map/ppermute | solution.py:638
  669.6 4.4 convert_element_type.318
  678.1 130.0 %all-reduce.3.cloned.1.call-done = (bf16[1024,256]{0,1:T(8,128)(2,1)}, bf16[1024,256]{0,1:T(8,128)(2,1)}, bf16[1024,256]{0,1:T(8,128)(2,1)}, bf16[1024,256]{0,1:...) async-done(((bf16[1024,256]{0,1:T(8,128)(2,1)}, ...) | async-done | bytes 8388624 | tf_op jit(solution)/shard_map/psum | solution.py:811
  (333 shorter events, 135.9 us)
Async XLA Ops:
  8.0 666.0 %reduce-scatter.3.cloned.1.call-start = ((), (), s32[]{:S(2)}) async-start(), calls=%async_computation.2 | async-start | bytes 1310720 | tf_op jit(solution)/shard_map/reduce_scatter | solution.py:785
  13.6 189.4 %collective-permute-start.6 = (bf16[1600,128]{1,0:T(8,128)(2,1)}, bf16[1600,128]{1,0:T(8,128)(2,1)}, u32[]{:S(2)}, u32[]{:S(2)}) collective-permute-start(bf16[1600,128]{1,0:T(8,128)(2,1)} %get-tuple-element.146), channel_id=1, source_target_pairs={{0,28},{4,0},{8,4},{12,8},{16,12},{20,16},{24,20},{28,24},{1,29},{... | collective-permute-start | bytes 1228808 | tf_op jit(solution)/shard_map/ppermute | solution.py:622
  19.6 182.1 %collective-permute-start.4 = (bf16[1600,128]{1,0:T(8,128)(2,1)}, bf16[1600,128]{1,0:T(8,128)(2,1)}, u32[]{:S(2)}, u32[]{:S(2)}) collective-permute-start(bf16[1600,128]{1,0:T(8,128)(2,1)} %get-tuple-element.147), channel_id=1, source_target_pairs={{0,20},{4,24},{8,28},{12,0},{16,4},{20,8},{24,12},{28,16},{1,21},{... | collective-permute-start | bytes 1228808 | tf_op jit(solution)/shard_map/ppermute | solution.py:622
  19.6 180.9 %collective-permute-start.3 = (bf16[1600,128]{1,0:T(8,128)(2,1)}, bf16[1600,128]{1,0:T(8,128)(2,1)}, u32[]{:S(2)}, u32[]{:S(2)}) collective-permute-start(bf16[1600,128]{1,0:T(8,128)(2,1)} %get-tuple-element.148), channel_id=1, source_target_pairs={{0,16},{4,20},{8,24},{12,28},{16,0},{20,4},{24,8},{28,12},{1,17},{... | collective-permute-start | bytes 1228808 | tf_op jit(solution)/shard_map/ppermute | solution.py:622
  19.6 161.3 %collective-permute-start.1 = (bf16[1600,128]{1,0:T(8,128)(2,1)}, bf16[1600,128]{1,0:T(8,128)(2,1)}, u32[]{:S(2)}, u32[]{:S(2)}) collective-permute-start(bf16[1600,128]{1,0:T(8,128)(2,1)} %get-tuple-element.150), channel_id=1, source_target_pairs={{0,8},{4,12},{8,16},{12,20},{16,24},{20,28},{24,0},{28,4},{1,9},{5... | collective-permute-start | bytes 1228808 | tf_op jit(solution)/shard_map/ppermute | solution.py:622
  21.0 158.5 %collective-permute-start = (bf16[1600,128]{1,0:T(8,128)(2,1)}, bf16[1600,128]{1,0:T(8,128)(2,1)}, u32[]{:S(2)}, u32[]{:S(2)}) collective-permute-start(bf16[1600,128]{1,0:T(8,128)(2,1)} %get-tuple-element.151), channel_id=1, source_target_pairs={{0,4},{4,8},{8,12},{12,16},{16,20},{20,24},{24,28},{28,0},{1,5},{5... | collective-permute-start | bytes 1228808 | tf_op jit(solution)/shard_map/ppermute | solution.py:622
  103.6 75.9 %copy-start.83 = (bf16[1600,128]{1,0:T(8,128)(2,1)S(1)}, bf16[1600,128]{1,0:T(8,128)(2,1)}, u32[]{:S(2)}) copy-start(bf16[1600,128]{1,0:T(8,128)(2,1)} %get-tuple-element.149) | copy-start | bytes 1228804
  112.6 89.0 %copy-start.8 = (bf16[512,1024]{1,0:T(8,128)(2,1)}, bf16[512,1024]{1,0:T(8,128)(2,1)S(1)}, u32[]{:S(2)}) copy-start(bf16[512,1024]{1,0:T(8,128)(2,1)S(1)} %get-tuple-element.136.left) | copy-start | bytes 3145732
  112.6 67.0 %copy-start.41 = (bf16[1600,1024]{1,0:T(8,128)(2,1)S(1)}, bf16[1600,1024]{1,0:T(8,128)(2,1)}, u32[]{:S(2)}) copy-start(bf16[1600,1024]{1,0:T(8,128)(2,1)} %copy-done.40) | copy-start | bytes 9830404
  112.6 68.3 %copy-start.82 = (bf16[1600,128]{1,0:T(8,128)(2,1)S(1)}, bf16[1600,128]{1,0:T(8,128)(2,1)}, u32[]{:S(2)}) copy-start(bf16[1600,128]{1,0:T(8,128)(2,1)} %get-tuple-element.153) | copy-start | bytes 1228804
  179.5 46.9 %copy-start.15 = (f32[128,1024]{1,0:T(8,128)}, f32[128,1024]{1,0:T(8,128)S(1)}, u32[]{:S(2)}) copy-start(f32[128,1024]{1,0:T(8,128)S(1)} %get-tuple-element.44.rows) | copy-start | bytes 1572868
  179.5 20.8 %collective-permute-start.2 = (bf16[1600,128]{1,0:T(8,128)(2,1)S(1)}, bf16[1600,128]{1,0:T(8,128)(2,1)S(1)}, u32[]{:S(2)}, u32[]{:S(2)}) collective-permute-start(bf16[1600,128]{1,0:T(8,128)(2,1)S(1)} %copy-done.83), channel_id=1, source_target_pairs={{0,12},{4,16},{8,20},{12,24},{16,28},{20,0},{24,4},{28,8},{1,13},{... | collective-permute-start | bytes 1228808 | tf_op jit(solution)/shard_map/ppermute | solution.py:622
  180.8 21.9 %collective-permute-start.5 = (bf16[1600,128]{1,0:T(8,128)(2,1)S(1)}, bf16[1600,128]{1,0:T(8,128)(2,1)S(1)}, u32[]{:S(2)}, u32[]{:S(2)}) collective-permute-start(bf16[1600,128]{1,0:T(8,128)(2,1)S(1)} %copy-done.82), channel_id=1, source_target_pairs={{0,24},{4,28},{8,0},{12,4},{16,8},{20,12},{24,16},{28,20},{1,25},{... | collective-permute-start | bytes 1228808 | tf_op jit(solution)/shard_map/ppermute | solution.py:622
  226.3 38.9 %copy-start.92 = (f32[16]{0:T(128)S(1)}, f32[16]{0:T(128)}, u32[]{:S(2)}) copy-start(f32[16]{0:T(128)} %log.42) | copy-start | bytes 196
  434.0 242.0 %reduce-scatter.5.cloned.1.call-start = ((), (), s32[]{:S(2)}) async-start(), calls=%async_computation.3 | async-start | bytes 2621440 | tf_op jit(solution)/shard_map/reduce_scatter | solution.py:788
  447.0 361.1 %all-reduce.3.cloned.1.call-start = ((), (), s32[]{:S(2)}) async-start(), calls=%async_computation.4 | async-start | bytes 16777216 | tf_op jit(solution)/shard_map/psum | solution.py:811
  491.0 120.3 %copy-start.91 = (f32[16]{0:T(128)S(1)}, f32[16]{0:T(128)}, u32[]{:S(2)}) copy-start(f32[16]{0:T(128)} %copy-done.90) | copy-start | bytes 196
  493.0 174.8 %collective-permute-start.13 = (bf16[1600,128]{1,0:T(8,128)(2,1)S(1)}, bf16[1600,128]{1,0:T(8,128)(2,1)}, u32[]{:S(2)}, u32[]{:S(2)}) collective-permute-start(bf16[1600,128]{1,0:T(8,128)(2,1)S(1)} %get-tuple-element.138), channel_id=1, source_target_pairs={{0,28},{4,0},{8,4},{12,8},{16,12},{20,16},{24,20},{28,24},{1,29},{... | collective-permute-start | bytes 1228808 | tf_op jit(solution)/shard_map/ppermute | solution.py:638
  495.5 170.5 %collective-permute-start.12 = (bf16[1600,128]{1,0:T(8,128)(2,1)S(1)}, bf16[1600,128]{1,0:T(8,128)(2,1)}, u32[]{:S(2)}, u32[]{:S(2)}) collective-permute-start(bf16[1600,128]{1,0:T(8,128)(2,1)S(1)} %get-tuple-element.139), channel_id=1, source_target_pairs={{0,24},{4,28},{8,0},{12,4},{16,8},{20,12},{24,16},{28,20},{1,25},{... | collective-permute-start | bytes 1228808 | tf_op jit(solution)/shard_map/ppermute | solution.py:638
  495.5 168.7 %collective-permute-start.11 = (bf16[1600,128]{1,0:T(8,128)(2,1)}, bf16[1600,128]{1,0:T(8,128)(2,1)}, u32[]{:S(2)}, u32[]{:S(2)}) collective-permute-start(bf16[1600,128]{1,0:T(8,128)(2,1)} %get-tuple-element.140), channel_id=1, source_target_pairs={{0,20},{4,24},{8,28},{12,0},{16,4},{20,8},{24,12},{28,16},{1,21},{... | collective-permute-start | bytes 1228808 | tf_op jit(solution)/shard_map/ppermute | solution.py:638
  495.5 119.9 %collective-permute-start.8 = (bf16[1600,128]{1,0:T(8,128)(2,1)}, bf16[1600,128]{1,0:T(8,128)(2,1)}, u32[]{:S(2)}, u32[]{:S(2)}) collective-permute-start(bf16[1600,128]{1,0:T(8,128)(2,1)} %get-tuple-element.143), channel_id=1, source_target_pairs={{0,8},{4,12},{8,16},{12,20},{16,24},{20,28},{24,0},{28,4},{1,9},{5... | collective-permute-start | bytes 1228808 | tf_op jit(solution)/shard_map/ppermute | solution.py:638
  497.6 114.4 %collective-permute-start.7 = (bf16[1600,128]{1,0:T(8,128)(2,1)}, bf16[1600,128]{1,0:T(8,128)(2,1)}, u32[]{:S(2)}, u32[]{:S(2)}) collective-permute-start(bf16[1600,128]{1,0:T(8,128)(2,1)} %get-tuple-element.144), channel_id=1, source_target_pairs={{0,4},{4,8},{8,12},{12,16},{16,20},{20,24},{24,28},{28,0},{1,5},{5... | collective-permute-start | bytes 1228808 | tf_op jit(solution)/shard_map/ppermute | solution.py:638
  612.0 48.0 %collective-permute-start.9 = (bf16[1600,128]{1,0:T(8,128)(2,1)}, bf16[1600,128]{1,0:T(8,128)(2,1)S(1)}, u32[]{:S(2)}, u32[]{:S(2)}) collective-permute-start(bf16[1600,128]{1,0:T(8,128)(2,1)} %get-tuple-element.142), channel_id=1, source_target_pairs={{0,12},{4,16},{8,20},{12,24},{16,28},{20,0},{24,4},{28,8},{1,13},{... | collective-permute-start | bytes 1228808 | tf_op jit(solution)/shard_map/ppermute | solution.py:638
  615.4 48.1 %collective-permute-start.10 = (bf16[1600,128]{1,0:T(8,128)(2,1)}, bf16[1600,128]{1,0:T(8,128)(2,1)S(1)}, u32[]{:S(2)}, u32[]{:S(2)}) collective-permute-start(bf16[1600,128]{1,0:T(8,128)(2,1)} %get-tuple-element.141), channel_id=1, source_target_pairs={{0,16},{4,20},{8,24},{12,28},{16,0},{20,4},{24,8},{28,12},{1,17},{... | collective-permute-start | bytes 1228808 | tf_op jit(solution)/shard_map/ppermute | solution.py:638
  (89 other events, 614.7 us)
Sparse Core Ops, SparseCore 0:
  434.1 23.5 reduce-scatter.2
  461.0 31.3 reduce-scatter.4
Sparse Core Ops, SparseCore 1:
  465.7 342.3 all-reduce.2

commit v3 on v2

--- a/solution.py
+++ b/solution.py
@@ -174,6 +174,41 @@
     return [to_far, to_near, passed]
 
 
+def table_copies(masks, back, source, target, sems):
+    block, place = lax.axis_index("dp"), lax.axis_index("mp")
+    total = lax.axis_size("dp")
+    part, width = (source if back else target).shape[0], (target if back else source).shape[1]
+    copies = []
+    for slot, mask in enumerate(masks):
+        other = flip(block, mask)
+        here = pl.ds(pl.multiple_of((block if back else other) * part, part), part)
+        there = pl.ds(pl.multiple_of((other if back else block) * width, width), width)
+        if back:
+            start, end = source.at[:, there], target.at[here, :]
+        else:
+            start, end = source.at[here, :], target.at[:, there]
+        if mask:
+            copies.append(remote(start, end, sems.at[0, slot], sems.at[1, slot], (other, place)))
+        else:
+            copy = pltpu.make_async_copy(start, end, sems.at[0, slot])
+            copy.start()
+            copies.append(copy)
+    return copies
+
+
+def finish(copies):
+    for copy in copies:
+        copy.wait()
+
+
+def split_refs(refs, *counts):
+    groups, start = [], 0
+    for count in counts:
+        groups.append(list(refs[start : start + count]))
+        start += count
+    return groups
+
+
 def norm_rows(rows, gain, shift):
     center = rows - jnp.mean(rows, axis=-1, keepdims=True)
     spread = jnp.mean(center * center, axis=-1, keepdims=True)
@@ -211,25 +246,30 @@
     ]
 
 
-def mix_norm_kernel(
-    total, left, weight, kept, gain, shift, ids, quarters, normed, rows, ids_all,
-    sib_send, sib_recv, far_send, far_recv, sems, ids_sems, ids_local,
-):
+def mix_norm_kernel(total, with_ids, masks, chained, *refs):
+    (left, weight, kept, gain, shift), ids, table, (quarters, normed, rows), ids_all, wide, refs = (
+        split_refs(
+            refs, 5, with_ids, (1 + chained) * bool(masks), 3, with_ids, bool(masks), len(refs)
+        )
+    )
+    sib_send, sib_recv, far_send, far_recv, sems = refs[:5]
+    refs = refs[5:]
     block, place = lax.axis_index("dp"), lax.axis_index("mp")
     near, far = (block, flip(place, 1)), (block, flip(place, 2))
     height = kept.shape[0]
-    peers = [near, far]
-    if ids is not None:
-        peers += [(flip(block, mask), place) for mask in range(1, total)]
-    greet(peers)
+    others = range(1, total) if with_ids else [mask for mask in masks if mask]
+    greet([near, far] + [(flip(block, mask), place) for mask in others])
     copies = []
-    if ids is not None:
-        own = pltpu.make_async_copy(ids, ids_all.at[block], ids_local)
+    if with_ids:
+        ids_sems, ids_local = refs[:2]
+        refs = refs[2:]
+        own = pltpu.make_async_copy(ids[0], ids_all[0].at[block], ids_local)
         own.start()
+        copies.append(own)
         for mask in range(1, total):
             copies.append(
                 remote(
-                    ids, ids_all.at[block], ids_sems.at[0, mask], ids_sems.at[1, mask],
+                    ids[0], ids_all[0].at[block], ids_sems.at[0, mask], ids_sems.at[1, mask],
                     (flip(block, mask), place),
                 )
             )
@@ -239,49 +279,61 @@
             rows_of(left, height, index), weight[...], preferred_element_type=jnp.float32
         )
 
-    branch, more = sum_quarter(
+    branch, sent = sum_quarter(
         place, block_of, near, far, sib_send, sib_recv, far_send, far_recv, sems
     )
+    if masks:
+        copies += table_copies(masks, False, table[0], wide[0], refs[0])
     outcome = kept[...].astype(jnp.float32) + branch
     rows[...] = outcome
     outcome = norm_rows(outcome, gain[...], shift[...])
     normed[...] = outcome
     quarters[place] = outcome.astype(jnp.bfloat16)
-    more += share_quarter(place, quarters, near, far, sems)
-    for copy in copies:
-        copy.wait_recv()
-    for copy in copies + more:
+    sent += share_quarter(place, quarters, near, far, sems)
+    finish(copies)
+    for copy in sent:
         copy.wait_send()
-    if ids is not None:
-        own.wait()
-
-
-def mix_norm(left, weight, kept, gain, shift, number, ids=None):
+
+
+def mix_norm(left, weight, kept, gain, shift, number, ids=None, table=None, wide=None, masks=()):
     height, width = kept.shape
     total = lax.axis_size("dp")
     quarter = jax.ShapeDtypeStruct((height, width), jnp.float32)
     out_shape = [
         jax.ShapeDtypeStruct((QUARTERS, height, width), jnp.bfloat16), quarter, quarter
     ]
+    out_specs = [VMEM] * 3
     given = [left, weight, kept, gain.reshape(1, -1), shift.reshape(1, -1)]
+    in_specs = [VMEM] * 5
     scratch = exchange_scratch(height, width)
-    if ids is None:
-        def kernel(left, weight, kept, gain, shift, quarters, normed, rows, *scratch):
-            mix_norm_kernel(
-                total, left, weight, kept, gain, shift, None, quarters, normed, rows, None,
-                *scratch, None, None,
-            )
-    else:
-        kernel = functools.partial(mix_norm_kernel, total)
+    aliases = {}
+    if ids is not None:
         given.append(ids)
+        in_specs.append(VMEM)
         out_shape.append(jax.ShapeDtypeStruct((total,) + ids.shape, ids.dtype))
+        out_specs.append(VMEM)
         scratch += [DMA((2, total)), DMA]
+    if masks:
+        given.append(table)
+        in_specs.append(ANY)
+        if wide is not None:
+            aliases = {len(given): len(out_shape)}
+            given.append(wide)
+            in_specs.append(ANY)
+        out_shape.append(
+            jax.ShapeDtypeStruct((table.shape[0] // total, table.shape[1] * total), table.dtype)
+        )
+        out_specs.append(ANY)
+        scratch.append(DMA((2, len(masks))))
     outcome = pl.pallas_call(
-        kernel,
+        functools.partial(
+            mix_norm_kernel, total, int(ids is not None), tuple(masks), int(wide is not None)
+        ),
         out_shape=out_shape,
-        in_specs=[VMEM] * len(given),
-        out_specs=[VMEM] * len(out_shape),
+        in_specs=in_specs,
+        out_specs=out_specs,
         scratch_shapes=scratch,
+        input_output_aliases=aliases,
         compiler_params=pltpu.CompilerParams(
             collective_id=number, has_side_effects=True, vmem_limit_bytes=48 * 2**20
         ),
@@ -289,21 +341,26 @@
     return (outcome[0].reshape(-1, width),) + tuple(outcome[1:])
 
 
-def feed_norm_kernel(
-    total, left, weight, kept, gain, shift, states, rows,
-    low, sib_send, sib_recv, far_send, far_recv, sems, hops, own_sem,
-):
+def feed_norm_kernel(total, early, late, *refs):
+    (left, weight, kept, gain, shift), table, (states, rows), wide, refs = split_refs(
+        refs, 5, 2 * bool(early), 2, bool(early), len(refs)
+    )
+    low, sib_send, sib_recv, far_send, far_recv, sems, hops, own_sem = refs[:8]
     block, place = lax.axis_index("dp"), lax.axis_index("mp")
     near, far = (block, flip(place, 1)), (block, flip(place, 2))
     beside = (flip(block, 1), place)
     height = kept.shape[0]
-    greet([near, far, beside] + [(flip(block, mask), place) for mask in range(2, total, 2)])
+    others = range(1, total) if early else [1] + list(range(2, total, 2))
+    greet([near, far] + [(flip(block, mask), place) for mask in others])
 
     def block_of(index):
         return jnp.dot(
             rows_of(left, height, index), weight[...], preferred_element_type=jnp.float32
         )
 
+    moved = []
+    if early:
+        moved = table_copies(early, False, table[0], wide[0], refs[8])
     branch, sent = sum_quarter(
         place, block_of, near, far, sib_send, sib_recv, far_send, far_recv, sems
     )
@@ -324,6 +381,8 @@
     first = {}
     for mask in range(2, total, 2):
         first[mask] = hop(0, mask, low, (flip(block, mask), place), block, place)
+    if late:
+        moved += table_copies(late, False, table[0], wide[0], refs[9])
     over = {}
     ends = []
 
@@ -350,37 +409,55 @@
     for copy in sent:
         copy.wait_send()
     own.wait()
-
-
-def feed_norm(left, weight, kept, gain, shift, number):
+    finish(moved)
+
+
+def feed_norm(left, weight, kept, gain, shift, number, table=None, wide=None, early=(), late=()):
     height, width = kept.shape
     total = lax.axis_size("dp")
-    states, rows = pl.pallas_call(
-        functools.partial(feed_norm_kernel, total),
-        out_shape=[
-            jax.ShapeDtypeStruct((total, QUARTERS, height, width), jnp.bfloat16),
-            jax.ShapeDtypeStruct((height, width), jnp.float32),
-        ],
-        in_specs=[VMEM] * 5,
-        out_specs=[ANY, VMEM],
-        scratch_shapes=[pltpu.VMEM((height, width), jnp.bfloat16)]
-        + exchange_scratch(height, width)
-        + [DMA((2, 4, total)), DMA],
+    given = [left, weight, kept, gain.reshape(1, -1), shift.reshape(1, -1)]
+    in_specs = [VMEM] * 5
+    out_shape = [
+        jax.ShapeDtypeStruct((total, QUARTERS, height, width), jnp.bfloat16),
+        jax.ShapeDtypeStruct((height, width), jnp.float32),
+    ]
+    out_specs = [ANY, VMEM]
+    scratch = [pltpu.VMEM((height, width), jnp.bfloat16)] + exchange_scratch(height, width)
+    scratch += [DMA((2, 4, total)), DMA]
+    aliases = {}
+    if early:
+        given += [table, wide]
+        in_specs += [ANY] * 2
+        out_shape.append(jax.ShapeDtypeStruct(wide.shape, wide.dtype))
+        out_specs.append(ANY)
+        aliases = {6: 2}
+        scratch += [DMA((2, len(early))), DMA((2, len(late)))]
+    outcome = pl.pallas_call(
+        functools.partial(feed_norm_kernel, total, tuple(early), tuple(late)),
+        out_shape=out_shape,
+        in_specs=in_specs,
+        out_specs=out_specs,
+        scratch_shapes=scratch,
+        input_output_aliases=aliases,
         compiler_params=pltpu.CompilerParams(
             collective_id=number, has_side_effects=True, vmem_limit_bytes=48 * 2**20
         ),
-    )(left, weight, kept, gain.reshape(1, -1), shift.reshape(1, -1))
-    return states.reshape(-1, width), rows
-
-
-def back_norm_kernel(
-    left, weight, kept, rows, gain, quarters, grad_rows, grad_vecs,
-    sib_send, sib_recv, far_send, far_recv, sems,
-):
+    )(*given)
+    return (outcome[0].reshape(-1, width),) + tuple(outcome[1:])
+
+
+def back_norm_kernel(masks, *refs):
+    (left, weight, kept, rows, gain), table, (quarters, grad_rows, grad_vecs), narrow, refs = (
+        split_refs(refs, 5, 2 * bool(masks), 3, bool(masks), len(refs))
+    )
+    sib_send, sib_recv, far_send, far_recv, sems = refs[:5]
     block, place = lax.axis_index("dp"), lax.axis_index("mp")
     near, far = (block, flip(place, 1)), (block, flip(place, 2))
     height = kept.shape[0]
-    greet([near, far])
+    greet([near, far] + [(flip(block, mask), place) for mask in masks])
+    moved = []
+    if masks:
+        moved = table_copies(masks, True, table[0], narrow[0], refs[5])
 
     def block_of(index):
         return lax.dot_general(
@@ -401,25 +478,40 @@
     sent += share_quarter(place, quarters, near, far, sems)
     for copy in sent:
         copy.wait_send()
-
-
-def back_norm(left, weight, kept, rows, gain, number):
+    finish(moved)
+
+
+def back_norm(left, weight, kept, rows, gain, number, table=None, narrow=None, masks=()):
     height, width = kept.shape
-    quarters, grad_rows, grad_vecs = pl.pallas_call(
-        back_norm_kernel,
-        out_shape=[
-            jax.ShapeDtypeStruct((QUARTERS, height, width), jnp.bfloat16),
-            jax.ShapeDtypeStruct((height, width), jnp.float32),
-            jax.ShapeDtypeStruct((2, width), jnp.float32),
-        ],
-        in_specs=[VMEM] * 5,
-        out_specs=[VMEM] * 3,
-        scratch_shapes=exchange_scratch(height, width),
+    given = [left, weight, kept, rows, gain.reshape(1, -1)]
+    in_specs = [VMEM] * 5
+    out_shape = [
+        jax.ShapeDtypeStruct((QUARTERS, height, width), jnp.bfloat16),
+        jax.ShapeDtypeStruct((height, width), jnp.float32),
+        jax.ShapeDtypeStruct((2, width), jnp.float32),
+    ]
+    out_specs = [VMEM] * 3
+    scratch = exchange_scratch(height, width)
+    aliases = {}
+    if masks:
+        given += [table, narrow]
+        in_specs += [ANY] * 2
+        out_shape.append(jax.ShapeDtypeStruct(narrow.shape, narrow.dtype))
+        out_specs.append(ANY)
+        aliases = {6: 3}
+        scratch.append(DMA((2, len(masks))))
+    outcome = pl.pallas_call(
+        functools.partial(back_norm_kernel, tuple(masks)),
+        out_shape=out_shape,
+        in_specs=in_specs,
+        out_specs=out_specs,
+        scratch_shapes=scratch,
+        input_output_aliases=aliases,
         compiler_params=pltpu.CompilerParams(
             collective_id=number, has_side_effects=True, vmem_limit_bytes=48 * 2**20
         ),
-    )(left, weight, kept, rows, gain.reshape(1, -1))
-    return quarters.reshape(-1, width), grad_rows, grad_vecs
+    )(*given)
+    return (outcome[0].reshape(-1, width),) + tuple(outcome[1:])
 
 
 def join_totals_kernel(total, given, outcome, sends, recvs, sems):
@@ -476,15 +568,20 @@
     return outcome.reshape(3, -1)
 
 
-def head_back_kernel(
-    total, parts, rows, gain, quarters, grad_rows, grad_vecs,
-    mine, sib_recv, far_recv, beside_recv, end_recv, sems, sib_sems, far_sems, beside_sems,
-    end_sems, load_sems,
-):
+def head_back_kernel(total, masks, *refs):
+    (parts, rows, gain), table, (quarters, grad_rows, grad_vecs), narrow, refs = split_refs(
+        refs, 3, bool(masks), 3, bool(masks), len(refs)
+    )
+    mine, sib_recv, far_recv, beside_recv, end_recv, sems = refs[:6]
+    sib_sems, far_sems, beside_sems, end_sems, load_sems = refs[6:11]
     block, place = lax.axis_index("dp"), lax.axis_index("mp")
     near, far = (block, flip(place, 1)), (block, flip(place, 2))
     beside = (flip(block, 1), place)
-    greet([near, far, beside] + [(flip(block, mask), place) for mask in range(2, total, 2)])
+    others = range(1, total) if masks else [1] + list(range(2, total, 2))
+    greet([near, far] + [(flip(block, mask), place) for mask in others])
+    moved = []
+    if masks:
+        moved = table_copies(masks, True, table[0], narrow[0], refs[11])
     order = [mask for mask in range(total - 1, -1, -1) if mask % 2]
     order += [mask for mask in range(total - 1, -1, -1) if mask % 2 == 0]
     sent, loads, sib, across, over, ends = [], {}, {}, {}, {}, {}
@@ -570,40 +667,197 @@
     sent += share_quarter(place, quarters, near, far, sems)
     for copy in sent:
         copy.wait_send()
-
-
-def head_back(parts, rows, gain, number):
+    finish(moved)
+
+
+def head_back(parts, rows, gain, number, table=None, masks=()):
     height, width = rows.shape
     total = lax.axis_size("dp")
     half = total // 2
     block = (height, width)
-    quarters, grad_rows, grad_vecs = pl.pallas_call(
-        functools.partial(head_back_kernel, total),
-        out_shape=[
-            jax.ShapeDtypeStruct((QUARTERS,) + block, jnp.bfloat16),
-            jax.ShapeDtypeStruct(block, jnp.float32),
-            jax.ShapeDtypeStruct((2, width), jnp.float32),
-        ],
-        in_specs=[ANY, VMEM, VMEM],
-        out_specs=[VMEM] * 3,
-        scratch_shapes=[
-            pltpu.VMEM((total, 2) + block, jnp.bfloat16),
-            pltpu.VMEM((total, 2) + block, jnp.bfloat16),
-            pltpu.VMEM((total,) + block, jnp.bfloat16),
-            pltpu.VMEM((half,) + block, jnp.bfloat16),
-            pltpu.VMEM((half,) + block, jnp.bfloat16),
-            DMA((2, 6)),
-            DMA((2, total, 2)),
-            DMA((2, total)),
-            DMA((2, half)),
-            DMA((2, half)),
-            DMA((total, 2)),
-        ],
+    given = [parts.reshape((total, QUARTERS) + block), rows, gain.reshape(1, -1)]
+    in_specs = [ANY, VMEM, VMEM]
+    out_shape = [
+        jax.ShapeDtypeStruct((QUARTERS,) + block, jnp.bfloat16),
+        jax.ShapeDtypeStruct(block, jnp.float32),
+        jax.ShapeDtypeStruct((2, width), jnp.float32),
+    ]
+    out_specs = [VMEM] * 3
+    scratch = [
+        pltpu.VMEM((total, 2) + block, jnp.bfloat16),
+        pltpu.VMEM((total, 2) + block, jnp.bfloat16),
+        pltpu.VMEM((total,) + block, jnp.bfloat16),
+        pltpu.VMEM((half,) + block, jnp.bfloat16),
+        pltpu.VMEM((half,) + block, jnp.bfloat16),
+        DMA((2, 6)),
+        DMA((2, total, 2)),
+        DMA((2, total)),
+        DMA((2, half)),
+        DMA((2, half)),
+        DMA((total, 2)),
+    ]
+    if masks:
+        given.append(table)
+        in_specs.append(ANY)
+        out_shape.append(
+            jax.ShapeDtypeStruct((table.shape[0] * total, table.shape[1] // total), table.dtype)
+        )
+        out_specs.append(ANY)
+        scratch.append(DMA((2, len(masks))))
+    outcome = pl.pallas_call(
+        functools.partial(head_back_kernel, total, tuple(masks)),
+        out_shape=out_shape,
+        in_specs=in_specs,
+        out_specs=out_specs,
+        scratch_shapes=scratch,
         compiler_params=pltpu.CompilerParams(
             collective_id=number, has_side_effects=True, vmem_limit_bytes=60 * 2**20
         ),
-    )(parts.reshape((total, QUARTERS) + block), rows, gain.reshape(1, -1))
-    return quarters.reshape(-1, width), grad_rows, grad_vecs
+    )(*given)
+    return (outcome[0].reshape(-1, width),) + tuple(outcome[1:])
+
+
+def join_weights_kernel(total, orders, given, vecs, outcome, vec_sums, work, recv, vec_send,
+                        vec_recv, sum_sems, gather_sems, vec_sems):
+    block, place = lax.axis_index("dp"), lax.axis_index("mp")
+    bits = (total - 1).bit_length()
+    height = given.shape[1]
+    near, far = (block, flip(place, 1)), (block, flip(place, 2))
+    over = [(flip(block, 1 << bit), place) for bit in range(bits)]
+    sides = [lax.rem(lax.div(block, 1 << bit), 2) for bit in range(bits)]
+    greet([near, far] + over)
+    pieces = range(len(orders))
+    kept = [[0] for _ in pieces]
+    copies, sent = {}, []
+
+    def part(ref, piece, start, rows):
+        unit = height >> bits
+        return ref.at[piece, pl.ds(pl.multiple_of(start, unit), rows), :]
+
+    def send_sum(piece, stage):
+        bit, rows = orders[piece][stage], height >> (stage + 1)
+        start = kept[piece][stage]
+        away = start + (1 - sides[bit]) * rows
+        kept[piece].append(start + sides[bit] * rows)
+        offset = height - 2 * rows
+        copies[piece, stage] = remote(
+            part(work if stage else given, piece, away, rows),
+            recv.at[piece, pl.ds(offset, rows), :],
+            sum_sems.at[0, piece, stage],
+            sum_sems.at[1, piece, stage],
+            over[bit],
+        )
+        sent.append(copies[piece, stage])
+
+    def take_sum(piece, stage):
+        rows = height >> (stage + 1)
+        copies[piece, stage].wait_recv()
+        start = kept[piece][stage + 1]
+        offset = height - 2 * rows
+        part(work if stage + 1 < bits else outcome, piece, start, rows)[...] = (
+            part(work if stage else given, piece, start, rows)[...].astype(jnp.float32)
+            + recv[piece, pl.ds(offset, rows), :].astype(jnp.float32)
+        ).astype(outcome.dtype)
+
+    def send_whole(piece, stage):
+        rows = height >> (stage + 1)
+        here = part(outcome, piece, kept[piece][stage + 1], rows)
+        copies[piece, stage, "whole"] = remote(
+            here, here, gather_sems.at[0, piece, stage], gather_sems.at[1, piece, stage],
+            over[orders[piece][stage]],
+        )
+        sent.append(copies[piece, stage, "whole"])
+
+    vec_peers = [(near, lax.rem(place, 2)), (far, lax.div(place, 2))]
+    vec_peers += list(zip(over, sides))
+    vec_copies = {}
+
+    def vec_start(stage, value):
+        vec_send[stage] = value
+        vec_copies[stage] = remote(
+            vec_send.at[stage], vec_recv.at[stage], vec_sems.at[0, stage], vec_sems.at[1, stage],
+            vec_peers[stage][0],
+        )
+        sent.append(vec_copies[stage])
+
+    def vec_end(stage):
+        vec_copies[stage].wait_recv()
+        return vec_send[stage] + vec_recv[stage]
+
+    for piece in pieces:
+        send_sum(piece, 0)
+    vec_start(0, vecs[...])
+    stages = len(vec_peers)
+    done = 0
+
+    def vec_next(done):
+        if done < stages:
+            value = vec_end(done)
+            if done + 1 < stages:
+                vec_start(done + 1, value)
+            else:
+                vec_sums[...] = value
+        return done + 1
+
+    for stage in range(bits):
+        for piece in pieces:
+            take_sum(piece, stage)
+            if stage + 1 < bits:
+                send_sum(piece, stage + 1)
+            else:
+                send_whole(piece, stage)
+        done = vec_next(done)
+    for stage in range(bits - 1, -1, -1):
+        for piece in pieces:
+            copies[piece, stage, "whole"].wait_recv()
+            if stage:
+                send_whole(piece, stage - 1)
+        done = vec_next(done)
+    while done < stages:
+        done = vec_next(done)
+    for copy in sent:
+        copy.wait_send()
+
+
+def join_weights(given, vecs, number):
+    total = lax.axis_size("dp")
+    bits = (total - 1).bit_length()
+    rest = list(range(2, bits))
+    orders = [[0, 1] + rest if piece % 4 else [1, 0] + rest for piece in range(given.shape[0])]
+    stages = bits + 2
+    return pl.pallas_call(
+        functools.partial(join_weights_kernel, total, orders),
+        out_shape=[
+            jax.ShapeDtypeStruct(given.shape, given.dtype),
+            jax.ShapeDtypeStruct(vecs.shape, vecs.dtype),
+        ],
+        in_specs=[VMEM] * 2,
+        out_specs=[VMEM] * 2,
+        scratch_shapes=[
+            pltpu.VMEM(given.shape, given.dtype),
+            pltpu.VMEM(given.shape, given.dtype),
+            pltpu.VMEM((stages,) + vecs.shape, vecs.dtype),
+            pltpu.VMEM((stages,) + vecs.shape, vecs.dtype),
+            DMA((2, given.shape[0], bits)),
+            DMA((2, given.shape[0], bits)),
+            DMA((2, stages)),
+        ],
+        compiler_params=pltpu.CompilerParams(
+            collective_id=number, has_side_effects=True, vmem_limit_bytes=48 * 2**20
+        ),
+    )(given, vecs)
+
+
+def fold(matrix, width):
+    return jnp.concatenate(
+        [matrix[:, start : start + width] for start in range(0, matrix.shape[1], width)], axis=0
+    )
+
+
+def unfold(matrix, height):
+    return jnp.concatenate(
+        [matrix[start : start + height] for start in range(0, matrix.shape[0], height)], axis=1
+    )
 
 
 def shift_pairs(total, step):
@@ -669,7 +923,8 @@
     embedding,
 ):
     row_count, row_len = segment_ids.shape
-    table_rows = spread_rows(embedding)
+    total = lax.axis_size("dp")
+    direct = total == 8 and embedding.shape[1] % 128 == 0
     span = SEG_ROW * MEM
     quarter = tokens.shape[0] // QUARTERS
     inputs = lax.dynamic_slice_in_dim(tokens, lax.axis_index("mp") * quarter, quarter, 0)
@@ -683,9 +938,10 @@
     key_self = product(tokens, self_key).astype(jnp.bfloat16)
     value_self = product(tokens, self_value).astype(jnp.bfloat16)
     self_mix, self_totals = run_rows(query_self, key_self, value_self, self_masks)
-    first_low, first_norm, rows_self, ids_all = mix_norm(
+    first_low, first_norm, rows_self, ids_all, *wide = mix_norm(
         self_mix, self_out, inputs, gain_self, shift_self, 0,
         jnp.concatenate([segment_ids, answer_ids, loss_mask], axis=0),
+        embedding, None, (4, 1, 0) if direct else (),
     )
     segments_all, answers_all, kept_all = (
         ids_all[:, kind * row_count : (kind + 1) * row_count].reshape(-1, row_len)
@@ -695,14 +951,17 @@
     key_cross = product(memory, cross_key).astype(jnp.bfloat16)
     value_cross = product(memory, cross_value).astype(jnp.bfloat16)
     cross_mix, cross_totals = run_rows(query_cross, key_cross, value_cross, cross_masks)
-    second_low, second_norm, rows_cross = mix_norm(
-        cross_mix, cross_out, first_norm, gain_cross, shift_cross, 1
+    second_low, second_norm, rows_cross, *wide = mix_norm(
+        cross_mix, cross_out, first_norm, gain_cross, shift_cross, 1, None,
+        embedding, *wide, masks=(5, 2) if direct else (),
     )
     feed_pre = product(second_low, feed_up)
     feed_act = gelu_exact(feed_pre).astype(jnp.bfloat16)
-    states, rows_feed = feed_norm(
-        feed_act, feed_down, second_norm, gain_feed, shift_feed, 2
-    )
+    states, rows_feed, *wide = feed_norm(
+        feed_act, feed_down, second_norm, gain_feed, shift_feed, 2,
+        embedding, *wide, early=(6, 3) if direct else (), late=(7,) if direct else (),
+    )
+    table_rows = wide[0] if direct else spread_rows(embedding)
     vocab_local = embedding.shape[0]
     part = table_rows.shape[0]
     logits = product_nt(states, table_rows)
@@ -742,19 +1001,26 @@
         grad_logp[:, None]
         * (answer_hot.astype(jnp.float32) - jnp.exp(logits - log_total[:, None]))
     ).astype(jnp.bfloat16)
-    grad_branch, grad_res3, grad_vecs_feed = head_back(
-        product(grad_logits, table_rows).astype(jnp.bfloat16), rows_feed, gain_feed, 4
-    )
-    grad_table = return_rows(
-        product_tn(grad_logits, states).astype(jnp.bfloat16), vocab_local
-    ).astype(jnp.float32)
+    grad_rows = product_tn(grad_logits, states).astype(jnp.bfloat16)
+    grad_states = product(grad_logits, table_rows).astype(jnp.bfloat16)
+    grad_states, grad_rows = lax.optimization_barrier((grad_states, grad_rows))
+    grad_branch, grad_res3, grad_vecs_feed, *narrow = head_back(
+        grad_states, rows_feed, gain_feed, 4, grad_rows, (4, 5, 1, 2, 3, 0) if direct else ()
+    )
     grad_feed_down = product_tn(feed_act, grad_branch)
     grad_act = product_nt(grad_branch, feed_down)
     act_value, act_pull = jax.vjp(gelu_exact, feed_pre)
     grad_pre = act_pull(grad_act)[0].astype(jnp.bfloat16)
     grad_feed_up = product_tn(second_low, grad_pre)
-    grad_branch, grad_res2, grad_vecs_cross = back_norm(
-        grad_pre, feed_up, grad_res3, rows_cross, gain_cross, 5
+    grad_pre, grad_feed_up, grad_feed_down = lax.optimization_barrier(
+        (grad_pre, grad_feed_up.astype(jnp.bfloat16), grad_feed_down.astype(jnp.bfloat16))
+    )
+    sum_up, sum_down = (
+        part.astype(jnp.float32) for part in lax.psum((grad_feed_up, grad_feed_down), "dp")
+    )
+    grad_branch, grad_res2, grad_vecs_cross, *narrow = back_norm(
+        grad_pre, feed_up, grad_res3, rows_cross, gain_cross, 5,
+        grad_rows, *narrow, masks=(6,) if direct else (),
     )
     grad_cross_out = product_tn(cross_mix, grad_branch)
     grad_mix = product_nt(grad_branch, cross_out).astype(jnp.bfloat16)
@@ -765,9 +1031,13 @@
     grad_cross_key = product_tn(memory, cross_gk)
     grad_cross_value = product_tn(memory, cross_gv)
     grad_memory_part = product_nt(cross_gk, cross_key) + product_nt(cross_gv, cross_value)
-    grad_branch, _, grad_vecs_self = back_norm(
-        cross_gq, cross_query, grad_res2, rows_self, gain_self, 6
-    )
+    grad_branch, _, grad_vecs_self, *narrow = back_norm(
+        cross_gq, cross_query, grad_res2, rows_self, gain_self, 6,
+        grad_rows, *narrow, masks=(7,) if direct else (),
+    )
+    grad_table = (
+        narrow[0] if direct else return_rows(grad_rows, vocab_local)
+    ).astype(jnp.float32)
     grad_self_out = product_tn(self_mix, grad_branch)
     grad_mix = product_nt(grad_branch, self_out).astype(jnp.bfloat16)
     self_gq, self_gk, self_gv = back_rows(
@@ -793,32 +1063,27 @@
     grad_tokens = input_share + lax.dynamic_slice_in_dim(
         grad_branch, column_start, input_share.shape[1], 1
     ).astype(jnp.float32)
-    grad_vecs = lax.psum(
-        jnp.concatenate([grad_vecs_self, grad_vecs_cross, grad_vecs_feed], axis=0), ("dp", "mp")
-    )
-    (
-        sum_sq,
-        sum_sk,
-        sum_sv,
-        sum_so,
-        sum_cq,
-        sum_ck,
-        sum_cv,
-        sum_co,
-        sum_up,
-        sum_down,
-    ) = (
-        lax.psum(grad_self_query.astype(jnp.bfloat16), "dp").astype(jnp.float32),
-        lax.psum(grad_self_key.astype(jnp.bfloat16), "dp").astype(jnp.float32),
-        lax.psum(grad_self_value.astype(jnp.bfloat16), "dp").astype(jnp.float32),
-        lax.psum(grad_self_out.astype(jnp.bfloat16), "dp").astype(jnp.float32),
-        lax.psum(grad_cross_query.astype(jnp.bfloat16), "dp").astype(jnp.float32),
-        lax.psum(grad_cross_key.astype(jnp.bfloat16), "dp").astype(jnp.float32),
-        lax.psum(grad_cross_value.astype(jnp.bfloat16), "dp").astype(jnp.float32),
-        lax.psum(grad_cross_out.astype(jnp.bfloat16), "dp").astype(jnp.float32),
-        lax.psum(grad_feed_up.astype(jnp.bfloat16), "dp").astype(jnp.float32),
-        lax.psum(grad_feed_down.astype(jnp.bfloat16), "dp").astype(jnp.float32),
-    )
+    width = grad_self_query.shape[1]
+    sums, grad_vecs = join_weights(
+        jnp.stack(
+            [
+                grad_cross_query,
+                grad_cross_key,
+                grad_cross_value,
+                fold(grad_cross_out, width),
+                grad_self_query,
+                grad_self_key,
+                grad_self_value,
+                fold(grad_self_out, width),
+            ]
+        ).astype(jnp.bfloat16),
+        jnp.concatenate([grad_vecs_self, grad_vecs_cross, grad_vecs_feed], axis=0),
+        7,
+    )
+    sum_cq, sum_ck, sum_cv, sum_co, sum_sq, sum_sk, sum_sv, sum_so = (
+        part.astype(jnp.float32) for part in sums
+    )
+    sum_co, sum_so = (unfold(part, grad_self_out.shape[0]) for part in (sum_co, sum_so))
     return (
         loss,
         grad_tokens,

time: 843 us -> 685 us (0.81)
  Pallas kernels: 257 us -> 433 us
  waiting for transfers between devices: 187 us -> 14.7 us
  blocking collectives: 112 us -> 0 us
  local copies, waits for them, and re-layouts: 49.2 us -> 17.6 us
  starting transfers between devices: 23.9 us -> 0.12 us
  other arithmetic: 40.5 us -> 51.1 us
    pallas_call x6 -> x7, Pallas kernels: 232 us -> 412 us  [the longest x1 157 us: join_weights(): pl.pallas_call(functools.partial(join_weights_kernel, total, orders), out...]
    psum x1, waiting for transfers between devices: 130 us -> 14.2 us  [local(): lax.psum((grad_feed_up, grad_feed_down), 'dp')]
    psum x1 -> x0, blocking collectives: 112 us -> none  [local(): lax.psum(jnp.concatenate([grad_vecs_self, grad_vecs_cross, grad_vecs_feed...]
    ppermute x14 -> x0, waiting for transfers between devices: 57.4 us -> none  [the longest x7 42.4 us: return_rows(): block = lax.ppermute(block, 'dp', shift_pairs(total, step))]
    ppermute x14 -> x0, starting transfers between devices: 23.5 us -> none  [the longest x7 12.9 us: spread_rows(): block = lax.ppermute(block, 'dp', shift_pairs(total, step))]
    dynamic_update_slice x14 -> x0, local copies, waits for them, and re-layouts: 16.6 us -> none  [the longest x7 10.5 us: return_rows(): lax.dynamic_update_slice_in_dim(whole, block, (place - step) % total * pa...]
    unnamed x200 -> x185, local copies, waits for them, and re-layouts: 22.8 us -> 12.3 us
  transfers between devices with their start and end apart: 17 -> 3, of which waited for: 4 -> 1; matrix products, arithmetic and copies ran while one was open for 13% -> 7% of each run, Pallas kernels for 14% -> 23%
where the time goes in v3:
time: 685 us; the launch traced here: 679 us
  Pallas kernels  433 us (63%)
  matrix products  143 us (21%)
  other arithmetic  51.1 us (7%)
  between operations  19 us (3%)
  local copies, waits for them, and re-layouts  17.6 us (3%)
  waiting for transfers between devices  14.7 us (2%)
    pallas_call x1, Pallas kernels, join_weights(): pl.pallas_call(functools.partial(join_weights_kernel, total, orders), out...  157 us
    pallas_call x1, Pallas kernels, feed_norm(): pl.pallas_call(functools.partial(feed_norm_kernel, total, tuple(early), t...  72.9 us
    pallas_call x1, Pallas kernels, head_back(): pl.pallas_call(functools.partial(head_back_kernel, total, tuple(masks)),...  72.3 us
    pallas_call x2, Pallas kernels, mix_norm(): pl.pallas_call(functools.partial(mix_norm_kernel, total, int(ids is not N...  66.4 us
    dot_general x11, matrix products, product_tn(): lax.dot_general(left_side, right_side, (((0,), (0,)), ((), ())), preferre...  44 us
    pallas_call x2, Pallas kernels, back_norm(): pl.pallas_call(functools.partial(back_norm_kernel, tuple(masks)), out_sha...  43.2 us
    dot_general x8, matrix products, product(): return jnp.dot(left_side, right_side, preferred_element_type=jnp.float32)  41 us
    dot_general x9, matrix products, product_nt(): lax.dot_general(left_side, right_side, (((1,), (1,)), ((), ())), preferre...  30.4 us
  transfers between devices with their start and end apart: 3, of which 1 were waited for; matrix products, arithmetic and copies ran while one was open for 7% of the time, Pallas kernels for 23%

profile of v3, /device:TPU:0, one launch (start us, length us, event | category | flops | bytes accessed | tf_op | source)
XLA Modules:
  0.0 679.2 jit_solution(4405764364958782800)
XLA Ops:
  26.1 35.4 %shard_map.391 = (bf16[4,128,1024]{2,1,0:T(8,128)(2,1)S(1)}, f32[128,1024]{1,0:T(8,128)S(1)}, f32[128,1024]{1,0:T(8,128)S(1)}, s32[8,3,512]{2,1,0:T(4,128)S(1)}, bf16[1600,1024]{1,0:T(8,128)(2,1)}) custom-call(bf16[512,256]{1,0:T(8,128)(2,1)S(1)} %copy.78.refs_0_, bf16[256,1024]{1,0:T(8,128)(2,1)S(1)} %copy-done.15, ...), custom_call_target="tpu_custom_call" | custom-call | tf_op jit(solution)/shard_map/pallas_call | solution.py:328
  71.6 31.1 %shard_map.392 = (bf16[4,128,1024]{2,1,0:T(8,128)(2,1)S(1)}, f32[128,1024]{1,0:T(8,128)S(1)}, f32[128,1024]{1,0:T(8,128)S(1)}, bf16[1600,1024]{1,0:T(8,128)(2,1)}) custom-call(bf16[512,256]{1,0:T(8,128)(2,1)S(1)} %copy.79.refs_0_, bf16[256,1024]{1,0:T(8,128)(2,1)S(1)} %copy-done.14, f32[128,1024]{1,0:T(8,128)S(1)} %copy-done.21, ...), custom_call_target="tpu_custom_call", output_to_operand_aliasing={{3}: (6, {})} | custom-call | tf_op jit(solution)/shard_map/pallas_call | solution.py:328
  103.5 6.9 %multiply_convert_fusion.3 = (bf16[512,1024]{1,0:T(8,128)(2,1)S(1)}, f32[512,1024]{1,0:T(8,128)}, f32[512,1024]{1,0:T(8,128)}) fusion(bf16[512,1024]{1,0:T(8,128)(2,1)S(1)} %bitcast.245, bf16[1024,1024]{1,0:T(8,128)(2,1)S(1)} %copy-done.1), kind=kOutput, calls=%fused_computation.32 | convolution fusion | flops 1107820544 | bytes 8388608 | tf_op jit(solution)/shard_map/dot_general | solution.py:21
  110.4 72.9 %shard_map.393 = (bf16[8,4,128,1024]{3,2,1,0:T(8,128)(2,1)}, f32[128,1024]{1,0:T(8,128)S(1)}, bf16[1600,1024]{1,0:T(8,128)(2,1)}) custom-call(bf16[512,1024]{1,0:T(8,128)(2,1)S(1)} %get-tuple-element.91.refs_0_, bf16[1024,1024]{1,0:T(8,128)(2,1)S(1)} %copy-done.3, f32[128,1024]{1,0:T(8,128)S(1)} %get-tuple-element.56.refs_2_, ...), custom_call_target="tpu_custom_call", output_to_operand_aliasing={{2}: (6, {})} | custom-call | tf_op jit(solution)/shard_map/pallas_call | solution.py:435
  183.3 22.2 %fusion.71 = (f32[4096]{0:T(1024)S(1)}, f32[4096,1600]{0,1:T(8,128)}) fusion(bf16[4096,1024]{1,0:T(8,128)(2,1)} %bitcast.304, bf16[1600,1024]{1,0:T(8,128)(2,1)} %get-tuple-element.59), kind=kOutput, calls=%fused_computation.171 | convolution fusion | flops 13428322304 | bytes 37896192 | tf_op jit(solution)/shard_map/dot_general | solution.py:31
  205.5 12.0 %exponential_reduce_fusion = (f32[4096]{0:T(1024)S(1)}, f32[4096]{0:T(1024)S(1)}) fusion(f32[4096,1600]{0,1:T(8,128)} %get-tuple-element.136, f32[4096]{0:T(1024)S(1)} %get-tuple-element.135, s32[4096]{0:T(1024)S(1)} %bitcast.285), kind=kLoop, calls=%fused_computation.3 | loop fusion | flops 32759808 | bytes 26279936 | tf_op jit(solution)/shard_map/reduce_sum | solution.py:975
  218.2 21.3 %shard_map.394 = f32[3,32,128]{2,1,0:T(8,128)} custom-call(f32[3,32,128]{2,1,0:T(8,128)} %pad_maximum_fusion.2.given), custom_call_target="tpu_custom_call" | custom-call | tf_op jit(solution)/shard_map/pallas_call | solution.py:556
  242.3 23.1 %convolution_convert_fusion.1.refs_3_.refs_5_ = bf16[1600,1024]{1,0:T(8,128)(2,1)} fusion(bf16[4096,1024]{1,0:T(8,128)(2,1)} %bitcast.305, f32[4096,1600]{0,1:T(8,128)} %get-tuple-element.136, f32[4096]{0:T(1024)S(1)} %get-tuple-element.120, f32[4096]{0:T(1024)S(1)} %mul.152, s32[4096]{0:T(1024)S(1)} %bitcast.286), kind=kOutput, calls=%fused_computation.23 | convolution fusion | flops 13462732800 | bytes 37928960 | tf_op jit(solution)/shard_map/dot_general | solution.py:25
  265.4 26.2 %convolution_convert_fusion = bf16[4096,1024]{1,0:T(8,128)(2,1)} fusion(bf16[1600,1024]{1,0:T(8,128)(2,1)} %get-tuple-element.59, f32[4096,1600]{0,1:T(8,128)} %get-tuple-element.136, f32[4096]{0:T(1024)S(1)} %get-tuple-element.120, f32[4096]{0:T(1024)S(1)} %mul.152, s32[4096]{0:T(1024)S(1)} %bitcast.287), kind=kOutput, calls=%fused_computation.10 | convolution fusion | flops 13465288704 | bytes 37928960 | tf_op jit(solution)/shard_map/dot_general | solution.py:21
  291.7 72.3 %shard_map.395 = (bf16[4,128,1024]{2,1,0:T(8,128)(2,1)}, f32[128,1024]{1,0:T(8,128)}, f32[2,1024]{1,0:T(2,128)}, bf16[12800,128]{1,0:T(8,128)(2,1)}) custom-call(bf16[8,4,128,1024]{3,2,1,0:T(8,128)(2,1)} %bitcast.249, f32[128,1024]{1,0:T(8,128)} %copy-done.19, f32[1,1024]{1,0:T(1,128)} %bitcast.238, bf16[1600,1024]{1,0:T(8,128)(2,1)} %convolution_convert_fusion.1.refs_3_.refs_5_), custom_call_target="tpu_custom_call" | custom-call | tf_op jit(solution)/shard_map/pallas_call | solution.py:707
  364.0 4.3 convolution_convert_fusion.2
  378.7 22.0 %shard_map.396 = (bf16[4,128,1024]{2,1,0:T(8,128)(2,1)S(1)}, f32[128,1024]{1,0:T(8,128)S(1)}, f32[2,1024]{1,0:T(2,128)S(1)}, bf16[12800,128]{1,0:T(8,128)(2,1)}) custom-call(bf16[512,1024]{1,0:T(8,128)(2,1)S(1)} %copy-done.10, bf16[1024,1024]{1,0:T(8,128)(2,1)S(1)} %copy-done.2, f32[128,1024]{1,0:T(8,128)S(1)} %copy-done.22, ...), custom_call_target="tpu_custom_call", output_to_operand_aliasing={{3}: (6, {})} | custom-call | tf_op jit(solution)/shard_map/pallas_call | solution.py:503
  401.3 7.8 %multiply_reduce_fusion = (f32[4,512]{1,0:T(4,128)S(1)}, f32[4,512,1024]{2,1,0:T(8,128)}) fusion(f32[4,512,1024]{2,1,0:T(8,128)} %copy-done.36, f32[4,512]{1,0:T(4,128)S(1)} %copy-done.76, bf16[512,4,64]{0,2,1:T(8,128)(2,1)S(1)} %bitcast.270, bf16[1024,4,64]{0,2,1:T(8,128)(2,1)S(1)} %bitcast.281), kind=kOutput, calls=%fused_computation.5 | convolution fusion | flops 274724864 | bytes 17580032 | tf_op jit(solution)/shard_map/qhd,khd->hqk/dot_general | solution.py:67
  409.2 4.6 multiply_convert_fusion.1
  418.1 21.2 %shard_map.397 = (bf16[4,128,1024]{2,1,0:T(8,128)(2,1)S(1)}, f32[128,1024]{1,0:T(8,128)}, f32[2,1024]{1,0:T(2,128)S(1)}, bf16[12800,128]{1,0:T(8,128)(2,1)}) custom-call(bf16[512,256]{1,0:T(8,128)(2,1)S(1)} %copy.81.refs_0_, bf16[1024,256]{1,0:T(8,128)(2,1)S(1)} %copy-done.5, f32[128,1024]{1,0:T(8,128)S(1)} %copy-done.26, ...), custom_call_target="tpu_custom_call", output_to_operand_aliasing={{3}: (6, {})} | custom-call | tf_op jit(solution)/shard_map/pallas_call | solution.py:503
  447.8 3.0 fusion.21
  452.4 5.4 fusion.18
  460.8 2.6 convolution_convert_fusion.8
  466.3 4.7 convert_element_type.293
  471.1 2.9 fusion.23
  482.0 157.1 %shard_map.398 = (bf16[8,1024,256]{2,1,0:T(8,128)(2,1)S(1)}, f32[6,1024]{1,0:T(8,128)S(1)}) custom-call(bf16[8,1024,256]{2,1,0:T(8,128)(2,1)} %fusion.44.given, f32[6,1024]{1,0:T(8,128)S(1)} %pad_maximum_fusion.3.vecs), custom_call_target="tpu_custom_call" | custom-call | tf_op jit(solution)/shard_map/pallas_call | solution.py:828
  639.1 2.7 slice_convert_fusion
  647.2 14.2 %all-reduce.3.cloned.1.call-done = (bf16[1024,1024]{1,0:T(8,128)(2,1)}, bf16[1024,1024]{1,0:T(8,128)(2,1)}) async-done(((bf16[1024,1024]{1,0:T(8,128)(2,1)}, bf16[1024,1024]{1,0:T(8,128)(2,1)}), (bf16[1024,1024]{1,0:T(8,128)(2,1)}, bf16[1024,1024]{1,0:T(8,128)(2,1)})) %all-reduce.3.cloned.1.call-update) | async-done | bytes 4194320 | tf_op jit(solution)/shard_map/psum | solution.py:1019
  661.4 4.2 convert_element_type.291
  (277 shorter events, 80.0 us)
Async XLA Ops:
  8.0 10.2 %copy-start = (bf16[1024,1024]{1,0:T(8,128)(2,1)S(1)}, bf16[1024,1024]{1,0:T(8,128)(2,1)}, u32[]{:S(2)}) copy-start(bf16[1024,1024]{1,0:T(8,128)(2,1)} %param.25) | copy-start | bytes 6291460
  8.0 9.0 %copy-start.78 = (s32[1,512]{1,0:T(1,128)S(1)}, s32[1,512]{1,0:T(1,128)}, u32[]{:S(2)}) copy-start(s32[1,512]{1,0:T(1,128)} %param.26) | copy-start | bytes 6148
  8.1 8.4 %copy-start.54 = (bf16[1024,256]{1,0:T(8,128)(2,1)S(1)}, bf16[1024,256]{1,0:T(8,128)(2,1)}, u32[]{:S(2)}) copy-start(bf16[1024,256]{1,0:T(8,128)(2,1)} %param.33) | copy-start | bytes 1572868
  8.1 637.3 %reduce-scatter.3.cloned.1.call-start = ((), (), s32[]{:S(2)}) async-start(), calls=%async_computation.2 | async-start | bytes 1310720 | tf_op jit(solution)/shard_map/reduce_scatter | solution.py:1055
  9.7 8.4 %copy-start.84 = (f32[16]{0:T(128)}, f32[16]{0:T(128)S(1)}, u32[]{:S(2)}) copy-start(f32[16]{0:T(128)S(1)} %exponential_reduce_fusion.1) | copy-start | bytes 196
  24.8 37.3 %copy-start.68 = (bf16[4,64,512]{2,1,0:T(8,128)(2,1)}, bf16[4,64,512]{2,1,0:T(8,128)(2,1)S(1)}, u32[]{:S(2)}) copy-start(bf16[4,64,512]{2,1,0:T(8,128)(2,1)S(1)} %fusion.40) | copy-start | bytes 786436
  24.8 36.8 %copy-start.5 = (bf16[1024,256]{1,0:T(8,128)(2,1)S(1)}, bf16[1024,256]{1,0:T(8,128)(2,1)}, u32[]{:S(2)}) copy-start(bf16[1024,256]{1,0:T(8,128)(2,1)} %refs_1_.9) | copy-start | bytes 1572868
  26.1 36.0 %copy-start.56 = (bf16[1024,256]{0,1:T(8,128)(2,1)S(1)}, bf16[1024,256]{0,1:T(8,128)(2,1)}, u32[]{:S(2)}) copy-start(bf16[1024,256]{0,1:T(8,128)(2,1)} %convolution_convert_fusion.12) | copy-start | bytes 1572868
  26.1 36.0 %copy-start.58 = (pred[512,1024]{1,0:T(8,128)(4,1)S(1)}, pred[512,1024]{1,0:T(8,128)(4,1)}, u32[]{:S(2)}) copy-start(pred[512,1024]{1,0:T(8,128)(4,1)} %broadcast_compare_fusion) | copy-start | bytes 1572868
  71.6 31.9 %copy-start.1 = (bf16[1024,1024]{1,0:T(8,128)(2,1)S(1)}, bf16[1024,1024]{1,0:T(8,128)(2,1)}, u32[]{:S(2)}) copy-start(bf16[1024,1024]{1,0:T(8,128)(2,1)} %refs_1_.8) | copy-start | bytes 6291460
  110.4 72.9 %copy-start.8 = (bf16[512,1024]{1,0:T(8,128)(2,1)}, bf16[512,1024]{1,0:T(8,128)(2,1)S(1)}, u32[]{:S(2)}) copy-start(bf16[512,1024]{1,0:T(8,128)(2,1)S(1)} %get-tuple-element.91.refs_0_) | copy-start | bytes 3145732
  183.3 22.2 %copy-start.19 = (f32[128,1024]{1,0:T(8,128)}, f32[128,1024]{1,0:T(8,128)S(1)}, u32[]{:S(2)}) copy-start(f32[128,1024]{1,0:T(8,128)S(1)} %get-tuple-element.61.refs_1_) | copy-start | bytes 1572868
  205.5 35.3 %copy-start.79 = (f32[16,4]{0,1:T(4,128)S(1)}, f32[16,4]{0,1:T(4,128)}, u32[]{:S(2)}) copy-start(f32[16,4]{0,1:T(4,128)} %param.29) | copy-start | bytes 772
  205.5 36.2 %copy-start.83 = (s32[64]{0:T(128)S(1)}, s32[64]{0:T(128)}, u32[]{:S(2)}) copy-start(s32[64]{0:T(128)} %param.30) | copy-start | bytes 772
  378.7 22.6 %copy-start.75 = (bf16[1024,256]{0,1:T(8,128)(2,1)S(1)}, bf16[1024,256]{0,1:T(8,128)(2,1)}, u32[]{:S(2)}) copy-start(bf16[1024,256]{0,1:T(8,128)(2,1)} %convolution_convert_fusion.13) | copy-start | bytes 1572868
  378.7 22.6 %copy-start.76 = (f32[4,512]{1,0:T(4,128)S(1)}, f32[4,512]{1,0:T(4,128)}, u32[]{:S(2)}) copy-start(f32[4,512]{1,0:T(4,128)} %log_add_fusion.1) | copy-start | bytes 24580
  400.7 8.4 %copy-start.13 = (bf16[4,128,1024]{2,1,0:T(8,128)(2,1)}, bf16[4,128,1024]{2,1,0:T(8,128)(2,1)S(1)}, u32[]{:S(2)}) copy-start(bf16[4,128,1024]{2,1,0:T(8,128)(2,1)S(1)} %get-tuple-element.68) | copy-start | bytes 3145732
  400.8 8.4 %copy-start.25 = (f32[128,1024]{1,0:T(8,128)}, f32[128,1024]{1,0:T(8,128)S(1)}, u32[]{:S(2)}) copy-start(f32[128,1024]{1,0:T(8,128)S(1)} %get-tuple-element.69.refs_2_) | copy-start | bytes 1572868
  401.3 7.9 %slice-start.1 = ((s8[8388608]{0:T(1024)(128)(4,1)}), s8[4194304]{0:T(1024)(128)(4,1)S(1)}, s32[]{:S(2)}) async-start(s8[8388608]{0:T(1024)(128)(4,1)} %bitcast.247), calls=%async_computation.6 | async-start | bytes 8388608
  418.1 21.2 %copy-start.16 = (bf16[256,1024]{1,0:T(8,128)(2,1)S(1)}, bf16[256,1024]{1,0:T(8,128)(2,1)}, u32[]{:S(2)}) copy-start(bf16[256,1024]{1,0:T(8,128)(2,1)} %refs_1_.5) | copy-start | bytes 1572868
  418.1 21.7 %copy-start.38 = (f32[4,512,512]{1,2,0:T(8,128)S(1)}, f32[4,512,512]{1,2,0:T(8,128)}, u32[]{:S(2)}) copy-start(f32[4,512,512]{1,2,0:T(8,128)} %copy-done.37) | copy-start | bytes 12582916
  418.1 21.7 %copy-start.77 = (f32[4,512]{1,0:T(4,128)S(1)}, f32[4,512]{1,0:T(4,128)}, u32[]{:S(2)}) copy-start(f32[4,512]{1,0:T(4,128)} %log_add_fusion.2) | copy-start | bytes 24580
  446.9 214.5 %all-reduce.3.cloned.1.call-start = ((), (), s32[]{:S(2)}) async-start(), calls=%async_computation.4 | async-start | bytes 8388608 | tf_op jit(solution)/shard_map/psum | solution.py:1019
  447.4 220.6 %reduce-scatter.5.cloned.1.call-start = ((), (), s32[]{:S(2)}) async-start(), calls=%async_computation.3 | async-start | bytes 2621440 | tf_op jit(solution)/shard_map/reduce_scatter | solution.py:1058
  (70 other events, 226.4 us)
Sparse Core Ops, SparseCore 0:
  447.0 24.4 reduce-scatter.2
  474.1 31.4 reduce-scatter.4
Sparse Core Ops, SparseCore 1:
  451.1 210.2 all-reduce.2

commit v4 on v3

v4 whole, which is shorter than its diff:
```python
import functools
import typing

import jax
import jax.numpy as jnp
from jax import lax
from jax.experimental import pallas as pl
from jax.experimental.pallas import tpu as pltpu
from jax.sharding import PartitionSpec as P

HEAD_DIM = 64
SEG_ROW = 8
MEM = 128


masked_score = -1e30
norm_eps = 1e-05
highest = lax.Precision.HIGHEST


def product(left_side, right_side):
    return jnp.dot(left_side, right_side, preferred_element_type=jnp.float32)


def product_tn(left_side, right_side):
    return lax.dot_general(
        left_side, right_side, (((0,), (0,)), ((), ())), preferred_element_type=jnp.float32
    )


def product_nt(left_side, right_side):
    return lax.dot_general(
        left_side, right_side, (((1,), (1,)), ((), ())), preferred_element_type=jnp.float32
    )


def gelu_exact(inputs):
    return jax.nn.gelu(inputs, approximate=False)


def split_heads(matrix):
    return matrix.reshape(matrix.shape[0], matrix.shape[1] // HEAD_DIM, HEAD_DIM)


def attention_scores(queries, keys, allowed):
    scores = jnp.einsum(
        "qhd,khd->hqk", split_heads(queries), split_heads(keys), preferred_element_type=jnp.float32
    ) * HEAD_DIM ** (-0.5)
    return jnp.where(allowed[None], scores, masked_score)


def attend_forward(queries, keys, values, allowed):
    scores = attention_scores(queries, keys, allowed)
    largest = jnp.max(scores, axis=-1, keepdims=True)
    weights = jnp.exp(scores - largest)
    total = jnp.sum(weights, axis=-1, keepdims=True)
    probabilities = (weights / total).astype(jnp.bfloat16)
    mixed_out = jnp.einsum(
        "hqk,khd->qhd", probabilities, split_heads(values), preferred_element_type=jnp.float32
    )
    return (mixed_out.reshape(queries.shape[0], queries.shape[1]), largest + jnp.log(total))


def run_rows(queries, keys, values, masks):
    mixed_out, log_total = attend_forward(queries, keys, values, masks[0])
    totals = [log_total]
    return (mixed_out.astype(jnp.bfloat16), totals)


MESH = pl.DeviceIdType.MESH
VMEM = pl.BlockSpec(memory_space=pltpu.VMEM)
ANY = pl.BlockSpec(memory_space=pl.ANY)
DMA = pltpu.SemaphoreType.DMA
QUARTERS = 4


def flip(index, mask):
    for bit in range(mask.bit_length()):
        if mask >> bit & 1:
            step = 1 << bit
            index = index + step * (1 - 2 * lax.rem(lax.div(index, step), 2))
    return index


def greet(peers):
    barrier = pltpu.get_barrier_semaphore()
    for peer in peers:
        pl.semaphore_signal(barrier, inc=1, device_id=peer, device_id_type=MESH)
    pl.semaphore_wait(barrier, len(peers))


def remote(source, target, send_sem, recv_sem, peer):
    copy = pltpu.make_async_remote_copy(
        src_ref=source,
        dst_ref=target,
        send_sem=send_sem,
        recv_sem=recv_sem,
        device_id=peer,
        device_id_type=MESH,
    )
    copy.start()
    return copy


def sum_quarter_steps(
    place, block_of, near, far, sib_send, sib_recv, far_send, far_recv, sems, outcome, sent
):
    copies = []
    for slot, mask in enumerate((3, 1)):
        sib_send[slot] = block_of(flip(place, mask)).astype(jnp.bfloat16)
        copies.append(
            remote(
                sib_send.at[slot], sib_recv.at[slot], sems.at[0, slot], sems.at[1, slot], near
            )
        )
    distant = block_of(flip(place, 2))
    copies[0].wait_recv()
    far_send[...] = (distant + sib_recv[0].astype(jnp.float32)).astype(jnp.bfloat16)
    copies.append(remote(far_send, far_recv, sems.at[0, 2], sems.at[1, 2], far))
    sent += copies
    own = block_of(place)
    copies[1].wait_recv()
    yield
    copies[2].wait_recv()
    outcome.append(own + sib_recv[1].astype(jnp.float32) + far_recv[...].astype(jnp.float32))


def share_quarter_steps(place, quarters, near, far, sems, sent):
    here = quarters.at[place]
    to_far = remote(here, here, sems.at[0, 3], sems.at[1, 3], far)
    to_near = remote(here, here, sems.at[0, 4], sems.at[1, 4], near)
    yield
    to_far.wait_recv()
    there = quarters.at[flip(place, 2)]
    passed = remote(there, there, sems.at[0, 5], sems.at[1, 5], near)
    to_near.wait_recv()
    passed.wait_recv()
    sent += [to_far, to_near, passed]


def run(steps, between=None):
    for _ in steps:
        if between is not None:
            between()


def sum_quarter(place, block_of, near, far, *buffers):
    outcome, sent = [], []
    run(sum_quarter_steps(place, block_of, near, far, *buffers, outcome, sent))
    return outcome[0], sent


def share_quarter(place, quarters, near, far, sems):
    sent = []
    run(share_quarter_steps(place, quarters, near, far, sems, sent))
    return sent


def table_copies(masks, back, source, target, sems):
    block, place = lax.axis_index("dp"), lax.axis_index("mp")
    total = lax.axis_size("dp")
    part, width = (source if back else target).shape[0], (target if back else source).shape[1]
    copies = []
    for slot, mask in enumerate(masks):
        other = flip(block, mask)
        here = pl.ds(pl.multiple_of((block if back else other) * part, part), part)
        there = pl.ds(pl.multiple_of((other if back else block) * width, width), width)
        if back:
            start, end = source.at[:, there], target.at[here, :]
        else:
            start, end = source.at[here, :], target.at[:, there]
        if mask:
            copies.append(remote(start, end, sems.at[0, slot], sems.at[1, slot], (other, place)))
        else:
            copy = pltpu.make_async_copy(start, end, sems.at[0, slot])
            copy.start()
            copies.append(copy)
    return copies


def finish(copies):
    for copy in copies:
        copy.wait()


def split_refs(refs, *counts):
    groups, start = [], 0
    for count in counts:
        groups.append(list(refs[start : start + count]))
        start += count
    return groups


def norm_rows(rows, gain, shift):
    center = rows - jnp.mean(rows, axis=-1, keepdims=True)
    spread = jnp.mean(center * center, axis=-1, keepdims=True)
    return center * lax.rsqrt(spread + norm_eps) * gain + shift


def norm_rows_back(rows, gain, grad):
    center = rows - jnp.mean(rows, axis=-1, keepdims=True)
    scale = lax.rsqrt(jnp.mean(center * center, axis=-1, keepdims=True) + norm_eps)
    normed = center * scale
    inner = grad * gain
    grad_rows = scale * (
        inner
        - jnp.mean(inner, axis=-1, keepdims=True)
        - normed * jnp.mean(inner * normed, axis=-1, keepdims=True)
    )
    return (
        grad_rows,
        jnp.sum(grad * normed, axis=0, keepdims=True),
        jnp.sum(grad, axis=0, keepdims=True),
    )


def rows_of(ref, height, index):
    return ref[pl.ds(pl.multiple_of(index * height, height), height), :]


def exchange_scratch(height, width):
    return [
        pltpu.VMEM((2, height, width), jnp.bfloat16),
        pltpu.VMEM((2, height, width), jnp.bfloat16),
        pltpu.VMEM((height, width), jnp.bfloat16),
        pltpu.VMEM((height, width), jnp.bfloat16),
        DMA((2, 6)),
    ]


def mix_norm_kernel(total, with_ids, masks, chained, *refs):
    (left, weight, kept, gain, shift), ids, table, (quarters, normed, rows), ids_all, wide, refs = (
        split_refs(
            refs, 5, with_ids, (1 + chained) * bool(masks), 3, with_ids, bool(masks), len(refs)
        )
    )
    sib_send, sib_recv, far_send, far_recv, sems = refs[:5]
    refs = refs[5:]
    block, place = lax.axis_index("dp"), lax.axis_index("mp")
    near, far = (block, flip(place, 1)), (block, flip(place, 2))
    height = kept.shape[0]
    others = range(1, total) if with_ids else [mask for mask in masks if mask]
    greet([near, far] + [(flip(block, mask), place) for mask in others])
    copies = []
    if with_ids:
        ids_sems, ids_local = refs[:2]
        refs = refs[2:]
        own = pltpu.make_async_copy(ids[0], ids_all[0].at[block], ids_local)
        own.start()
        copies.append(own)
        for mask in range(1, total):
            copies.append(
                remote(
                    ids[0], ids_all[0].at[block], ids_sems.at[0, mask], ids_sems.at[1, mask],
                    (flip(block, mask), place),
                )
            )

    def block_of(index):
        return jnp.dot(
            rows_of(left, height, index), weight[...], preferred_element_type=jnp.float32
        )

    if masks:
        copies += table_copies(masks, False, table[0], wide[0], refs[0])
    branch, sent = sum_quarter(
        place, block_of, near, far, sib_send, sib_recv, far_send, far_recv, sems
    )
    outcome = kept[...].astype(jnp.float32) + branch
    rows[...] = outcome
    outcome = norm_rows(outcome, gain[...], shift[...])
    normed[...] = outcome
    quarters[place] = outcome.astype(jnp.bfloat16)
    sent += share_quarter(place, quarters, near, far, sems)
    finish(copies)
    for copy in sent:
        copy.wait_send()


def mix_norm(left, weight, kept, gain, shift, number, ids=None, table=None, wide=None, masks=()):
    height, width = kept.shape
    total = lax.axis_size("dp")
    quarter = jax.ShapeDtypeStruct((height, width), jnp.float32)
    out_shape = [
        jax.ShapeDtypeStruct((QUARTERS, height, width), jnp.bfloat16), quarter, quarter
    ]
    out_specs = [VMEM] * 3
    given = [left, weight, kept, gain.reshape(1, -1), shift.reshape(1, -1)]
    in_specs = [VMEM] * 5
    scratch = exchange_scratch(height, width)
    aliases = {}
    if ids is not None:
        given.append(ids)
        in_specs.append(VMEM)
        out_shape.append(jax.ShapeDtypeStruct((total,) + ids.shape, ids.dtype))
        out_specs.append(VMEM)
        scratch += [DMA((2, total)), DMA]
    if masks:
        given.append(table)
        in_specs.append(ANY)
        if wide is not None:
            aliases = {len(given): len(out_shape)}
            given.append(wide)
            in_specs.append(ANY)
        out_shape.append(
            jax.ShapeDtypeStruct((table.shape[0] // total, table.shape[1] * total), table.dtype)
        )
        out_specs.append(ANY)
        scratch.append(DMA((2, len(masks))))
    outcome = pl.pallas_call(
        functools.partial(
            mix_norm_kernel, total, int(ids is not None), tuple(masks), int(wide is not None)
        ),
        out_shape=out_shape,
        in_specs=in_specs,
        out_specs=out_specs,
        scratch_shapes=scratch,
        input_output_aliases=aliases,
        compiler_params=pltpu.CompilerParams(
            collective_id=number, has_side_effects=True, vmem_limit_bytes=48 * 2**20
        ),
    )(*given)
    return (outcome[0].reshape(-1, width),) + tuple(outcome[1:])


def chunk_of(rows):
    return max(size for size in range(16, min(rows, 400) + 1, 16) if rows % size == 0)


def feed_norm_kernel(total, early, *refs):
    (left, weight, kept, gain, shift, targets), words, (states, rows, logits, totals), wide, refs = (
        split_refs(refs, 6, 1 + 2 * bool(early), 4, bool(early), len(refs))
    )
    last = words[-1]
    low, sib_send, sib_recv, far_send, far_recv, sems, hops, own_sem = refs[:8]
    (held, staged, sends, recvs, held_sem, staged_sems, stage_sems), refs = refs[8:15], refs[15:]
    block, place = lax.axis_index("dp"), lax.axis_index("mp")
    near, far = (block, flip(place, 1)), (block, flip(place, 2))
    beside = (flip(block, 1), place)
    height = kept.shape[0]
    bits = (total - 1).bit_length()
    others = set(range(1, total) if early else range(2, total, 2))
    others |= {1 << bit for bit in range(bits)}
    greet([near, far] + [(flip(block, mask), place) for mask in sorted(others)])

    def block_of(index):
        return jnp.dot(
            rows_of(left, height, index), weight[...], preferred_element_type=jnp.float32
        )

    moved = []
    if early:
        moved = table_copies(early, False, words[0], wide[0], refs[0])
    branch, sent = sum_quarter(
        place, block_of, near, far, sib_send, sib_recv, far_send, far_recv, sems
    )
    outcome = kept[...] + branch
    rows[...] = outcome
    low[...] = norm_rows(outcome, gain[...], shift[...]).astype(jnp.bfloat16)
    own = pltpu.make_async_copy(low, states.at[block, place], own_sem)
    own.start()
    across = flip(place, 2)

    def hop(kind, mask, source, peer, row, column):
        copy = remote(
            source, states.at[row, column], hops.at[0, kind, mask], hops.at[1, kind, mask], peer
        )
        sent.append(copy)
        return copy

    first = {}
    for mask in range(2, total, 2):
        first[mask] = hop(0, mask, low, (flip(block, mask), place), block, place)
    over, ends = {}, {}

    def pass_on(mask):
        over[mask].wait_recv()
        row = flip(block, mask)
        ends[mask, 1] = hop(3, mask, states.at[row, across], near, row, across)

    def arrive(mask):
        row = flip(block, mask)
        if mask:
            first[mask].wait_recv()
        source = states.at[row, place] if mask else low
        if mask % 2 == 0:
            first[mask + 1] = hop(0, mask + 1, source, beside, row, place)
        over[mask] = hop(1, mask, source, far, row, place)
        ends[mask, 0] = hop(2, mask, source, near, row, place)

    part, width = held.shape
    chunk = chunk_of(part)
    span = QUARTERS * height
    writes = {}

    def make(mask):
        row, slot = flip(block, mask), mask % 2
        for side in (0, 1):
            ends[mask, side].wait_recv()
        if mask >= 2:
            writes[mask - 2].wait()
        block_states = states[row].reshape(span, width)
        target = targets[row]

        def body(turn, carry):
            top, amount, picked = carry
            start = pl.multiple_of(turn * chunk, chunk)
            scores = product_nt(held[pl.ds(start, chunk), :], block_states)
            staged[slot, pl.ds(start, chunk), :] = scores
            ahead = jnp.maximum(top, jnp.max(scores, axis=0, keepdims=True))
            ids = start + lax.broadcasted_iota(jnp.int32, (chunk, 1), 0)
            return (
                ahead,
                amount * jnp.exp(top - ahead)
                + jnp.sum(jnp.exp(scores - ahead), axis=0, keepdims=True),
                picked
                + jnp.sum(jnp.where(ids == target, scores, 0.0), axis=0, keepdims=True),
            )

        scores = product_nt(held[0:chunk, :], block_states)
        staged[slot, 0:chunk, :] = scores
        top = jnp.max(scores, axis=0, keepdims=True)
        ids = lax.broadcasted_iota(jnp.int32, (chunk, 1), 0)
        carry = (
            top,
            jnp.sum(jnp.exp(scores - top), axis=0, keepdims=True),
            jnp.sum(jnp.where(ids == target, scores, 0.0), axis=0, keepdims=True),
        )
        if part > chunk:
            carry = lax.fori_loop(1, part // chunk, body, carry)
        for index in range(3):
            sends[0, index, pl.ds(row, 1), :] = carry[index]
        writes[mask] = pltpu.make_async_copy(
            staged.at[slot], logits.at[row], staged_sems.at[slot]
        )
        writes[mask].start()

    lag = 3
    for step in range(total + lag):
        if step < total:
            arrive(step)
        if 2 <= step < total + 2:
            pass_on(step - 2)
        if step == lag:
            finish(moved)
            load = pltpu.make_async_copy(wide[0] if early else words[0], held, held_sem)
            load.start()
            own.wait()
            load.wait()
            if early:
                spot = pl.ds(pl.multiple_of(flip(block, total - 1) * last.shape[1], 128), 128)
                load = pltpu.make_async_copy(last, held.at[:, spot], held_sem)
                load.start()
                load.wait()
        if step >= lag:
            make(step - lag)
    lead = max(total - 2, 0)
    for mask in range(lead, total):
        writes[mask].wait()

    peers = [(near, lax.rem(place, 2)), (far, lax.div(place, 2))]
    for bit in range(bits):
        step = 1 << bit
        peers.append(((flip(block, step), place), lax.rem(lax.div(block, step), 2)))
    for stage, (peer, side) in enumerate(peers):
        copy = remote(
            sends.at[stage], recvs.at[stage], stage_sems.at[0, stage], stage_sems.at[1, stage],
            peer,
        )
        copy.wait_recv()
        sent.append(copy)
        mine = [sends[stage, index] for index in range(3)]
        theirs = [recvs[stage, index] for index in range(3)]
        leading = side == 0
        soon = [jnp.where(leading, one, other) for one, other in zip(mine, theirs)]
        late_ones = [jnp.where(leading, other, one) for one, other in zip(mine, theirs)]
        top = jnp.maximum(soon[0], late_ones[0])
        values = [
            top,
            soon[1] * jnp.exp(soon[0] - top) + late_ones[1] * jnp.exp(late_ones[0] - top),
            soon[2] + late_ones[2],
        ]
        for index in range(3):
            if stage + 1 < len(peers):
                sends[stage + 1, index] = values[index]
            else:
                totals[index] = values[index]
    for copy in sent:
        copy.wait_send()


def feed_norm(
    left, weight, kept, gain, shift, targets, number, table, wide=None, last=None, early=()
):
    height, width = kept.shape
    total = lax.axis_size("dp")
    stages = 2 + (total - 1).bit_length()
    span = QUARTERS * height
    words = wide if early else table
    part = words.shape[0]
    given = [left, weight, kept, gain.reshape(1, -1), shift.reshape(1, -1), targets, table]
    in_specs = [VMEM] * 6 + [ANY]
    out_shape = [
        jax.ShapeDtypeStruct((total, QUARTERS, height, width), jnp.bfloat16),
        jax.ShapeDtypeStruct((height, width), jnp.float32),
        jax.ShapeDtypeStruct((total, part, span), jnp.float32),
        jax.ShapeDtypeStruct((3, total, span), jnp.float32),
    ]
    out_specs = [VMEM, VMEM, ANY, VMEM]
    scratch = [pltpu.VMEM((height, width), jnp.bfloat16)] + exchange_scratch(height, width)
    scratch += [
        DMA((2, 4, total)),
        DMA,
        pltpu.VMEM((part, width), jnp.bfloat16),
        pltpu.VMEM((2, part, span), jnp.float32),
        pltpu.VMEM((stages, 3, total, span), jnp.float32),
        pltpu.VMEM((stages, 3, total, span), jnp.float32),
        DMA,
        DMA((2,)),
        DMA((2, stages)),
    ]
    aliases = {}
    if early:
        given += [wide, last]
        in_specs += [ANY] * 2
        out_shape.append(jax.ShapeDtypeStruct(wide.shape, wide.dtype))
        out_specs.append(ANY)
        aliases = {7: 4}
        scratch.append(DMA((2, len(early))))
    outcome = pl.pallas_call(
        functools.partial(feed_norm_kernel, total, tuple(early)),
        out_shape=out_shape,
        in_specs=in_specs,
        out_specs=out_specs,
        scratch_shapes=scratch,
        input_output_aliases=aliases,
        compiler_params=pltpu.CompilerParams(
            collective_id=number, has_side_effects=True, vmem_limit_bytes=62 * 2**20
        ),
    )(*given)
    return tuple(outcome)


def head_back_kernel(total, masks, fused, *refs):
    (parts, rows, gain), more, (quarters, grad_rows, grad_vecs), table, narrow, refs = split_refs(
        refs, 3, 5 * fused, 3, fused, bool(masks), len(refs)
    )
    mine, sib_recv, far_recv, beside_recv, across_recv, end_recv, sems = refs[:7]
    sib_sems, far_sems, beside_sems, end_sems, load_sems = refs[7:12]
    refs = refs[12:]
    block, place = lax.axis_index("dp"), lax.axis_index("mp")
    near, far = (block, flip(place, 1)), (block, flip(place, 2))
    beside = (flip(block, 1), place)
    height = rows.shape[0]
    others = range(1, total) if masks else [1] + list(range(2, total, 2))
    greet([near, far] + [(flip(block, mask), place) for mask in others])
    moved = []
    aside = [mask + 1 for mask in range(0, total // 2, 2)]
    order = []
    for late, soon in zip(range(total - 1, total // 2, -2), aside[::-1]):
        order += [late, soon]
    order += [mask for mask in range(total - 1, -1, -1) if mask % 2 == 0]
    sent, loads, sib, across, over, ends = [], {}, {}, {}, {}, {}

    def to_near(mask, slot, source):
        sib[mask, slot] = remote(
            source,
            sib_recv.at[mask, slot],
            sib_sems.at[0, mask, slot],
            sib_sems.at[1, mask, slot],
            near,
        )
        sent.append(sib[mask, slot])

    if fused:
        words, states, log_totals, grad_logp, targets = more
        if masks:
            move_sems, refs = refs[0], refs[1:]
        logits, held, grads, acc, held_sems = refs
        part = words.shape[0]
        chunk = chunk_of(part)
        span = grads.shape[2]

        def load(step):
            slot = step % 2
            loads[step] = pltpu.make_async_copy(
                parts.at[flip(block, order[step])], logits.at[slot], load_sems.at[slot, 0]
            )
            loads[step].start()

        def load_states(step):
            slot = step % 2
            loads[step, None] = pltpu.make_async_copy(
                states.at[flip(block, order[step])], held.at[slot], held_sems.at[slot]
            )
            loads[step, None].start()

        load(0)
    else:
        for mask in order:
            row = flip(block, mask)
            for turn in range(QUARTERS):
                if turn % 2 == 0:
                    loads[mask, turn] = pltpu.make_async_copy(
                        parts.at[row, flip(place, turn)],
                        mine.at[mask, 1 - turn // 2],
                        load_sems.at[mask, turn // 2],
                    )
                    loads[mask, turn].start()
                else:
                    to_near(mask, (3 - turn) // 2, parts.at[row, flip(place, turn)])

    def make(step):
        mask = order[step]
        if not fused:
            for turn in (0, 2):
                loads[mask, turn].wait()
            return
        if step + 1 < len(order):
            load(step + 1)
        elif masks or fused:
            load_states(0)
        loads[step].wait()
        row, slot = flip(block, mask), step % 2
        target, log_total, scale = targets[row], log_totals[row], grad_logp[row]

        def body(turn, carry):
            start = pl.multiple_of(turn * chunk, chunk)
            ids = start + lax.broadcasted_iota(jnp.int32, (chunk, 1), 0)
            hot = (ids == target).astype(jnp.float32)
            chances = jnp.exp(logits[slot, pl.ds(start, chunk), :] - log_total)
            grads[step, pl.ds(start, chunk), :] = (scale * (hot - chances)).astype(jnp.bfloat16)
            return carry

        lax.fori_loop(0, part // chunk, body, 0)
        mine[mask] = (
            product_tn(grads[step], words[...]).astype(jnp.bfloat16).reshape(mine.shape[1:])
        )
        for slot, turn in enumerate((3, 1)):
            to_near(mask, slot, mine.at[mask, flip(place, turn)])

    def make_rows(step):
        if step + 1 < len(order):
            load_states(step + 1)
        loads[step, None].wait()
        block_states = held[step % 2].reshape(span, rows.shape[1])

        def body(turn, carry):
            here = pl.ds(pl.multiple_of(turn * chunk, chunk), chunk)
            value = dot_nn(grads[step, here, :], block_states)
            if step:
                value = value + acc[here, :]
            if step + 1 < len(order):
                acc[here, :] = value
            else:
                table[0][here, :] = value.astype(jnp.bfloat16)
            return carry

        lax.fori_loop(0, part // chunk, body, 0)

    own = (flip(place, 2), place) if fused else (0, 1)

    def join(mask, slot, *others):
        value = mine[mask, own[slot]].astype(jnp.float32)
        for other in others:
            value = value + other.astype(jnp.float32)
        return value

    def send_beside(mask, slot, target, sem_row):
        index = mask // 2
        copy = remote(
            mine.at[mask, own[slot]],
            target.at[index],
            beside_sems.at[0, sem_row, index],
            beside_sems.at[1, sem_row, index],
            beside,
        )
        sent.append(copy)
        return copy

    def to_far(mask):
        for slot in (0, 1):
            sib[mask, slot].wait_recv()
        terms = [sib_recv[mask, 0]]
        if mask + 1 in aside:
            across[mask + 1].wait_recv()
            terms.append(across_recv[mask // 2])
        mine[mask, own[0]] = join(mask, 0, *terms).astype(jnp.bfloat16)
        if mask in aside:
            mine[mask, own[1]] = join(mask, 1, sib_recv[mask, 1]).astype(jnp.bfloat16)
            across[mask] = send_beside(mask, 0, across_recv, 0)
            over[mask] = send_beside(mask, 1, beside_recv, 1)
            return
        across[mask] = remote(
            mine.at[mask, own[0]], far_recv.at[mask], far_sems.at[0, mask], far_sems.at[1, mask], far
        )
        sent.append(across[mask])

    def to_beside(mask):
        if mask in aside:
            return
        across[mask].wait_recv()
        mine[mask, own[1]] = join(mask, 1, sib_recv[mask, 1], far_recv[mask]).astype(jnp.bfloat16)
        over[mask] = send_beside(mask, 1, beside_recv, 1)

    def to_end(mask):
        across[mask].wait_recv()
        over[mask + 1].wait_recv()
        value = join(mask, 1, sib_recv[mask, 1], far_recv[mask], beside_recv[mask // 2])
        if mask == 0:
            return value
        mine[mask, own[1]] = value.astype(jnp.bfloat16)
        ends[mask] = remote(
            mine.at[mask, own[1]],
            end_recv.at[mask // 2],
            end_sems.at[0, mask // 2],
            end_sems.at[1, mask // 2],
            (flip(block, mask), place),
        )
        sent.append(ends[mask])
        return None

    outcome = None
    count = len(order)
    make(0)
    rows_made = 0
    for step in range(count + 2):
        if step + 1 < count:
            make(step + 1)
        if step < count:
            to_far(order[step])
        if step >= 2:
            mask = order[step - 2]
            if mask % 2:
                to_beside(mask)
            else:
                outcome = to_end(mask)
        if fused and step + 2 >= count:
            for _ in range(2):
                make_rows(rows_made)
                rows_made += 1
    if fused:
        while rows_made < count:
            make_rows(rows_made)
            rows_made += 1
        if masks:
            moved = table_copies(masks, True, table[0], narrow[0], move_sems)
    for mask in range(total - 2, 0, -2):
        ends[mask].wait_recv()
        outcome = outcome + end_recv[mask // 2].astype(jnp.float32)
    outcome, grad_gain, grad_shift = norm_rows_back(rows[...], gain[...], outcome)
    grad_rows[...] = outcome
    grad_vecs[0:1] = grad_gain
    grad_vecs[1:2] = grad_shift
    quarters[place] = outcome.astype(jnp.bfloat16)
    sent += share_quarter(place, quarters, near, far, sems)
    for copy in sent:
        copy.wait_send()
    finish(moved)


def head_back(values, rows, gain, number, masks=()):
    height, width = rows.shape
    total = lax.axis_size("dp")
    half = total // 2
    block = (height, width)
    fused = len(values) > 1
    out_shape = [
        jax.ShapeDtypeStruct((QUARTERS,) + block, jnp.bfloat16),
        jax.ShapeDtypeStruct(block, jnp.float32),
        jax.ShapeDtypeStruct((2, width), jnp.float32),
    ]
    out_specs = [VMEM] * 3
    scratch = [
        pltpu.VMEM((total, QUARTERS if fused else 2) + block, jnp.bfloat16),
        pltpu.VMEM((total, 2) + block, jnp.bfloat16),
        pltpu.VMEM((total,) + block, jnp.bfloat16),
        pltpu.VMEM((half,) + block, jnp.bfloat16),
        pltpu.VMEM((half,) + block, jnp.bfloat16),
        pltpu.VMEM((half,) + block, jnp.bfloat16),
        DMA((2, 6)),
        DMA((2, total, 2)),
        DMA((2, total)),
        DMA((2, 2, half)),
        DMA((2, half)),
        DMA((total, 2)),
    ]
    given = [values[0], rows, gain.reshape(1, -1)]
    in_specs = [ANY, VMEM, VMEM]
    if fused:
        words, states = values[1:3]
        part, span = values[0].shape[1:]
        given += list(values[1:])
        in_specs += [VMEM, ANY, VMEM, VMEM, VMEM]
        out_shape.append(jax.ShapeDtypeStruct(words.shape, jnp.bfloat16))
        out_specs.append(VMEM)
        if masks:
            narrow = (part * total, width // total)
            out_shape.append(jax.ShapeDtypeStruct(narrow, jnp.bfloat16))
            out_specs.append(ANY)
            scratch.append(DMA((2, len(masks))))
        scratch += [
            pltpu.VMEM((2, part, span), jnp.float32),
            pltpu.VMEM((2, QUARTERS) + block, jnp.bfloat16),
            pltpu.VMEM((total, part, span), jnp.bfloat16),
            pltpu.VMEM((part, width), jnp.float32),
            DMA((2,)),
        ]
    outcome = pl.pallas_call(
        functools.partial(head_back_kernel, total, tuple(masks), int(fused)),
        out_shape=out_shape,
        in_specs=in_specs,
        out_specs=out_specs,
        scratch_shapes=scratch,
        compiler_params=pltpu.CompilerParams(
            collective_id=number, has_side_effects=True, vmem_limit_bytes=63 * 2**20
        ),
    )(*given)
    return (outcome[0].reshape(-1, width),) + tuple(outcome[1:])


def dot_nn(left, right):
    return jnp.dot(left, right, preferred_element_type=jnp.float32)


def attend_back(queries, keys, values, grads, totals, allowed_at, acc_keys, acc_values, grad_queries,
                grad_keys, grad_values):
    span, width = keys.shape
    rows = queries.shape[0]
    step = min(256, rows)
    pair = 2 * HEAD_DIM
    lanes = lax.broadcasted_iota(jnp.int32, (1, pair), 1)
    sides = [(lanes // HEAD_DIM == side).astype(jnp.bfloat16) for side in range(2)]
    acc_keys[0:span] = jnp.zeros((span, width), jnp.float32)
    acc_values[0:span] = jnp.zeros((span, width), jnp.float32)

    def body(turn, carry):
        here = pl.ds(pl.multiple_of(turn * step, step), step)
        allowed = allowed_at(here)
        for start in range(0, width, pair):
            group = slice(start, start + pair)
            key, value = keys[:, group], values[:, group]
            query, grad = queries[here, group], grads[here, group]
            grad_query = jnp.zeros((step, pair), jnp.float32)
            for side in range(2):
                head = start // HEAD_DIM + side
                query_head, grad_head = query * sides[side], grad * sides[side]
                scores = product_nt(key, query_head) * HEAD_DIM ** (-0.5)
                scores = jnp.where(allowed, scores, masked_score)
                weights = jnp.exp(scores - totals[head : head + 1, here])
                grad_weights = product_nt(value, grad_head)
                row_dot = jnp.sum(grad_weights * weights, axis=0, keepdims=True)
                grad_scores = (weights * (grad_weights - row_dot)).astype(jnp.bfloat16)
                acc_values[0:span, group] += dot_nn(weights.astype(jnp.bfloat16), grad_head)
                acc_keys[0:span, group] += dot_nn(grad_scores, query_head)
                grad_query += product_tn(grad_scores, key * sides[side])
            grad_queries[here, group] = (grad_query * HEAD_DIM ** (-0.5)).astype(jnp.bfloat16)
        return carry

    lax.fori_loop(0, rows // step, body, 0)
    grad_keys[...] = (acc_keys[0:span] * HEAD_DIM ** (-0.5)).astype(jnp.bfloat16)
    grad_values[...] = acc_values[0:span].astype(jnp.bfloat16)


class Loaded(typing.NamedTuple):
    grad_out: typing.Any
    feed_down: typing.Any
    gelu_slope: typing.Any
    feed_up: typing.Any
    feed_act: typing.Any
    second_low: typing.Any
    cross_out: typing.Any
    cross_query: typing.Any
    query_cross: typing.Any
    key_cross: typing.Any
    value_cross: typing.Any
    cross_totals: typing.Any
    cross_mix: typing.Any
    first_low: typing.Any
    memory: typing.Any
    cross_key: typing.Any
    cross_value: typing.Any
    self_out: typing.Any
    query_self: typing.Any
    key_self: typing.Any
    value_self: typing.Any
    self_totals: typing.Any
    self_mix: typing.Any
    tokens: typing.Any
    self_query: typing.Any
    self_key: typing.Any
    self_value: typing.Any


class Plain(typing.NamedTuple):
    grad_rows: typing.Any
    rows_cross: typing.Any
    gain_cross: typing.Any
    rows_self: typing.Any
    gain_self: typing.Any
    grad_vecs: typing.Any
    segment_row: typing.Any
    segment_column: typing.Any


LOADS = len(Loaded._fields)
PIECES = 16


def layer_back_kernel(total, orders, moves, *refs):
    given_hbm, plain, table, outs, narrow, held, refs = split_refs(
        refs, LOADS, len(Plain._fields), 2 * bool(moves), 4, bool(moves), LOADS, len(refs)
    )
    outcome, vec_sums, token_share, memory_share = outs
    load_sems, refs = refs[0], refs[1:]
    (pieces, recv, vec_send, vec_recv, sum_sems, gather_sems, vec_sems), refs = refs[:7], refs[7:]
    norm_buffers = [refs[0:5], refs[5:10]]
    quarters, refs = refs[10:12], refs[12:]
    rows_all = quarters[0].shape[0] * quarters[0].shape[1]
    column_buffers = [
        [pieces.at[0:2], pieces.at[2:4]] + refs[0:3],
        [pieces.at[4:6, 0:rows_all], pieces.at[6:8, 0:rows_all]] + refs[3:6],
    ]
    refs = refs[6:]
    grad_pre, grad_mix, grad_queries, grad_cross, grad_self = refs[:5]
    move_sems = refs[5:]
    loads = [
        pltpu.make_async_copy(source, target, load_sems.at[index])
        for index, (source, target) in enumerate(zip(given_hbm, held))
    ]
    for copy in loads:
        copy.start()
    loaded = set()

    def get(index):
        if index not in loaded:
            loaded.add(index)
            loads[index].wait()
        return held[index]

    at = Loaded(*range(LOADS))
    simple = Plain(*plain)
    block, place = lax.axis_index("dp"), lax.axis_index("mp")
    near, far = (block, flip(place, 1)), (block, flip(place, 2))
    bits = (total - 1).bit_length()
    over = [(flip(block, 1 << bit), place) for bit in range(bits)]
    sides = [lax.rem(lax.div(block, 1 << bit), 2) for bit in range(bits)]
    others = range(1, total) if moves else [1 << bit for bit in range(bits)]
    greet([near, far] + [(flip(block, mask), place) for mask in others])
    sent, moved = [], []
    if moves:
        moved = table_copies(moves, True, table[0], narrow[0], move_sems[0])

    height = pieces.shape[1]
    unit = height >> bits
    kept = [[0] for _ in range(PIECES)]
    copies = {}

    def offset(stage):
        return height - 2 * (height >> (stage + 1))

    def send_sum(piece, stage):
        side, rows = sides[orders[piece][stage]], height >> (stage + 1)
        kept[piece].append(kept[piece][stage] + side * rows)
        if stage:
            source, start = recv, offset(stage - 1) + (1 - side) * rows
        else:
            source, start = pieces, (1 - side) * rows
        copies[piece, stage] = remote(
            source.at[piece, pl.ds(pl.multiple_of(start, unit), rows), :],
            recv.at[piece, pl.ds(offset(stage), rows), :],
            sum_sems.at[0, piece, stage],
            sum_sems.at[1, piece, stage],
            over[orders[piece][stage]],
        )
        if stage or piece >= 8:
            sent.append(copies[piece, stage])

    def take_sum(piece, stage):
        side, rows = sides[orders[piece][stage]], height >> (stage + 1)
        copies[piece, stage].wait_recv()
        if stage:
            source, start = recv, offset(stage - 1) + side * rows
        else:
            source, start = pieces, side * rows
        mine = source[piece, pl.ds(pl.multiple_of(start, unit), rows), :]
        there = pl.ds(offset(stage), rows)
        value = (
            mine.astype(jnp.float32) + recv[piece, there, :].astype(jnp.float32)
        ).astype(jnp.bfloat16)
        if stage + 1 < bits:
            recv[piece, there, :] = value
            send_sum(piece, stage + 1)
        else:
            start = kept[piece][bits]
            outcome[piece, pl.ds(pl.multiple_of(start, unit), rows), :] = value
            send_whole(piece, stage)

    def send_whole(piece, stage):
        rows = height >> (stage + 1)
        start = pl.multiple_of(kept[piece][stage + 1], unit)
        here = outcome.at[piece, pl.ds(start, rows), :]
        copies[piece, stage, True] = remote(
            here, here, gather_sems.at[0, piece, stage], gather_sems.at[1, piece, stage],
            over[orders[piece][stage]],
        )
        sent.append(copies[piece, stage, True])

    def pump(group, turn):
        for piece in group:
            if turn < bits:
                take_sum(piece, turn)
            else:
                stage = 2 * bits - 1 - turn
                copies[piece, stage, True].wait_recv()
                if stage:
                    send_whole(piece, stage - 1)

    def weight_piece(piece, left, right):
        pieces[piece] = product_tn(left, right).astype(jnp.bfloat16)
        send_sum(piece, 0)

    def folded_piece(piece, left, right):
        part = left.shape[1]
        for turn in range(height // part):
            columns = slice(turn * part, (turn + 1) * part)
            pieces[piece, columns, :] = product_tn(left[...], right[:, columns]).astype(
                jnp.bfloat16
            )
        send_sum(piece, 0)

    tasks = []

    def work(amount):
        for task in tasks[:amount]:
            task()
        del tasks[:amount]

    def norm_back(turn, block_of, kept_rows, rows, gain, first_amount):
        outcome_list = []
        run(
            sum_quarter_steps(
                place, block_of, near, far, *norm_buffers[turn], outcome_list, sent
            ),
            lambda: work(first_amount),
        )
        grad, grad_gain, grad_shift = norm_rows_back(
            rows[...], gain[...], kept_rows + outcome_list[0]
        )
        quarters[turn][place] = grad.astype(jnp.bfloat16)
        run(
            share_quarter_steps(place, quarters[turn], near, far, norm_buffers[turn][4], sent),
            lambda: work(len(tasks)),
        )
        return grad, grad_gain, grad_shift

    grad_out = get(at.grad_out)
    grad_act = product_nt(grad_out[...], get(at.feed_down)[...])
    slope = get(at.gelu_slope)
    acc_keys, acc_values = slope.at[0], slope.at[1]
    wide = pieces.shape[2]
    for turn in range(grad_pre.shape[1] // wide):
        columns = slice(turn * wide, (turn + 1) * wide)
        start = turn * rows_all
        grad_pre[:, columns] = (
            slope[start // height, start % height : start % height + rows_all]
            * grad_act[:, columns]
        ).astype(jnp.bfloat16)
    for index in (at.feed_up, at.feed_act, at.second_low):
        get(index)
    for turn in range(4):
        columns = slice(turn * wide, (turn + 1) * wide)
        tasks.append(
            functools.partial(
                lambda turn, columns: weight_piece(
                    turn, get(at.feed_act)[...], grad_out[:, columns]
                ),
                turn, columns,
            )
        )
    for turn in range(4):
        columns = slice(turn * wide, (turn + 1) * wide)
        tasks.append(
            functools.partial(
                lambda turn, columns: weight_piece(
                    4 + turn, get(at.second_low)[...], grad_pre[:, columns]
                ),
                turn, columns,
            )
        )
    quarter = rows_all // QUARTERS
    grad_second, *vecs_cross = norm_back(
        0,
        lambda index: product_nt(rows_of(grad_pre, quarter, index), get(at.feed_up)[...]),
        simple.grad_rows[...], simple.rows_cross, simple.gain_cross, 4,
    )

    grad_out = quarters[0]
    for index in range(QUARTERS):
        grad_mix[index * quarter : (index + 1) * quarter] = product_nt(
            grad_out[index], get(at.cross_out)[...]
        ).astype(jnp.bfloat16)
    for index in (at.query_cross, at.key_cross, at.value_cross, at.cross_totals):
        get(index)
    span = get(at.key_cross).shape[0]
    owners = lax.broadcasted_iota(jnp.int32, (span, 1), 0) // MEM
    attend_back(
        get(at.query_cross), get(at.key_cross), get(at.value_cross), grad_mix, get(at.cross_totals),
        lambda here: owners == simple.segment_row[:, here],
        acc_keys, acc_values, grad_queries, grad_cross.at[0], grad_cross.at[1],
    )
    pump(range(0, 8), 0)
    for piece in range(8):
        copies[piece, 0].wait_send()
    for index in (at.cross_query, at.cross_mix, at.first_low, at.memory, at.cross_key, at.cross_value):
        get(index)
    for kind in range(2):
        tasks.append(
            functools.partial(
                lambda kind: weight_piece(8 + kind, get(at.memory)[...], grad_cross[kind]), kind
            )
        )
    tasks.append(lambda: weight_piece(10, get(at.first_low)[...], grad_queries[...]))
    tasks.append(
        lambda: folded_piece(
            11, get(at.cross_mix), grad_out[...].reshape(rows_all, grad_out.shape[2])
        )
    )

    def memory_block(index):
        return product_nt(
            grad_cross[0], rows_of(get(at.cross_key), wide, index)
        ) + product_nt(grad_cross[1], rows_of(get(at.cross_value), wide, index))

    memory_total = []
    memory_steps = sum_quarter_steps(
        place, memory_block, near, far, *column_buffers[0], memory_total, sent
    )
    grad_first, *vecs_self = norm_back(
        1,
        lambda index: product_nt(rows_of(grad_queries, quarter, index), get(at.cross_query)[...]),
        grad_second, simple.rows_self, simple.gain_self, 3,
    )
    vec_peers = [near, far] + over

    def vec_start(stage, value):
        vec_send[stage] = value
        copies[None, stage] = remote(
            vec_send.at[stage], vec_recv.at[stage], vec_sems.at[0, stage], vec_sems.at[1, stage],
            vec_peers[stage],
        )
        sent.append(copies[None, stage])

    def vec_next(stage):
        if stage >= len(vec_peers):
            return
        copies[None, stage].wait_recv()
        value = vec_send[stage] + vec_recv[stage]
        if stage + 1 < len(vec_peers):
            vec_start(stage + 1, value)
        else:
            vec_sums[...] = value

    vec_start(
        0, jnp.concatenate(vecs_self + vecs_cross + [simple.grad_vecs[...]], axis=0)
    )

    grad_out = quarters[1]
    pump(range(0, 8), 1)
    for index in range(QUARTERS):
        grad_mix[index * quarter : (index + 1) * quarter] = product_nt(
            grad_out[index], get(at.self_out)[...]
        ).astype(jnp.bfloat16)
    for index in (at.query_self, at.key_self, at.value_self, at.self_totals):
        get(index)
    key_place = lax.broadcasted_iota(jnp.int32, (rows_all, 1), 0)

    def allowed_self(here):
        query_place = here.start + lax.broadcasted_iota(jnp.int32, (1, here.size), 1)
        return (simple.segment_column[...] == simple.segment_row[:, here]) & (
            key_place <= query_place
        )

    attend_back(
        get(at.query_self), get(at.key_self), get(at.value_self), grad_mix, get(at.self_totals),
        allowed_self, acc_keys, acc_values, grad_queries, grad_self.at[0], grad_self.at[1],
    )
    for index in (at.tokens, at.self_mix, at.self_query, at.self_key, at.self_value):
        get(index)
    weight_piece(12, get(at.tokens)[...], grad_queries[...])
    weight_piece(13, get(at.tokens)[...], grad_self[0])
    weight_piece(14, get(at.tokens)[...], grad_self[1])
    folded_piece(15, get(at.self_mix), grad_out[...].reshape(rows_all, grad_out.shape[2]))
    pump(range(8, 12), 0)
    vec_next(0)
    pump(range(0, 8), 2)

    def token_block(index):
        return (
            product_nt(grad_queries[...], rows_of(get(at.self_query), wide, index))
            + product_nt(grad_self[0], rows_of(get(at.self_key), wide, index))
            + product_nt(grad_self[1], rows_of(get(at.self_value), wide, index))
        )

    token_total = []
    token_steps = sum_quarter_steps(
        place, token_block, near, far, *column_buffers[1], token_total, sent
    )
    next(token_steps)
    next(memory_steps)
    pump(range(12, 16), 0)
    vec_next(1)
    pump(range(8, 12), 1)
    run(token_steps)
    own_columns = pl.ds(pl.multiple_of(place * wide, wide), wide)
    token_share[...] = token_total[0] + quarters[1][:, :, own_columns].reshape(
        rows_all, wide
    ).astype(jnp.float32)
    pump(range(0, 8), 3)
    vec_next(2)
    run(memory_steps)
    memory_share[...] = memory_total[0]
    groups = [(range(0, 8), 4), (range(8, 12), 2), (range(12, 16), 1)]
    stage = 3
    while groups:
        for group, turn in groups:
            pump(group, turn)
        vec_next(stage)
        stage += 1
        groups = [(group, turn + 1) for group, turn in groups if turn + 1 < 2 * bits]
    while stage < len(vec_peers):
        vec_next(stage)
        stage += 1
    for copy in sent:
        copy.wait_send()
    finish(moved)


def layer_back(values, plain, number, table=None, narrow=None, moves=()):
    total = lax.axis_size("dp")
    bits = (total - 1).bit_length()
    rest = list(range(2, bits))
    orders = [[0, 1] + rest if piece % 4 else [1, 0] + rest for piece in range(PIECES)]
    given = list(values) + list(plain)
    in_specs = [ANY] * len(values) + [VMEM] * len(plain)
    rows, width = values.tokens.shape
    span = values.memory.shape[0]
    part = values.self_query.shape[1]
    quarter = rows // QUARTERS
    stages = bits + 2
    vecs = (6, width)
    out_shape = [
        jax.ShapeDtypeStruct((PIECES, width, part), jnp.bfloat16),
        jax.ShapeDtypeStruct(vecs, jnp.float32),
        jax.ShapeDtypeStruct((rows, part), jnp.float32),
        jax.ShapeDtypeStruct((span, part), jnp.float32),
    ]
    out_specs = [VMEM] * 4
    scratch = [pltpu.VMEM(value.shape, value.dtype) for value in values]
    scratch += [
        DMA((LOADS,)),
        pltpu.VMEM((PIECES, width, part), jnp.bfloat16),
        pltpu.VMEM((PIECES, width - (width >> bits), part), jnp.bfloat16),
        pltpu.VMEM((stages,) + vecs, jnp.float32),
        pltpu.VMEM((stages,) + vecs, jnp.float32),
        DMA((2, PIECES, bits)),
        DMA((2, PIECES, bits)),
        DMA((2, stages)),
    ]
    scratch += exchange_scratch(quarter, width) * 2
    scratch += [pltpu.VMEM((QUARTERS, quarter, width), jnp.bfloat16)] * 2
    scratch += exchange_scratch(span, part)[2:] + exchange_scratch(rows, part)[2:]
    scratch += [
        pltpu.VMEM((rows, values.feed_up.shape[1]), jnp.bfloat16),
        pltpu.VMEM((rows, part), jnp.bfloat16),
        pltpu.VMEM((rows, part), jnp.bfloat16),
        pltpu.VMEM((2, span, part), jnp.bfloat16),
        pltpu.VMEM((2, rows, part), jnp.bfloat16),
    ]
    aliases = {}
    if moves:
        aliases = {len(given) + 1: len(out_shape)}
        given += [table, narrow]
        in_specs += [ANY] * 2
        out_shape.append(jax.ShapeDtypeStruct(narrow.shape, narrow.dtype))
        out_specs.append(ANY)
        scratch.append(DMA((2, len(moves))))
    return pl.pallas_call(
        functools.partial(layer_back_kernel, total, orders, tuple(moves)),
        out_shape=out_shape,
        in_specs=in_specs,
        out_specs=out_specs,
        scratch_shapes=scratch,
        input_output_aliases=aliases,
        compiler_params=pltpu.CompilerParams(
            collective_id=number, has_side_effects=True, vmem_limit_bytes=62 * 2**20
        ),
    )(*given)


def unfold(matrix, height):
    return jnp.concatenate(
        [matrix[start : start + height] for start in range(0, matrix.shape[0], height)], axis=1
    )


def shift_pairs(total, step):
    return [(index, (index + step) % total) for index in range(total)]


def spread_rows(table):
    total = lax.axis_size("dp")
    place = lax.axis_index("dp")
    width = table.shape[1]
    part = table.shape[0] // total
    whole = jnp.zeros((part, width * total), table.dtype)
    for step in range(total):
        block = lax.dynamic_slice_in_dim(table, (place + step) % total * part, part, 0)
        if step:
            block = lax.ppermute(block, "dp", shift_pairs(total, step))
        whole = lax.dynamic_update_slice_in_dim(
            whole, block, (place - step) % total * width, 1
        )
    return whole


def return_rows(rows, height):
    total = lax.axis_size("dp")
    place = lax.axis_index("dp")
    part = rows.shape[0]
    width = rows.shape[1] // total
    whole = jnp.zeros((height, width), rows.dtype)
    for step in range(total):
        block = lax.dynamic_slice_in_dim(rows, (place + step) % total * width, width, 1)
        if step:
            block = lax.ppermute(block, "dp", shift_pairs(total, step))
        whole = lax.dynamic_update_slice_in_dim(
            whole, block, (place - step) % total * part, 0
        )
    return whole


def local(
    tokens,
    memory,
    segment_ids,
    answer_ids,
    loss_mask,
    doc_scores,
    slot_place,
    self_query,
    self_key,
    self_value,
    self_out,
    cross_query,
    cross_key,
    cross_value,
    cross_out,
    feed_up,
    feed_down,
    gain_self,
    shift_self,
    gain_cross,
    shift_cross,
    gain_feed,
    shift_feed,
    embedding,
):
    row_count, row_len = segment_ids.shape
    total = lax.axis_size("dp")
    direct = total == 8 and embedding.shape[1] % 128 == 0
    last = None
    if direct:
        part = embedding.shape[0] // total
        last = lax.ppermute(
            lax.dynamic_slice_in_dim(
                embedding, (total - 1 - lax.axis_index("dp")) * part, part, 0
            ),
            "dp",
            [(index, total - 1 - index) for index in range(total)],
        )
    span = SEG_ROW * MEM
    quarter = tokens.shape[0] // QUARTERS
    inputs = lax.dynamic_slice_in_dim(tokens, lax.axis_index("mp") * quarter, quarter, 0)
    places = jnp.arange(row_len, dtype=jnp.int32)
    owners = jnp.arange(span, dtype=jnp.int32) // MEM
    self_masks = [
        (segment_ids[0][:, None] == segment_ids[0][None, :]) & (places[None, :] <= places[:, None])
    ]
    cross_masks = [segment_ids[0][:, None] == owners[None, :]]
    query_self = product(tokens, self_query).astype(jnp.bfloat16)
    key_self = product(tokens, self_key).astype(jnp.bfloat16)
    value_self = product(tokens, self_value).astype(jnp.bfloat16)
    self_mix, self_totals = run_rows(query_self, key_self, value_self, self_masks)
    first_low, first_norm, rows_self, ids_all, *wide = mix_norm(
        self_mix, self_out, inputs, gain_self, shift_self, 0,
        jnp.concatenate([segment_ids, answer_ids, loss_mask], axis=0),
        embedding, None, (4, 1, 0) if direct else (),
    )
    segments_all, answers_all, kept_all = (
        ids_all[:, kind * row_count : (kind + 1) * row_count].reshape(-1, row_len)
        for kind in range(3)
    )
    query_cross = product(first_low, cross_query).astype(jnp.bfloat16)
    key_cross = product(memory, cross_key).astype(jnp.bfloat16)
    value_cross = product(memory, cross_value).astype(jnp.bfloat16)
    cross_mix, cross_totals = run_rows(query_cross, key_cross, value_cross, cross_masks)
    second_low, second_norm, rows_cross, *wide = mix_norm(
        cross_mix, cross_out, first_norm, gain_cross, shift_cross, 1, None,
        embedding, *wide, masks=(5, 2) if direct else (),
    )
    feed_pre = product(second_low, feed_up)
    feed_act, gelu_pull = jax.vjp(gelu_exact, feed_pre)
    gelu_slope = gelu_pull(jnp.ones_like(feed_pre))[0]
    feed_act = feed_act.astype(jnp.bfloat16)
    vocab_local = embedding.shape[0]
    part = vocab_local // total
    offset = lax.axis_index("mp") * vocab_local + lax.axis_index("dp") * part
    targets = (answers_all - offset)[:, None, :]
    table = embedding if direct else spread_rows(embedding)
    states, rows_feed, logits, totals, *wide = feed_norm(
        feed_act, feed_down, second_norm, gain_feed, shift_feed, targets, 2,
        table, *wide, last=last, early=(6, 3) if direct else (),
    )
    if direct:
        spot = (total - 1 - lax.axis_index("dp")) * last.shape[1]
        table_rows = lax.dynamic_update_slice_in_dim(wide[0], last, spot, 1)
    else:
        table_rows = table
    log_total = totals[0] + jnp.log(totals[1])
    picked = totals[2]
    keeper = kept_all.astype(jnp.float32)
    token_logp = (picked - log_total) * keeper
    seg_hot = (
        segments_all[:, :, None] == jnp.arange(SEG_ROW, dtype=jnp.int32)[None, None, :]
    ).astype(jnp.float32)
    seg_sums = jnp.sum(seg_hot * token_logp[:, :, None], axis=1)
    counts = jnp.sum(seg_hot * keeper[:, :, None], axis=1)
    likely_all = (seg_sums / jnp.maximum(counts, 1.0)).reshape(-1)
    place_hot = (
        slot_place[:, None] == jnp.arange(likely_all.shape[0], dtype=jnp.int32)[None, :]
    ).astype(jnp.float32)

    def marginal(scores, likely):
        joint_score = jax.nn.log_softmax(scores, axis=1) + jnp.dot(
            place_hot, likely, precision=highest
        ).reshape(scores.shape)
        return -jnp.sum(jax.nn.logsumexp(joint_score, axis=1))

    loss, pullback = jax.vjp(marginal, doc_scores, likely_all)
    grad_scores, grad_likely = pullback(jnp.ones_like(loss))
    per_segment = grad_likely.reshape(counts.shape) / jnp.maximum(counts, 1.0)
    grad_logp = (jnp.sum(seg_hot * per_segment[:, None, :], axis=2) * keeper)[:, None, :]
    log_total = log_total[:, None, :]
    if direct:
        head_values = (logits, table_rows, states, log_total, grad_logp, targets)
    else:
        hot = (targets == jnp.arange(part, dtype=jnp.int32)[None, :, None]).astype(jnp.float32)
        grad_logits = (grad_logp * (hot - jnp.exp(logits - log_total))).astype(jnp.bfloat16)
        parts = jnp.einsum(
            "rvt,vd->rtd", grad_logits, table_rows, preferred_element_type=jnp.float32
        ).astype(jnp.bfloat16)
        head_values = (parts.reshape(states.shape),)
        grad_words = jnp.einsum(
            "rvt,rtd->vd",
            grad_logits,
            states.reshape(total, -1, states.shape[3]),
            preferred_element_type=jnp.float32,
        ).astype(jnp.bfloat16)
    grad_branch, grad_res3, grad_vecs_feed, *words = head_back(
        head_values, rows_feed, gain_feed, 3, (4, 1, 0) if direct else ()
    )
    grad_words, *narrow = words if direct else (grad_words,)
    values = Loaded(
        grad_out=grad_branch,
        feed_down=feed_down,
        gelu_slope=jnp.concatenate(
            jnp.split(gelu_slope, gelu_slope.shape[1] // self_query.shape[1], axis=1), axis=0
        ).reshape((2,) + self_query.shape),
        feed_up=feed_up,
        feed_act=feed_act,
        second_low=second_low,
        cross_out=cross_out,
        cross_query=cross_query,
        query_cross=query_cross,
        key_cross=key_cross,
        value_cross=value_cross,
        cross_totals=cross_totals[0][..., 0],
        cross_mix=cross_mix,
        first_low=first_low,
        memory=memory,
        cross_key=cross_key,
        cross_value=cross_value,
        self_out=self_out,
        query_self=query_self,
        key_self=key_self,
        value_self=value_self,
        self_totals=self_totals[0][..., 0],
        self_mix=self_mix,
        tokens=tokens,
        self_query=self_query,
        self_key=self_key,
        self_value=self_value,
    )
    plain = Plain(
        grad_rows=grad_res3,
        rows_cross=rows_cross,
        gain_cross=gain_cross.reshape(1, -1),
        rows_self=rows_self,
        gain_self=gain_self.reshape(1, -1),
        grad_vecs=grad_vecs_feed,
        segment_row=segment_ids.reshape(1, -1),
        segment_column=segment_ids.reshape(-1, 1),
    )
    sums, grad_vecs, grad_tokens, memory_share, *narrow = layer_back(
        values, plain, 4, grad_words, *narrow, moves=(5, 6, 7, 2, 3) if direct else ()
    )
    grad_table = (
        narrow[0] if direct else return_rows(grad_words, vocab_local)
    ).astype(jnp.float32)
    sums = [part.astype(jnp.float32) for part in sums]
    sum_down = jnp.concatenate(sums[0:4], axis=1)
    sum_up = jnp.concatenate(sums[4:8], axis=1)
    sum_ck, sum_cv, sum_cq, sum_co, sum_sq, sum_sk, sum_sv, sum_so = sums[8:]
    sum_co, sum_so = (unfold(part, self_out.shape[0]) for part in (sum_co, sum_so))
    return (
        loss,
        grad_tokens,
        memory_share,
        sum_sq,
        sum_sk,
        sum_sv,
        sum_so,
        sum_cq,
        sum_ck,
        sum_cv,
        sum_co,
        sum_up,
        sum_down,
        *grad_vecs,
        grad_table,
        grad_scores,
    )


def solution(mesh):
    return jax.shard_map(
        local,
        mesh=mesh,
        in_specs=(
            P("dp", None),
            P("dp", None),
            P("dp", None),
            P("dp", None),
            P("dp", None),
            P(),
            P(),
            P(None, "mp"),
            P(None, "mp"),
            P(None, "mp"),
            P("mp", None),
            P(None, "mp"),
            P(None, "mp"),
            P(None, "mp"),
            P("mp", None),
            P(None, "mp"),
            P("mp", None),
            P(),
            P(),
            P(),
            P(),
            P(),
            P(),
            P("mp", "dp"),
        ),
        out_specs=(
            P(),
            P("dp", "mp"),
            P("dp", "mp"),
            P(None, "mp"),
            P(None, "mp"),
            P(None, "mp"),
            P("mp", None),
            P(None, "mp"),
            P(None, "mp"),
            P(None, "mp"),
            P("mp", None),
            P(None, "mp"),
            P("mp", None),
            P(),
            P(),
            P(),
            P(),
            P(),
            P(),
            P("mp", "dp"),
            P(),
        ),
        check_vma=False,
    )
```

time: 685 us -> 557 us (0.81)
  matrix products: 143 us -> 23.6 us
  Pallas kernels: 433 us -> 472 us
  other arithmetic: 51.1 us -> 32.3 us
  between operations: 19 us -> 3.41 us
  waiting for transfers between devices: 14.7 us -> 0.01 us
    dot_general x28 -> x0, matrix products: 95.7 us -> none  [the longest x11 44 us: product_tn(): lax.dot_general(left_side, right_side, (((0,), (0,)), ((), ())), preferre...]
    pallas_call x6 -> x3, Pallas kernels: 367 us -> 422 us  [the longest x1 239 us: layer_back(): pl.pallas_call(functools.partial(layer_back_kernel, total, orders, tuple(...]
    dot_general x8 -> x7, matrix products: 41 us -> 16.1 us  [product(): return jnp.dot(left_side, right_side, preferred_element_type=jnp.float32)]
    pallas_call x2, Pallas kernels: 66.4 us -> 49.9 us  [mix_norm(): pl.pallas_call(functools.partial(mix_norm_kernel, total, int(ids is not N...]
    psum x1 -> x0, waiting for transfers between devices: 14.2 us -> none  [local(): lax.psum((grad_feed_up, grad_feed_down), 'dp')]
    reduce_sum x1 -> x0, other arithmetic: 12 us -> none  [local(): jnp.sum(jnp.exp(logits - local_top[:, None]), axis=1)]
    convert_element_type x7 -> x3, other arithmetic: 22.1 us -> 12.7 us  [the longest x1 6.02 us: local(): sums = [part.astype(jnp.float32) for part in sums]]
    concatenate x1 -> x3, other arithmetic: 0.02 us -> 7.82 us  [the longest x1 3.79 us: local(): sum_down = jnp.concatenate(sums[0:4], axis=1)]
  transfers between devices with their start and end apart: 3 -> 1, of which waited for: 1 -> 0; matrix products, arithmetic and copies ran while one was open for 7% -> 7% of each run, Pallas kernels for 23% -> 9%
where the time goes in v4:
time: 557 us; the launch traced here: 552 us
  Pallas kernels  472 us (85%)
  other arithmetic  32.3 us (6%)
  matrix products  23.6 us (4%)
  local copies, waits for them, and re-layouts  15.1 us (3%)
  starting transfers between devices  5.98 us (1%)
    pallas_call x1, Pallas kernels, layer_back(): pl.pallas_call(functools.partial(layer_back_kernel, total, orders, tuple(...  239 us
    pallas_call x1, Pallas kernels, feed_norm(): pl.pallas_call(functools.partial(feed_norm_kernel, total, tuple(early)),...  95.9 us
    pallas_call x1, Pallas kernels, head_back(): pl.pallas_call(functools.partial(head_back_kernel, total, tuple(masks), i...  87.2 us
    pallas_call x2, Pallas kernels, mix_norm(): pl.pallas_call(functools.partial(mix_norm_kernel, total, int(ids is not N...  49.9 us
    dot_general x7, matrix products, product(): return jnp.dot(left_side, right_side, preferred_element_type=jnp.float32)  16.1 us
  transfers between devices with their start and end apart: 1, of which 0 were waited for; matrix products, arithmetic and copies ran while one was open for 7% of the time, Pallas kernels for 9%

profile of v4, /device:TPU:0, one launch (start us, length us, event | category | flops | bytes accessed | tf_op | source)
XLA Modules:
  0.0 552.4 jit_solution(12355398552297906960)
XLA Ops:
  0.7 1.9 constant_dynamic-slice_fusion
  2.5 6.0 %collective-permute-start = (bf16[1600,128]{1,0:T(8,128)(2,1)}, bf16[1600,128]{1,0:T(8,128)(2,1)}, u32[]{:S(2)}, u32[]{:S(2)}) collective-permute-start(bf16[1600,128]{1,0:T(8,128)(2,1)} %constant_dynamic-slice_fusion), channel_id=1, source_target_pairs={{0,28},{4,24},{8,20},{12,16},{16,12},{20,8},{24,4},{28,0},{1,29},{... | collective-permute-start | bytes 1228808 | tf_op jit(solution)/shard_map/ppermute | solution.py:1375
  9.5 1.9 convolution_convert_fusion.4.refs_18_
  11.5 1.5 convolution_convert_fusion.3.refs_19_
  15.7 1.4 fusion.13
  17.4 28.2 %shard_map.391 = (bf16[4,128,1024]{2,1,0:T(8,128)(2,1)S(1)}, f32[128,1024]{1,0:T(8,128)S(1)}, f32[128,1024]{1,0:T(8,128)S(1)}, s32[8,3,512]{2,1,0:T(4,128)S(1)}, bf16[1600,1024]{1,0:T(8,128)(2,1)}) custom-call(bf16[512,256]{1,0:T(8,128)(2,1)S(1)} %copy.94.refs_0_.refs_22_, bf16[256,1024]{1,0:T(8,128)(2,1)S(1)} %copy-done.2, ...), custom_call_target="tpu_custom_call" | custom-call | tf_op jit(solution)/shard_map/pallas_call | solution.py:310
  48.3 2.3 convolution_convert_fusion.refs_9_
  50.9 2.4 convolution_convert_fusion.1.refs_10_
  54.3 1.7 fusion
  56.0 2.3 fusion.1
  59.0 2.9 fusion.12
  62.1 21.7 %shard_map.392 = (bf16[4,128,1024]{2,1,0:T(8,128)(2,1)S(1)}, f32[128,1024]{1,0:T(8,128)S(1)}, f32[128,1024]{1,0:T(8,128)S(1)}, bf16[1600,1024]{1,0:T(8,128)(2,1)}) custom-call(bf16[512,256]{1,0:T(8,128)(2,1)S(1)} %copy.101.refs_0_.refs_12_, bf16[256,1024]{1,0:T(8,128)(2,1)S(1)} %copy-done.3, ...), custom_call_target="tpu_custom_call", output_to_operand_aliasing={{3}: (6, {})} | custom-call | tf_op jit(solution)/shard_map/pallas_call | solution.py:310
  83.9 7.2 %multiply_add_fusion = (f32[512,1024]{1,0:T(8,128)S(1)}, f32[512,1024]{1,0:T(8,128)}, f32[512,1024]{1,0:T(8,128)}) fusion(bf16[512,1024]{1,0:T(8,128)(2,1)S(1)} %bitcast.124, bf16[1024,1024]{1,0:T(8,128)(2,1)S(1)} %copy-done.16), kind=kOutput, calls=%fused_computation.16 | convolution fusion | flops 1109393408 | bytes 9437184 | tf_op jit(solution)/shard_map/dot_general | solution.py:22
  91.9 1.5 pad_maximum_fusion
  94.5 3.7 multiply_convert_fusion.refs_0_.refs_4_
  98.2 95.9 %shard_map.393 = (bf16[8,4,128,1024]{3,2,1,0:T(8,128)(2,1)}, f32[128,1024]{1,0:T(8,128)}, f32[8,1600,512]{2,1,0:T(8,128)}, f32[3,8,512]{2,1,0:T(8,128)}, bf16[1600,1024]{1,0:T(8,128)(2,1)}) custom-call(bf16[512,1024]{1,0:T(8,128)(2,1)} %multiply_convert_fusion.refs_0_.refs_4_, bf16[1024,1024]{1,0:T(8,128)(2,1)} %refs_1_.7, ...), custom_call_target="tpu_custom_call", output_to_operand_aliasing={{4}: (7, {})} | custom-call | tf_op jit(solution)/shard_map/pallas_call | solution.py:530
  199.4 1.9 constant_dynamic-update-slice_fusion.refs_3_
  201.2 87.2 %shard_map.394 = (bf16[4,128,1024]{2,1,0:T(8,128)(2,1)}, f32[128,1024]{1,0:T(8,128)}, f32[2,1024]{1,0:T(2,128)}, bf16[1600,1024]{1,0:T(8,128)(2,1)}, bf16[12800,128]{1,0:T(8,128)(2,1)}) custom-call(f32[8,1600,512]{2,1,0:T(8,128)} %get-tuple-element.53.refs_0_, f32[128,1024]{1,0:T(8,128)} %get-tuple-element.54.refs_1_, f32[1,1024]{1,0:T(1,128)} %bitcast.149, ...), custom_call_target="tpu_custom_call" | custom-call | tf_op jit(solution)/shard_map/pallas_call | solution.py:809
  288.4 239.0 %shard_map.395 = (bf16[16,1024,256]{2,1,0:T(8,128)(2,1)}, f32[6,1024]{1,0:T(8,128)}, f32[512,256]{1,0:T(8,128)}, f32[1024,256]{1,0:T(8,128)}, bf16[12800,128]{1,0:T(8,128)(2,1)}) custom-call(bf16[512,1024]{1,0:T(8,128)(2,1)} %bitcast.134, bf16[1024,1024]{1,0:T(8,128)(2,1)} %refs_1_.7, f32[2,1024,256]{2,1,0:T(8,128)} %bitcast.132, ...), custom_call_target="tpu_custom_call", output_to_operand_aliasing={{4}: (36, {})} | custom-call | tf_op jit(solution)/shard_map/pallas_call | solution.py:1288
  527.5 6.0 %slice_bitcast_fusion.3 = (bf16[1024,256]{1,0:T(8,128)(2,1)S(1)}, bf16[1024,256]{1,0:T(8,128)(2,1)S(1)}, bf16[1024,256]{1,0:T(8,128)(2,1)}, bf16[1024,256]{1,0:T...) fusion(bf16[16,1024,256]{2,1,0:T(8,128)(2,1)} %get-tuple-element.66), kind=kLoop, calls=%fused_computation.54 | loop fusion | flops 2097152 | bytes 20971520 | tf_op jit(solution)/shard_map/convert_element_type | solution.py:1521
  536.1 3.0 convert_element_type.175
  540.4 3.8 maximum_convert_fusion.1
  544.1 2.6 maximum_convert_fusion
  546.8 1.1 pad_maximum_fusion.2
  (138 shorter events, 22.2 us)
Async XLA Ops:
  0.7 10.9 %copy-start.17 = (bf16[512,1024]{1,0:T(8,128)(2,1)S(1)}, bf16[512,1024]{1,0:T(8,128)(2,1)}, u32[]{:S(2)}) copy-start(bf16[512,1024]{1,0:T(8,128)(2,1)} %refs_23_.1) | copy-start | bytes 3145732
  2.5 95.6 %collective-permute-start = (bf16[1600,128]{1,0:T(8,128)(2,1)}, bf16[1600,128]{1,0:T(8,128)(2,1)}, u32[]{:S(2)}, u32[]{:S(2)}) collective-permute-start(bf16[1600,128]{1,0:T(8,128)(2,1)} %constant_dynamic-slice_fusion), channel_id=1, source_target_pairs={{0,28},{4,24},{8,20},{12,16},{16,12},{20,8},{24,4},{28,0},{1,29},{... | collective-permute-start | bytes 1228808 | tf_op jit(solution)/shard_map/ppermute | solution.py:1375
  9.5 3.7 copy-start.30
  17.2 28.3 %copy-start = (bf16[512,256]{1,0:T(8,128)(2,1)}, bf16[512,256]{1,0:T(8,128)(2,1)S(1)}, u32[]{:S(2)}) copy-start(bf16[512,256]{1,0:T(8,128)(2,1)S(1)} %copy.94.refs_0_.refs_22_) | copy-start | bytes 786436
  17.4 30.0 %copy-start.31 = (bf16[1024,256]{1,0:T(8,128)(2,1)S(1)}, bf16[1024,256]{1,0:T(8,128)(2,1)}, u32[]{:S(2)}) copy-start(bf16[1024,256]{1,0:T(8,128)(2,1)} %refs_7_.1) | copy-start | bytes 1572868
  47.8 2.8 copy-start.21
  50.6 2.6 copy-start.14
  53.3 2.7 copy-start.15
  56.0 3.0 copy-start.34
  58.9 3.1 copy-start.36
  58.9 3.2 copy-start.3
  58.9 3.2 copy-start.9
  59.0 3.2 copy-start.11
  62.0 21.8 %copy-start.1 = (bf16[512,256]{1,0:T(8,128)(2,1)}, bf16[512,256]{1,0:T(8,128)(2,1)S(1)}, u32[]{:S(2)}) copy-start(bf16[512,256]{1,0:T(8,128)(2,1)S(1)} %copy.101.refs_0_.refs_12_) | copy-start | bytes 786436
  62.1 21.8 %copy-start.16 = (bf16[1024,1024]{1,0:T(8,128)(2,1)S(1)}, bf16[1024,1024]{1,0:T(8,128)(2,1)}, u32[]{:S(2)}) copy-start(bf16[1024,1024]{1,0:T(8,128)(2,1)} %refs_3_.1) | copy-start | bytes 6291460
  83.9 7.2 %copy-start.5 = (bf16[4,128,1024]{2,1,0:T(8,128)(2,1)}, bf16[4,128,1024]{2,1,0:T(8,128)(2,1)S(1)}, u32[]{:S(2)}) copy-start(bf16[4,128,1024]{2,1,0:T(8,128)(2,1)S(1)} %get-tuple-element.49) | copy-start | bytes 3145732
  83.9 7.2 %copy-start.7 = (f32[128,1024]{1,0:T(8,128)}, f32[128,1024]{1,0:T(8,128)S(1)}, u32[]{:S(2)}) copy-start(f32[128,1024]{1,0:T(8,128)S(1)} %get-tuple-element.59.refs_28_) | copy-start | bytes 1572868
  83.9 7.2 %copy-start.8 = (f32[128,1024]{1,0:T(8,128)}, f32[128,1024]{1,0:T(8,128)S(1)}, u32[]{:S(2)}) copy-start(f32[128,1024]{1,0:T(8,128)S(1)} %get-tuple-element.50.refs_2_) | copy-start | bytes 1572868
  533.5 2.6 copy-start.13
  536.1 3.0 copy-start.37
  544.1 2.6 copy-start.23
  544.1 2.6 copy-start.24
  544.1 2.6 copy-start.25
  546.8 2.5 copy-start.33
  (18 other events, 27.3 us)

commit v5 on v4

--- a/solution.py
+++ b/solution.py
@@ -58,13 +58,8 @@
     mixed_out = jnp.einsum(
         "hqk,khd->qhd", probabilities, split_heads(values), preferred_element_type=jnp.float32
     )
-    return (mixed_out.reshape(queries.shape[0], queries.shape[1]), largest + jnp.log(total))
-
-
-def run_rows(queries, keys, values, masks):
-    mixed_out, log_total = attend_forward(queries, keys, values, masks[0])
-    totals = [log_total]
-    return (mixed_out.astype(jnp.bfloat16), totals)
+    mixed_out = mixed_out.reshape(queries.shape).astype(jnp.bfloat16)
+    return mixed_out, (largest + jnp.log(total))[..., 0]
 
 
 MESH = pl.DeviceIdType.MESH
@@ -369,8 +364,13 @@
         return copy
 
     first = {}
-    for mask in range(2, total, 2):
-        first[mask] = hop(0, mask, low, (flip(block, mask), place), block, place)
+
+    def spread(masks):
+        for mask in masks:
+            first[mask] = hop(0, mask, low, (flip(block, mask), place), block, place)
+
+    spread([2])
+    nearest = len(sent) - 1
     over, ends = {}, {}
 
     def pass_on(mask):
@@ -439,6 +439,10 @@
     for step in range(total + lag):
         if step < total:
             arrive(step)
+        if step == 0:
+            del sent[nearest]
+            first[2].wait_send()
+            spread(range(4, total, 2))
         if 2 <= step < total + 2:
             pass_on(step - 2)
         if step == lag:
@@ -555,11 +559,9 @@
     others = range(1, total) if masks else [1] + list(range(2, total, 2))
     greet([near, far] + [(flip(block, mask), place) for mask in others])
     moved = []
-    aside = [mask + 1 for mask in range(0, total // 2, 2)]
-    order = []
-    for late, soon in zip(range(total - 1, total // 2, -2), aside[::-1]):
-        order += [late, soon]
-    order += [mask for mask in range(total - 1, -1, -1) if mask % 2 == 0]
+    aside = [1]
+    order = [mask for mask in range(total - 1, -1, -1) if mask != 1]
+    order.insert(1, 1)
     sent, loads, sib, across, over, ends = [], {}, {}, {}, {}, {}
 
     def to_near(mask, slot, source):
@@ -860,6 +862,425 @@
     lax.fori_loop(0, rows // step, body, 0)
     grad_keys[...] = (acc_keys[0:span] * HEAD_DIM ** (-0.5)).astype(jnp.bfloat16)
     grad_values[...] = acc_values[0:span].astype(jnp.bfloat16)
+
+
+def attend(queries, keys, values, allowed_at, mixed, totals):
+    rows, width = queries.shape
+    step = min(256, rows)
+    pair = 2 * HEAD_DIM
+    lanes = lax.broadcasted_iota(jnp.int32, (1, pair), 1)
+    sides = [(lanes // HEAD_DIM == side).astype(jnp.bfloat16) for side in range(2)]
+
+    def body(turn, carry):
+        here = pl.ds(pl.multiple_of(turn * step, step), step)
+        allowed = allowed_at(here)
+        for start in range(0, width, pair):
+            group = slice(start, start + pair)
+            key, value, query = keys[:, group], values[:, group], queries[here, group]
+            mix = jnp.zeros((step, pair), jnp.float32)
+            for side in range(2):
+                head = start // HEAD_DIM + side
+                scores = product_nt(key, query * sides[side]) * HEAD_DIM ** (-0.5)
+                scores = jnp.where(allowed, scores, masked_score)
+                largest = jnp.max(scores, axis=0, keepdims=True)
+                weights = jnp.exp(scores - largest)
+                amount = jnp.sum(weights, axis=0, keepdims=True)
+                chances = (weights * (1.0 / amount)).astype(jnp.bfloat16)
+                mix += product_tn(chances, value * sides[side])
+                totals[head : head + 1, here] = largest + jnp.log(amount)
+            mixed[here, group] = mix.astype(jnp.bfloat16)
+        return carry
+
+    lax.fori_loop(0, rows // step, body, 0)
+
+
+class Given(typing.NamedTuple):
+    tokens: typing.Any
+    self_query: typing.Any
+    self_key: typing.Any
+    self_value: typing.Any
+    self_out: typing.Any
+    memory: typing.Any
+    cross_key: typing.Any
+    cross_value: typing.Any
+    cross_query: typing.Any
+    cross_out: typing.Any
+    feed_up: typing.Any
+    feed_down: typing.Any
+
+
+class Small(typing.NamedTuple):
+    ids: typing.Any
+    segment_row: typing.Any
+    segment_column: typing.Any
+    gain_self: typing.Any
+    shift_self: typing.Any
+    gain_cross: typing.Any
+    shift_cross: typing.Any
+    gain_feed: typing.Any
+    shift_feed: typing.Any
+
+
+class Kept(typing.NamedTuple):
+    query_self: typing.Any
+    key_self: typing.Any
+    value_self: typing.Any
+    self_totals: typing.Any
+    self_mix: typing.Any
+    first_low: typing.Any
+    rows_self: typing.Any
+    key_cross: typing.Any
+    value_cross: typing.Any
+    query_cross: typing.Any
+    cross_totals: typing.Any
+    cross_mix: typing.Any
+    second_low: typing.Any
+    rows_cross: typing.Any
+    feed_act: typing.Any
+    gelu_slope: typing.Any
+    rows_feed: typing.Any
+    words: typing.Any
+    states: typing.Any
+
+
+def layer_kernel(total, *refs):
+    count, made = len(Given._fields), len(Kept._fields)
+    sources, small, table, targets, (logits, totals, ids_all), held, kept, refs = split_refs(
+        refs, count, len(Small._fields), 1, made, 3, count, made, len(refs)
+    )
+    load_sems, keep_sems, ids_sems, ids_local, move_sems = refs[:5]
+    buffers, refs = [refs[5:10], refs[10:15], refs[15:20]], refs[20:]
+    normed, hops, staged, sends, recvs, staged_sems, stage_sems = refs
+    small, kept = Small(*small), Kept(*kept)
+    block, place = lax.axis_index("dp"), lax.axis_index("mp")
+    near, far = (block, flip(place, 1)), (block, flip(place, 2))
+    beside = (flip(block, 1), place)
+    bits = (total - 1).bit_length()
+    loads = [
+        pltpu.make_async_copy(source, target, load_sems.at[index])
+        for index, (source, target) in enumerate(zip(sources, held))
+    ]
+    for copy in loads:
+        copy.start()
+    loaded = set()
+
+    def get(index):
+        if index not in loaded:
+            loaded.add(index)
+            loads[index].wait()
+        return held[index]
+
+    at = Given(*range(count))
+    places = Kept(*range(made))
+    saves = [
+        pltpu.make_async_copy(source, target, keep_sems.at[index])
+        for index, (source, target) in enumerate(zip(kept, targets))
+    ]
+
+    def save(*indices):
+        for index in indices:
+            saves[index].start()
+
+    greet([near, far] + [(flip(block, mask), place) for mask in range(1, total)])
+    moved = table_copies((4, 5, 6, 7, 1, 2, 3, 0), False, table[0], kept.words, move_sems)
+    ids_copies = [pltpu.make_async_copy(small.ids, ids_all.at[block], ids_local)]
+    ids_copies[0].start()
+    for mask in range(1, total):
+        ids_copies.append(
+            remote(
+                small.ids, ids_all.at[block], ids_sems.at[0, mask], ids_sems.at[1, mask],
+                (flip(block, mask), place),
+            )
+        )
+    sent = []
+    tokens = get(at.tokens)
+    span, width = tokens.shape
+    height = span // QUARTERS
+    for weight, outcome, index in (
+        (at.self_query, kept.query_self, places.query_self),
+        (at.self_key, kept.key_self, places.key_self),
+        (at.self_value, kept.value_self, places.value_self),
+    ):
+        outcome[...] = dot_nn(tokens[...], get(weight)[...]).astype(jnp.bfloat16)
+        save(index)
+    key_place = lax.broadcasted_iota(jnp.int32, (span, 1), 0)
+
+    def allowed_self(here):
+        query_place = here.start + lax.broadcasted_iota(jnp.int32, (1, here.size), 1)
+        return (small.segment_column[...] == small.segment_row[:, here]) & (
+            key_place <= query_place
+        )
+
+    attend(
+        kept.query_self, kept.key_self, kept.value_self, allowed_self, kept.self_mix,
+        kept.self_totals,
+    )
+    save(places.self_totals, places.self_mix)
+
+    def join(turn, left, weight, residual, rows, fill):
+        outcome = []
+        run(
+            sum_quarter_steps(
+                place,
+                lambda index: dot_nn(rows_of(left, height, index), weight[...]),
+                near, far, *buffers[turn], outcome, sent,
+            ),
+            fill,
+        )
+        rows[...] = residual + outcome[0]
+
+    def share(turn, quarters, fill):
+        run(share_quarter_steps(place, quarters, near, far, buffers[turn][4], sent), fill)
+
+    def make_keys():
+        kept.key_cross[...] = dot_nn(get(at.memory)[...], get(at.cross_key)[...]).astype(
+            jnp.bfloat16
+        )
+
+    def make_values():
+        kept.value_cross[...] = dot_nn(get(at.memory)[...], get(at.cross_value)[...]).astype(
+            jnp.bfloat16
+        )
+
+    join(
+        0, kept.self_mix, get(at.self_out),
+        rows_of(tokens, height, place).astype(jnp.float32), kept.rows_self, make_keys,
+    )
+    normed[...] = norm_rows(kept.rows_self[...], small.gain_self[...], small.shift_self[...])
+    kept.first_low[place] = normed[...].astype(jnp.bfloat16)
+    share(0, kept.first_low, make_values)
+    save(places.key_cross, places.value_cross, places.rows_self, places.first_low)
+
+    kept.query_cross[...] = dot_nn(
+        kept.first_low[...].reshape(span, width), get(at.cross_query)[...]
+    ).astype(jnp.bfloat16)
+    owners = lax.broadcasted_iota(jnp.int32, (kept.key_cross.shape[0], 1), 0) // MEM
+    attend(
+        kept.query_cross, kept.key_cross, kept.value_cross,
+        lambda here: owners == small.segment_row[:, here], kept.cross_mix, kept.cross_totals,
+    )
+    save(places.query_cross, places.cross_totals, places.cross_mix)
+    join(1, kept.cross_mix, get(at.cross_out), normed[...], kept.rows_cross, None)
+    normed[...] = norm_rows(kept.rows_cross[...], small.gain_cross[...], small.shift_cross[...])
+    kept.second_low[place] = normed[...].astype(jnp.bfloat16)
+    share(1, kept.second_low, None)
+    save(places.rows_cross, places.second_low)
+
+    get(at.feed_up)
+    wide = kept.gelu_slope.shape[2]
+    depth = kept.gelu_slope.shape[1]
+    second = kept.second_low[...].reshape(span, width)
+    for turn in range(kept.feed_act.shape[1] // wide):
+        columns = slice(turn * wide, (turn + 1) * wide)
+        pre = dot_nn(second, get(at.feed_up)[:, columns])
+        chance = 0.5 + 0.5 * lax.erf(pre * 0.5**0.5)
+        kept.feed_act[:, columns] = (pre * chance).astype(jnp.bfloat16)
+        start = turn * span
+        kept.gelu_slope[start // depth, start % depth : start % depth + span] = (
+            chance + pre * jnp.exp(-0.5 * pre * pre) * (0.5 / jnp.pi) ** 0.5
+        )
+    save(places.feed_act, places.gelu_slope)
+    join(2, kept.feed_act, get(at.feed_down), normed[...], kept.rows_feed, None)
+    save(places.rows_feed)
+    states = kept.states
+    low = states.at[block, place]
+    low[...] = norm_rows(
+        kept.rows_feed[...], small.gain_feed[...], small.shift_feed[...]
+    ).astype(jnp.bfloat16)
+    across = flip(place, 2)
+
+    def hop(kind, mask, peer, row, column):
+        here = states.at[row, column]
+        copy = remote(here, here, hops.at[0, kind, mask], hops.at[1, kind, mask], peer)
+        sent.append(copy)
+        return copy
+
+    first, over, ends = {}, {}, {}
+
+    def spread(masks):
+        for mask in masks:
+            first[mask] = hop(0, mask, (flip(block, mask), place), block, place)
+
+    def pass_on(mask):
+        over[mask].wait_recv()
+        ends[mask, 1] = hop(3, mask, near, flip(block, mask), across)
+
+    def arrive(mask):
+        row = flip(block, mask)
+        if mask:
+            first[mask].wait_recv()
+        if mask % 2 == 0:
+            first[mask + 1] = hop(0, mask + 1, beside, row, place)
+        over[mask] = hop(1, mask, far, row, place)
+        ends[mask, 0] = hop(2, mask, near, row, place)
+
+    words = kept.words
+    part = words.shape[0]
+    chunk = chunk_of(part)
+    offset = (place * total + block) * part
+    writes = {}
+
+    def make(mask):
+        row, slot = flip(block, mask), mask % 2
+        for side in (0, 1):
+            ends[mask, side].wait_recv()
+        if mask >= 2:
+            writes[mask - 2].wait()
+        block_states = states[row].reshape(span, width)
+        target = ids_all[row, 1:2] - offset
+
+        def chunk_at(start):
+            scores = product_nt(words[pl.ds(start, chunk), :], block_states)
+            staged[slot, pl.ds(start, chunk), :] = scores
+            ids = start + lax.broadcasted_iota(jnp.int32, (chunk, 1), 0)
+            return (
+                scores,
+                jnp.max(scores, axis=0, keepdims=True),
+                jnp.sum(jnp.where(ids == target, scores, 0.0), axis=0, keepdims=True),
+            )
+
+        def body(turn, carry):
+            top, amount, picked = carry
+            scores, ahead, more = chunk_at(pl.multiple_of(turn * chunk, chunk))
+            ahead = jnp.maximum(top, ahead)
+            return (
+                ahead,
+                amount * jnp.exp(top - ahead)
+                + jnp.sum(jnp.exp(scores - ahead), axis=0, keepdims=True),
+                picked + more,
+            )
+
+        scores, top, picked = chunk_at(0)
+        carry = (top, jnp.sum(jnp.exp(scores - top), axis=0, keepdims=True), picked)
+        carry = lax.fori_loop(1, part // chunk, body, carry)
+        for index in range(3):
+            sends[0, index, pl.ds(row, 1), :] = carry[index]
+        writes[mask] = pltpu.make_async_copy(
+            staged.at[slot], logits.at[row], staged_sems.at[slot]
+        )
+        writes[mask].start()
+
+    spread([2])
+    nearest = len(sent) - 1
+    lag = 3
+    for step in range(total + lag):
+        if step < total:
+            arrive(step)
+        if step == 0:
+            del sent[nearest]
+            first[2].wait_send()
+            spread(range(4, total, 2))
+        if 2 <= step < total + 2:
+            pass_on(step - 2)
+        if step == lag:
+            finish(ids_copies)
+            finish(moved)
+            save(places.words)
+        if step >= lag:
+            make(step - lag)
+    save(places.states)
+
+    peers = [(near, lax.rem(place, 2)), (far, lax.div(place, 2))]
+    for bit in range(bits):
+        step = 1 << bit
+        peers.append(((flip(block, step), place), lax.rem(lax.div(block, step), 2)))
+    for stage, (peer, side) in enumerate(peers):
+        copy = remote(
+            sends.at[stage], recvs.at[stage], stage_sems.at[0, stage], stage_sems.at[1, stage],
+            peer,
+        )
+        copy.wait_recv()
+        sent.append(copy)
+        mine = [sends[stage, index] for index in range(3)]
+        theirs = [recvs[stage, index] for index in range(3)]
+        leading = side == 0
+        soon = [jnp.where(leading, one, other) for one, other in zip(mine, theirs)]
+        later = [jnp.where(leading, other, one) for one, other in zip(mine, theirs)]
+        top = jnp.maximum(soon[0], later[0])
+        values = [
+            top,
+            soon[1] * jnp.exp(soon[0] - top) + later[1] * jnp.exp(later[0] - top),
+            soon[2] + later[2],
+        ]
+        for index in range(3):
+            if stage + 1 < len(peers):
+                sends[stage + 1, index] = values[index]
+            else:
+                totals[index] = values[index]
+    for mask in range(total - 2, total):
+        writes[mask].wait()
+    for copy in sent:
+        copy.wait_send()
+    for copy in saves:
+        copy.wait()
+
+
+def layer_forward(given, small, table, number):
+    total = lax.axis_size("dp")
+    rows, width = given.tokens.shape
+    span = given.memory.shape[0]
+    part = given.self_query.shape[1]
+    hidden = given.feed_up.shape[1]
+    height = rows // QUARTERS
+    words = table.shape[0] // total
+    stages = 2 + (total - 1).bit_length()
+    heads = part // HEAD_DIM
+
+    def low(*shape):
+        return jax.ShapeDtypeStruct(shape, jnp.bfloat16)
+
+    def full(*shape):
+        return jax.ShapeDtypeStruct(shape, jnp.float32)
+
+    kept = Kept(
+        query_self=low(rows, part),
+        key_self=low(rows, part),
+        value_self=low(rows, part),
+        self_totals=full(heads, rows),
+        self_mix=low(rows, part),
+        first_low=low(QUARTERS, height, width),
+        rows_self=full(height, width),
+        key_cross=low(span, part),
+        value_cross=low(span, part),
+        query_cross=low(rows, part),
+        cross_totals=full(heads, rows),
+        cross_mix=low(rows, part),
+        second_low=low(QUARTERS, height, width),
+        rows_cross=full(height, width),
+        feed_act=low(rows, hidden),
+        gelu_slope=full(rows * hidden // (width * part), width, part),
+        rows_feed=full(height, width),
+        words=low(words, width),
+        states=low(total, QUARTERS, height, width),
+    )
+    out_shape = list(kept) + [
+        full(total, words, rows),
+        full(3, total, rows),
+        jax.ShapeDtypeStruct((total,) + small.ids.shape, small.ids.dtype),
+    ]
+    outcome = pl.pallas_call(
+        functools.partial(layer_kernel, total),
+        out_shape=out_shape,
+        in_specs=[ANY] * len(given) + [VMEM] * len(small) + [ANY],
+        out_specs=[ANY] * len(kept) + [ANY, VMEM, VMEM],
+        scratch_shapes=[pltpu.VMEM(value.shape, value.dtype) for value in given]
+        + [pltpu.VMEM(value.shape, value.dtype) for value in kept]
+        + [DMA((len(given),)), DMA((len(kept),)), DMA((2, total)), DMA, DMA((2, total))]
+        + exchange_scratch(height, width) * 3
+        + [
+            pltpu.VMEM((height, width), jnp.float32),
+            DMA((2, 4, total)),
+            pltpu.VMEM((2, words, rows), jnp.float32),
+            pltpu.VMEM((stages, 3, total, rows), jnp.float32),
+            pltpu.VMEM((stages, 3, total, rows), jnp.float32),
+            DMA((2,)),
+            DMA((2, stages)),
+        ],
+        compiler_params=pltpu.CompilerParams(
+            collective_id=number, has_side_effects=True, vmem_limit_bytes=62 * 2**20
+        ),
+    )(*given, *small, table)
+    return (Kept(*outcome[: len(kept)]),) + tuple(outcome[len(kept) :])
 
 
 class Loaded(typing.NamedTuple):
@@ -1340,6 +1761,53 @@
     return whole
 
 
+def layer_apart(
+    tokens, memory, segment_ids, ids, offset, words, self_query, self_key, self_value, self_out,
+    cross_query, cross_key, cross_value, cross_out, feed_up, feed_down, gain_self, shift_self,
+    gain_cross, shift_cross, gain_feed, shift_feed,
+):
+    row_len = segment_ids.shape[1]
+    places = jnp.arange(row_len, dtype=jnp.int32)
+    owners = jnp.arange(memory.shape[0], dtype=jnp.int32) // MEM
+    self_mask = (segment_ids[0][:, None] == segment_ids[0][None, :]) & (
+        places[None, :] <= places[:, None]
+    )
+    cross_mask = segment_ids[0][:, None] == owners[None, :]
+    quarter = tokens.shape[0] // QUARTERS
+    inputs = lax.dynamic_slice_in_dim(tokens, lax.axis_index("mp") * quarter, quarter, 0)
+    query_self = product(tokens, self_query).astype(jnp.bfloat16)
+    key_self = product(tokens, self_key).astype(jnp.bfloat16)
+    value_self = product(tokens, self_value).astype(jnp.bfloat16)
+    self_mix, self_totals = attend_forward(query_self, key_self, value_self, self_mask)
+    first_low, first_norm, rows_self, ids_all = mix_norm(
+        self_mix, self_out, inputs, gain_self, shift_self, 0, ids
+    )
+    query_cross = product(first_low, cross_query).astype(jnp.bfloat16)
+    key_cross = product(memory, cross_key).astype(jnp.bfloat16)
+    value_cross = product(memory, cross_value).astype(jnp.bfloat16)
+    cross_mix, cross_totals = attend_forward(query_cross, key_cross, value_cross, cross_mask)
+    second_low, second_norm, rows_cross = mix_norm(
+        cross_mix, cross_out, first_norm, gain_cross, shift_cross, 1
+    )
+    feed_pre = product(second_low, feed_up)
+    feed_act, gelu_pull = jax.vjp(gelu_exact, feed_pre)
+    gelu_slope = gelu_pull(jnp.ones_like(feed_pre))[0]
+    feed_act = feed_act.astype(jnp.bfloat16)
+    answers = ids_all[:, ids.shape[0] // 3 : 2 * (ids.shape[0] // 3)].reshape(-1, 1, row_len)
+    states, rows_feed, logits, totals = feed_norm(
+        feed_act, feed_down, second_norm, gain_feed, shift_feed, answers - offset, 2, words
+    )
+    gelu_slope = jnp.concatenate(
+        jnp.split(gelu_slope, gelu_slope.shape[1] // self_query.shape[1], axis=1), axis=0
+    ).reshape((2,) + self_query.shape)
+    kept = Kept(
+        query_self, key_self, value_self, self_totals, self_mix, first_low, rows_self, key_cross,
+        value_cross, query_cross, cross_totals, cross_mix, second_low, rows_cross, feed_act,
+        gelu_slope, rows_feed, words, states,
+    )
+    return kept, logits, totals, ids_all
+
+
 def local(
     tokens,
     memory,
@@ -1369,64 +1837,36 @@
     row_count, row_len = segment_ids.shape
     total = lax.axis_size("dp")
     direct = total == 8 and embedding.shape[1] % 128 == 0
-    last = None
+    vocab_local = embedding.shape[0]
+    part = vocab_local // total
+    offset = lax.axis_index("mp") * vocab_local + lax.axis_index("dp") * part
+    ids = jnp.concatenate([segment_ids, answer_ids, loss_mask], axis=0)
+    norms = (gain_self, shift_self, gain_cross, shift_cross, gain_feed, shift_feed)
     if direct:
-        part = embedding.shape[0] // total
-        last = lax.ppermute(
-            lax.dynamic_slice_in_dim(
-                embedding, (total - 1 - lax.axis_index("dp")) * part, part, 0
+        kept, logits, totals, ids_all = layer_forward(
+            Given(
+                tokens, self_query, self_key, self_value, self_out, memory, cross_key,
+                cross_value, cross_query, cross_out, feed_up, feed_down,
             ),
-            "dp",
-            [(index, total - 1 - index) for index in range(total)],
-        )
-    span = SEG_ROW * MEM
-    quarter = tokens.shape[0] // QUARTERS
-    inputs = lax.dynamic_slice_in_dim(tokens, lax.axis_index("mp") * quarter, quarter, 0)
-    places = jnp.arange(row_len, dtype=jnp.int32)
-    owners = jnp.arange(span, dtype=jnp.int32) // MEM
-    self_masks = [
-        (segment_ids[0][:, None] == segment_ids[0][None, :]) & (places[None, :] <= places[:, None])
-    ]
-    cross_masks = [segment_ids[0][:, None] == owners[None, :]]
-    query_self = product(tokens, self_query).astype(jnp.bfloat16)
-    key_self = product(tokens, self_key).astype(jnp.bfloat16)
-    value_self = product(tokens, self_value).astype(jnp.bfloat16)
-    self_mix, self_totals = run_rows(query_self, key_self, value_self, self_masks)
-    first_low, first_norm, rows_self, ids_all, *wide = mix_norm(
-        self_mix, self_out, inputs, gain_self, shift_self, 0,
-        jnp.concatenate([segment_ids, answer_ids, loss_mask], axis=0),
-        embedding, None, (4, 1, 0) if direct else (),
-    )
+            Small(
+                ids, segment_ids.reshape(1, -1), segment_ids.reshape(-1, 1),
+                *(vector.reshape(1, -1) for vector in norms),
+            ),
+            embedding,
+            0,
+        )
+        words = kept.words
+    else:
+        words = spread_rows(embedding)
+        kept, logits, totals, ids_all = layer_apart(
+            tokens, memory, segment_ids, ids, offset, words, self_query, self_key, self_value,
+            self_out, cross_query, cross_key, cross_value, cross_out, feed_up, feed_down, *norms,
+        )
     segments_all, answers_all, kept_all = (
         ids_all[:, kind * row_count : (kind + 1) * row_count].reshape(-1, row_len)
         for kind in range(3)
     )
-    query_cross = product(first_low, cross_query).astype(jnp.bfloat16)
-    key_cross = product(memory, cross_key).astype(jnp.bfloat16)
-    value_cross = product(memory, cross_value).astype(jnp.bfloat16)
-    cross_mix, cross_totals = run_rows(query_cross, key_cross, value_cross, cross_masks)
-    second_low, second_norm, rows_cross, *wide = mix_norm(
-        cross_mix, cross_out, first_norm, gain_cross, shift_cross, 1, None,
-        embedding, *wide, masks=(5, 2) if direct else (),
-    )
-    feed_pre = product(second_low, feed_up)
-    feed_act, gelu_pull = jax.vjp(gelu_exact, feed_pre)
-    gelu_slope = gelu_pull(jnp.ones_like(feed_pre))[0]
-    feed_act = feed_act.astype(jnp.bfloat16)
-    vocab_local = embedding.shape[0]
-    part = vocab_local // total
-    offset = lax.axis_index("mp") * vocab_local + lax.axis_index("dp") * part
     targets = (answers_all - offset)[:, None, :]
-    table = embedding if direct else spread_rows(embedding)
-    states, rows_feed, logits, totals, *wide = feed_norm(
-        feed_act, feed_down, second_norm, gain_feed, shift_feed, targets, 2,
-        table, *wide, last=last, early=(6, 3) if direct else (),
-    )
-    if direct:
-        spot = (total - 1 - lax.axis_index("dp")) * last.shape[1]
-        table_rows = lax.dynamic_update_slice_in_dim(wide[0], last, spot, 1)
-    else:
-        table_rows = table
     log_total = totals[0] + jnp.log(totals[1])
     picked = totals[2]
     keeper = kept_all.astype(jnp.float32)
@@ -1453,50 +1893,48 @@
     grad_logp = (jnp.sum(seg_hot * per_segment[:, None, :], axis=2) * keeper)[:, None, :]
     log_total = log_total[:, None, :]
     if direct:
-        head_values = (logits, table_rows, states, log_total, grad_logp, targets)
+        head_values = (logits, words, kept.states, log_total, grad_logp, targets)
     else:
         hot = (targets == jnp.arange(part, dtype=jnp.int32)[None, :, None]).astype(jnp.float32)
         grad_logits = (grad_logp * (hot - jnp.exp(logits - log_total))).astype(jnp.bfloat16)
         parts = jnp.einsum(
-            "rvt,vd->rtd", grad_logits, table_rows, preferred_element_type=jnp.float32
+            "rvt,vd->rtd", grad_logits, words, preferred_element_type=jnp.float32
         ).astype(jnp.bfloat16)
-        head_values = (parts.reshape(states.shape),)
+        head_values = (parts.reshape(kept.states.shape),)
         grad_words = jnp.einsum(
             "rvt,rtd->vd",
             grad_logits,
-            states.reshape(total, -1, states.shape[3]),
+            kept.states.reshape(total, -1, kept.states.shape[3]),
             preferred_element_type=jnp.float32,
         ).astype(jnp.bfloat16)
-    grad_branch, grad_res3, grad_vecs_feed, *words = head_back(
-        head_values, rows_feed, gain_feed, 3, (4, 1, 0) if direct else ()
-    )
-    grad_words, *narrow = words if direct else (grad_words,)
+    grad_branch, grad_res3, grad_vecs_feed, *made = head_back(
+        head_values, kept.rows_feed, gain_feed, 3, (4, 1, 0) if direct else ()
+    )
+    grad_words, *narrow = made if direct else (grad_words,)
     values = Loaded(
         grad_out=grad_branch,
         feed_down=feed_down,
-        gelu_slope=jnp.concatenate(
-            jnp.split(gelu_slope, gelu_slope.shape[1] // self_query.shape[1], axis=1), axis=0
-        ).reshape((2,) + self_query.shape),
+        gelu_slope=kept.gelu_slope,
         feed_up=feed_up,
-        feed_act=feed_act,
-        second_low=second_low,
+        feed_act=kept.feed_act,
+        second_low=kept.second_low.reshape(tokens.shape),
         cross_out=cross_out,
         cross_query=cross_query,
-        query_cross=query_cross,
-        key_cross=key_cross,
-        value_cross=value_cross,
-        cross_totals=cross_totals[0][..., 0],
-        cross_mix=cross_mix,
-        first_low=first_low,
+        query_cross=kept.query_cross,
+        key_cross=kept.key_cross,
+        value_cross=kept.value_cross,
+        cross_totals=kept.cross_totals,
+        cross_mix=kept.cross_mix,
+        first_low=kept.first_low.reshape(tokens.shape),
         memory=memory,
         cross_key=cross_key,
         cross_value=cross_value,
         self_out=self_out,
-        query_self=query_self,
-        key_self=key_self,
-        value_self=value_self,
-        self_totals=self_totals[0][..., 0],
-        self_mix=self_mix,
+        query_self=kept.query_self,
+        key_self=kept.key_self,
+        value_self=kept.value_self,
+        self_totals=kept.self_totals,
+        self_mix=kept.self_mix,
         tokens=tokens,
         self_query=self_query,
         self_key=self_key,
@@ -1504,9 +1942,9 @@
     )
     plain = Plain(
         grad_rows=grad_res3,
-        rows_cross=rows_cross,
+        rows_cross=kept.rows_cross,
         gain_cross=gain_cross.reshape(1, -1),
-        rows_self=rows_self,
+        rows_self=kept.rows_self,
         gain_self=gain_self.reshape(1, -1),
         grad_vecs=grad_vecs_feed,
         segment_row=segment_ids.reshape(1, -1),

time: 557 us -> 508 us (0.912)
  matrix products: 23.6 us -> 0.67 us
  other arithmetic: 32.3 us -> 22.9 us
  local copies, waits for them, and re-layouts: 15.1 us -> 8.55 us
  Pallas kernels: 472 us -> 466 us
  starting transfers between devices: 5.98 us -> 0 us
    dot_general x11 -> x0, matrix products: 23 us -> none  [the longest x7 16.1 us: product(): return jnp.dot(left_side, right_side, preferred_element_type=jnp.float32)]
    ppermute x1 -> x0, starting transfers between devices: 5.98 us -> none  [local(): lax.ppermute(lax.dynamic_slice_in_dim(embedding, (total - 1 - lax.axis_in...]
    pallas_call x3 -> x1, Pallas kernels: 146 us -> 143 us  [layer_forward(): pl.pallas_call(functools.partial(layer_kernel, total), out_shape=out_shap...]
  transfers between devices with their start and end apart: 1 -> 0, of which waited for: 0 -> 0; matrix products, arithmetic and copies ran while one was open for 7% -> 0% of each run, Pallas kernels for 9% -> 0%
where the time goes in v5:
time: 508 us; the launch traced here: 501 us
  Pallas kernels  466 us (92%)
  other arithmetic  22.9 us (5%)
  local copies, waits for them, and re-layouts  8.55 us (2%)
    pallas_call x1, Pallas kernels, layer_back(): pl.pallas_call(functools.partial(layer_back_kernel, total, orders, tuple(...  239 us
    pallas_call x1, Pallas kernels, layer_forward(): pl.pallas_call(functools.partial(layer_kernel, total), out_shape=out_shap...  143 us
    pallas_call x1, Pallas kernels, head_back(): pl.pallas_call(functools.partial(head_back_kernel, total, tuple(masks), i...  83.8 us

profile of v5, /device:TPU:0, one launch (start us, length us, event | category | flops | bytes accessed | tf_op | source)
XLA Modules:
  0.0 501.0 jit_solution(10993522352220395077)
XLA Ops:
  0.7 0.7 reduce_max.19
  1.4 0.7 exponential_reduce_fusion
  2.1 1.3 pad_add_fusion.refs_12_
  3.4 0.7 eq.68
  4.2 1.5 copy.54.refs_14_.refs_34_
  5.8 143.2 %shard_map.391 = (bf16[512,256]{1,0:T(8,128)(2,1)}, bf16[512,256]{1,0:T(8,128)(2,1)}, bf16[512,256]{1,0:T(8,128)(2,1)}, f32[4,512]{1,0:T(4,128)}, bf16[512,256]{...) custom-call(bf16[512,1024]{1,0:T(8,128)(2,1)} %refs_23_.1, ...), custom_call_target="tpu_custom_call" | custom-call | tf_op jit(solution)/shard_map/pallas_call | solution.py:1261
  149.0 0.7 fusion.8
  149.7 0.6 copy.56.refs_5_
  150.4 1.6 slice_subtract_fusion
  152.0 0.8 bitcast_multiply_fusion
  153.3 0.6 fusion.11
  154.6 0.6 multiply_add_fusion.1
  155.9 1.5 reshape_multiply_fusion.refs_6_
  157.4 83.8 %shard_map.392 = (bf16[4,128,1024]{2,1,0:T(8,128)(2,1)}, f32[128,1024]{1,0:T(8,128)}, f32[2,1024]{1,0:T(2,128)}, bf16[1600,1024]{1,0:T(8,128)(2,1)}, bf16[12800,128]{1,0:T(8,128)(2,1)}) custom-call(f32[8,1600,512]{2,1,0:T(8,128)} %get-tuple-element.55.refs_0_, f32[128,1024]{1,0:T(8,128)} %get-tuple-element.56.refs_1_, f32[1,1024]{1,0:T(1,128)} %bitcast.100, ...), custom_call_target="tpu_custom_call" | custom-call | tf_op jit(solution)/shard_map/pallas_call | solution.py:811
  241.2 238.9 %shard_map.393 = (bf16[16,1024,256]{2,1,0:T(8,128)(2,1)}, f32[6,1024]{1,0:T(8,128)}, f32[512,256]{1,0:T(8,128)}, f32[1024,256]{1,0:T(8,128)}, bf16[12800,128]{1,0:T(8,128)(2,1)}) custom-call(bf16[512,1024]{1,0:T(8,128)(2,1)} %bitcast.90, bf16[1024,1024]{1,0:T(8,128)(2,1)} %refs_1_.3, ...), custom_call_target="tpu_custom_call", output_to_operand_aliasing={{4}: (36, {})} | custom-call | tf_op jit(solution)/shard_map/pallas_call | solution.py:1709
  480.1 1.7 fusion.16
  481.8 5.1 %convert_element_type.119 = f32[12800,128]{1,0:T(8,128)} convert(bf16[12800,128]{1,0:T(8,128)(2,1)} %get-tuple-element.84) | non-fusion elementwise | flops 1638400 | bytes 9830400 | tf_op jit(solution)/shard_map/convert_element_type | solution.py:1958
  486.9 1.6 copy-done
  488.6 2.8 slice_bitcast_fusion.3
  491.6 1.1 pad_maximum_fusion.1
  492.7 1.1 pad_maximum_fusion
  493.8 3.9 maximum_convert_fusion
  497.7 0.8 copy.71
  498.5 1.0 copy.72
  (29 shorter events, 1.6 us)
Async XLA Ops:
  5.8 147.5 %copy-start.3 = (f32[16,4]{0,1:T(4,128)S(1)}, f32[16,4]{0,1:T(4,128)}, u32[]{:S(2)}) copy-start(f32[16,4]{0,1:T(4,128)} %param.29) | copy-start | bytes 772
  5.8 149.6 %copy-start.4 = (s32[64]{0:T(128)S(1)}, s32[64]{0:T(128)}, u32[]{:S(2)}) copy-start(s32[64]{0:T(128)} %param.30) | copy-start | bytes 772
  481.8 6.7 %copy-start = (bf16[16,1024,256]{2,1,0:T(8,128)(2,1)S(1)}, bf16[16,1024,256]{2,1,0:T(8,128)(2,1)}, u32[]{:S(2)}) copy-start(bf16[16,1024,256]{2,1,0:T(8,128)(2,1)} %get-tuple-element.82) | copy-start | bytes 25165828
  493.7 3.9 copy-start.2
  493.8 4.7 copy-start.1

commit v6 on v5

--- a/solution.py
+++ b/solution.py
@@ -101,23 +101,25 @@
     place, block_of, near, far, sib_send, sib_recv, far_send, far_recv, sems, outcome, sent
 ):
     copies = []
+    sends, recvs = (
+        slots if isinstance(slots, list) else [slots.at[0], slots.at[1]]
+        for slots in (sib_send, sib_recv)
+    )
     for slot, mask in enumerate((3, 1)):
-        sib_send[slot] = block_of(flip(place, mask)).astype(jnp.bfloat16)
+        sends[slot][...] = block_of(flip(place, mask)).astype(jnp.bfloat16)
         copies.append(
-            remote(
-                sib_send.at[slot], sib_recv.at[slot], sems.at[0, slot], sems.at[1, slot], near
-            )
+            remote(sends[slot], recvs[slot], sems.at[0, slot], sems.at[1, slot], near)
         )
     distant = block_of(flip(place, 2))
     copies[0].wait_recv()
-    far_send[...] = (distant + sib_recv[0].astype(jnp.float32)).astype(jnp.bfloat16)
+    far_send[...] = (distant + recvs[0][...].astype(jnp.float32)).astype(jnp.bfloat16)
     copies.append(remote(far_send, far_recv, sems.at[0, 2], sems.at[1, 2], far))
     sent += copies
     own = block_of(place)
     copies[1].wait_recv()
     yield
     copies[2].wait_recv()
-    outcome.append(own + sib_recv[1].astype(jnp.float32) + far_recv[...].astype(jnp.float32))
+    outcome.append(own + recvs[1][...].astype(jnp.float32) + far_recv[...].astype(jnp.float32))
 
 
 def share_quarter_steps(place, quarters, near, far, sems, sent):
@@ -598,6 +600,7 @@
             loads[step, None].start()
 
         load(0)
+        load_states(0)
     else:
         for mask in order:
             row = flip(block, mask)
@@ -620,8 +623,6 @@
             return
         if step + 1 < len(order):
             load(step + 1)
-        elif masks or fused:
-            load_states(0)
         loads[step].wait()
         row, slot = flip(block, mask), step % 2
         target, log_total, scale = targets[row], log_totals[row], grad_logp[row]
@@ -725,7 +726,6 @@
     outcome = None
     count = len(order)
     make(0)
-    rows_made = 0
     for step in range(count + 2):
         if step + 1 < count:
             make(step + 1)
@@ -737,16 +737,10 @@
                 to_beside(mask)
             else:
                 outcome = to_end(mask)
-        if fused and step + 2 >= count:
-            for _ in range(2):
-                make_rows(rows_made)
-                rows_made += 1
-    if fused:
-        while rows_made < count:
-            make_rows(rows_made)
-            rows_made += 1
-        if masks:
-            moved = table_copies(masks, True, table[0], narrow[0], move_sems)
+        if fused and 1 <= step <= count:
+            make_rows(step - 1)
+            if masks and step == count:
+                moved = table_copies(masks, True, table[0], narrow[0], move_sems)
     for mask in range(total - 2, 0, -2):
         ends[mask].wait_recv()
         outcome = outcome + end_recv[mask // 2].astype(jnp.float32)
@@ -1326,9 +1320,47 @@
 
 LOADS = len(Loaded._fields)
 PIECES = 16
-
-
-def layer_back_kernel(total, orders, moves, *refs):
+CROSSWISE = (8, 11)
+PLANS = (
+    (
+        0, 6,
+    ),
+    (
+        1, 7, 12, 18, 48,
+    ),
+    (
+        2, 24, 8, 13, 30, 66,
+    ),
+    (
+        3, 19, 25, 36,
+    ),
+    (
+        9, 42, 14, 31, 54, 4, 20, 60, 26, 37, 49, 10, 67, 43, 15, 72, 32, 55, 21, 61, 78, 27,
+        16, 38, 84, 50, 68, 73, 90, 44, 22, 33, 5, 56, 62, 79, 11, 28, 39, 17, 85, 51, 23, 69,
+        91, 74, 29, 34, 45, 52, 57, 70, 40, 63, 80, 35, 46, 86, 92, 41, 75, 53, 47, 58, 71, 59,
+        64, 81, 76, 87, 65, 93, 82, 88, 77, 94, 83, 89, 95,
+    ),
+)
+
+
+def plans_of(bits):
+    turns = 2 * bits
+    if turns == 6:
+        return [[divmod(code, turns) for code in plan] for plan in PLANS]
+    feed, rest = range(0, 8), range(8, PIECES)
+    plans = [
+        [(piece, 0) for piece in feed],
+        [(piece, 1) for piece in feed],
+        [],
+        [(piece, 0) for piece in range(8, 12)],
+    ]
+    plans.append([(piece, 0) for piece in range(12, PIECES)])
+    plans[4] += [(piece, 1) for piece in rest]
+    plans[4] += [(piece, turn) for turn in range(2, turns) for piece in range(PIECES)]
+    return plans
+
+
+def layer_back_kernel(total, orders, plans, moves, *refs):
     given_hbm, plain, table, outs, narrow, held, refs = split_refs(
         refs, LOADS, len(Plain._fields), 2 * bool(moves), 4, bool(moves), LOADS, len(refs)
     )
@@ -1338,9 +1370,15 @@
     norm_buffers = [refs[0:5], refs[5:10]]
     quarters, refs = refs[10:12], refs[12:]
     rows_all = quarters[0].shape[0] * quarters[0].shape[1]
+    down, up = held[1], held[3]
+    part = pieces.shape[2]
     column_buffers = [
-        [pieces.at[0:2], pieces.at[2:4]] + refs[0:3],
-        [pieces.at[4:6, 0:rows_all], pieces.at[6:8, 0:rows_all]] + refs[3:6],
+        [
+            [weight.at[0:size, turn * part : (turn + 1) * part] for turn in pair]
+            for pair in ((0, 1), (2, 3))
+        ]
+        + refs[start : start + 3]
+        for weight, size, start in ((down, pieces.shape[1], 0), (up, rows_all, 3))
     ]
     refs = refs[6:]
     grad_pre, grad_mix, grad_queries, grad_cross, grad_self = refs[:5]
@@ -1394,8 +1432,7 @@
             sum_sems.at[1, piece, stage],
             over[orders[piece][stage]],
         )
-        if stage or piece >= 8:
-            sent.append(copies[piece, stage])
+        sent.append(copies[piece, stage])
 
     def take_sum(piece, stage):
         side, rows = sides[orders[piece][stage]], height >> (stage + 1)
@@ -1427,15 +1464,15 @@
         )
         sent.append(copies[piece, stage, True])
 
-    def pump(group, turn):
-        for piece in group:
+    def move_on(plan):
+        for piece, turn in plan:
             if turn < bits:
                 take_sum(piece, turn)
-            else:
-                stage = 2 * bits - 1 - turn
-                copies[piece, stage, True].wait_recv()
-                if stage:
-                    send_whole(piece, stage - 1)
+                continue
+            stage = 2 * bits - 1 - turn
+            copies[piece, stage, True].wait_recv()
+            if stage:
+                send_whole(piece, stage - 1)
 
     def weight_piece(piece, left, right):
         pieces[piece] = product_tn(left, right).astype(jnp.bfloat16)
@@ -1530,9 +1567,7 @@
         lambda here: owners == simple.segment_row[:, here],
         acc_keys, acc_values, grad_queries, grad_cross.at[0], grad_cross.at[1],
     )
-    pump(range(0, 8), 0)
-    for piece in range(8):
-        copies[piece, 0].wait_send()
+    move_on(plans[0])
     for index in (at.cross_query, at.cross_mix, at.first_low, at.memory, at.cross_key, at.cross_value):
         get(index)
     for kind in range(2):
@@ -1587,7 +1622,7 @@
     )
 
     grad_out = quarters[1]
-    pump(range(0, 8), 1)
+    move_on(plans[1])
     for index in range(QUARTERS):
         grad_mix[index * quarter : (index + 1) * quarter] = product_nt(
             grad_out[index], get(at.self_out)[...]
@@ -1608,13 +1643,13 @@
     )
     for index in (at.tokens, at.self_mix, at.self_query, at.self_key, at.self_value):
         get(index)
+    move_on(plans[2])
     weight_piece(12, get(at.tokens)[...], grad_queries[...])
     weight_piece(13, get(at.tokens)[...], grad_self[0])
     weight_piece(14, get(at.tokens)[...], grad_self[1])
     folded_piece(15, get(at.self_mix), grad_out[...].reshape(rows_all, grad_out.shape[2]))
-    pump(range(8, 12), 0)
+    move_on(plans[3])
     vec_next(0)
-    pump(range(0, 8), 2)
 
     def token_block(index):
         return (
@@ -1629,29 +1664,21 @@
     )
     next(token_steps)
     next(memory_steps)
-    pump(range(12, 16), 0)
-    vec_next(1)
-    pump(range(8, 12), 1)
-    run(token_steps)
     own_columns = pl.ds(pl.multiple_of(place * wide, wide), wide)
-    token_share[...] = token_total[0] + quarters[1][:, :, own_columns].reshape(
-        rows_all, wide
-    ).astype(jnp.float32)
-    pump(range(0, 8), 3)
-    vec_next(2)
-    run(memory_steps)
-    memory_share[...] = memory_total[0]
-    groups = [(range(0, 8), 4), (range(8, 12), 2), (range(12, 16), 1)]
-    stage = 3
-    while groups:
-        for group, turn in groups:
-            pump(group, turn)
-        vec_next(stage)
-        stage += 1
-        groups = [(group, turn + 1) for group, turn in groups if turn + 1 < 2 * bits]
-    while stage < len(vec_peers):
-        vec_next(stage)
-        stage += 1
+    step = 12
+    for turn, start in enumerate(range(0, len(plans[4]), step)):
+        move_on(plans[4][start : start + step])
+        if turn == 0:
+            run(token_steps)
+            token_share[...] = token_total[0] + quarters[1][:, :, own_columns].reshape(
+                rows_all, wide
+            ).astype(jnp.float32)
+        if turn == 1:
+            run(memory_steps)
+            memory_share[...] = memory_total[0]
+        vec_next(turn + 1)
+    for turn in range(-(-len(plans[4]) // step) + 1, len(vec_peers)):
+        vec_next(turn)
     for copy in sent:
         copy.wait_send()
     finish(moved)
@@ -1661,7 +1688,7 @@
     total = lax.axis_size("dp")
     bits = (total - 1).bit_length()
     rest = list(range(2, bits))
-    orders = [[0, 1] + rest if piece % 4 else [1, 0] + rest for piece in range(PIECES)]
+    orders = [[1, 0] + rest if piece in CROSSWISE else [0, 1] + rest for piece in range(PIECES)]
     given = list(values) + list(plain)
     in_specs = [ANY] * len(values) + [VMEM] * len(plain)
     rows, width = values.tokens.shape
@@ -1707,7 +1734,7 @@
         out_specs.append(ANY)
         scratch.append(DMA((2, len(moves))))
     return pl.pallas_call(
-        functools.partial(layer_back_kernel, total, orders, tuple(moves)),
+        functools.partial(layer_back_kernel, total, orders, plans_of(bits), tuple(moves)),
         out_shape=out_shape,
         in_specs=in_specs,
         out_specs=out_specs,

time: 508 us -> 487 us (0.959)
  Pallas kernels: 466 us -> 445 us
    pallas_call x1, Pallas kernels: 239 us -> 222 us  [layer_back(): pl.pallas_call(functools.partial(layer_back_kernel, total, orders, plans_...]
where the time goes in v6:
time: 487 us; the launch traced here: 480 us
  Pallas kernels  445 us (91%)
  other arithmetic  22.9 us (5%)
  local copies, waits for them, and re-layouts  8.55 us (2%)
    pallas_call x1, Pallas kernels, layer_back(): pl.pallas_call(functools.partial(layer_back_kernel, total, orders, plans_...  222 us
    pallas_call x1, Pallas kernels, layer_forward(): pl.pallas_call(functools.partial(layer_kernel, total), out_shape=out_shap...  143 us
    pallas_call x1, Pallas kernels, head_back(): pl.pallas_call(functools.partial(head_back_kernel, total, tuple(masks), i...  80.2 us

profile of v6, /device:TPU:0, one launch (start us, length us, event | category | flops | bytes accessed | tf_op | source)
XLA Modules:
  0.0 480.2 jit_solution(852243190343816287)
XLA Ops:
  0.7 0.7 reduce_max.19
  1.4 0.7 exponential_reduce_fusion
  2.1 1.3 pad_add_fusion.refs_12_
  3.4 0.7 eq.68
  4.2 1.5 copy.54.refs_14_.refs_34_
  5.8 143.2 %shard_map.391 = (bf16[512,256]{1,0:T(8,128)(2,1)}, bf16[512,256]{1,0:T(8,128)(2,1)}, bf16[512,256]{1,0:T(8,128)(2,1)}, f32[4,512]{1,0:T(4,128)}, bf16[512,256]{...) custom-call(bf16[512,1024]{1,0:T(8,128)(2,1)} %refs_23_.1, ...), custom_call_target="tpu_custom_call" | custom-call | tf_op jit(solution)/shard_map/pallas_call | solution.py:1255
  149.0 0.7 fusion.8
  149.7 0.6 copy.56.refs_5_
  150.4 1.6 slice_subtract_fusion
  152.0 0.8 bitcast_multiply_fusion
  153.3 0.6 fusion.11
  154.6 0.6 multiply_add_fusion.1
  155.9 1.5 reshape_multiply_fusion.refs_6_
  157.4 80.2 %shard_map.392 = (bf16[4,128,1024]{2,1,0:T(8,128)(2,1)}, f32[128,1024]{1,0:T(8,128)}, f32[2,1024]{1,0:T(2,128)}, bf16[1600,1024]{1,0:T(8,128)(2,1)}, bf16[12800,128]{1,0:T(8,128)(2,1)}) custom-call(f32[8,1600,512]{2,1,0:T(8,128)} %get-tuple-element.55.refs_0_, f32[128,1024]{1,0:T(8,128)} %get-tuple-element.56.refs_1_, f32[1,1024]{1,0:T(1,128)} %bitcast.100, ...), custom_call_target="tpu_custom_call" | custom-call | tf_op jit(solution)/shard_map/pallas_call | solution.py:805
  237.6 221.6 %shard_map.393 = (bf16[16,1024,256]{2,1,0:T(8,128)(2,1)}, f32[6,1024]{1,0:T(8,128)}, f32[512,256]{1,0:T(8,128)}, f32[1024,256]{1,0:T(8,128)}, bf16[12800,128]{1,0:T(8,128)(2,1)}) custom-call(bf16[512,1024]{1,0:T(8,128)(2,1)} %bitcast.90, bf16[1024,1024]{1,0:T(8,128)(2,1)} %refs_1_.3, ...), custom_call_target="tpu_custom_call", output_to_operand_aliasing={{4}: (36, {})} | custom-call | tf_op jit(solution)/shard_map/pallas_call | solution.py:1736
  459.3 1.7 fusion.16
  461.0 5.1 %convert_element_type.119 = f32[12800,128]{1,0:T(8,128)} convert(bf16[12800,128]{1,0:T(8,128)(2,1)} %get-tuple-element.84) | non-fusion elementwise | flops 1638400 | bytes 9830400 | tf_op jit(solution)/shard_map/convert_element_type | solution.py:1985
  466.1 1.6 copy-done
  467.7 2.8 slice_bitcast_fusion.3
  470.7 1.1 pad_maximum_fusion.1
  471.8 1.1 pad_maximum_fusion
  472.9 3.9 maximum_convert_fusion
  476.8 0.8 copy.71
  477.6 1.0 copy.72
  (29 shorter events, 1.6 us)
Async XLA Ops:
  5.8 147.5 %copy-start.3 = (f32[16,4]{0,1:T(4,128)S(1)}, f32[16,4]{0,1:T(4,128)}, u32[]{:S(2)}) copy-start(f32[16,4]{0,1:T(4,128)} %param.29) | copy-start | bytes 772
  5.8 149.6 %copy-start.4 = (s32[64]{0:T(128)S(1)}, s32[64]{0:T(128)}, u32[]{:S(2)}) copy-start(s32[64]{0:T(128)} %param.30) | copy-start | bytes 772
  461.0 6.7 %copy-start = (bf16[16,1024,256]{2,1,0:T(8,128)(2,1)S(1)}, bf16[16,1024,256]{2,1,0:T(8,128)(2,1)}, u32[]{:S(2)}) copy-start(bf16[16,1024,256]{2,1,0:T(8,128)(2,1)} %get-tuple-element.82) | copy-start | bytes 25165828
  472.9 3.9 copy-start.2
  472.9 4.7 copy-start.1

commit v7 on v6

--- a/solution.py
+++ b/solution.py
@@ -577,7 +577,7 @@
         sent.append(sib[mask, slot])
 
     if fused:
-        words, states, log_totals, grad_logp, targets = more
+        words, states, log_totals, grad_logp, ids_all = more
         if masks:
             move_sems, refs = refs[0], refs[1:]
         logits, held, grads, acc, held_sems = refs
@@ -625,7 +625,8 @@
             load(step + 1)
         loads[step].wait()
         row, slot = flip(block, mask), step % 2
-        target, log_total, scale = targets[row], log_totals[row], grad_logp[row]
+        target = ids_all[row, 1:2] - (place * total + block) * part
+        log_total, scale = log_totals[pl.ds(row, 1), :], grad_logp[pl.ds(row, 1), :]
 
         def body(turn, carry):
             start = pl.multiple_of(turn * chunk, chunk)
@@ -904,7 +905,8 @@
 
 
 class Small(typing.NamedTuple):
-    ids: typing.Any
+    answers: typing.Any
+    counted: typing.Any
     segment_row: typing.Any
     segment_column: typing.Any
     gain_self: typing.Any
@@ -944,7 +946,7 @@
     )
     load_sems, keep_sems, ids_sems, ids_local, move_sems = refs[:5]
     buffers, refs = [refs[5:10], refs[10:15], refs[15:20]], refs[20:]
-    normed, hops, staged, sends, recvs, staged_sems, stage_sems = refs
+    normed, hops, staged, sends, recvs, staged_sems, stage_sems, ids = refs
     small, kept = Small(*small), Kept(*kept)
     block, place = lax.axis_index("dp"), lax.axis_index("mp")
     near, far = (block, flip(place, 1)), (block, flip(place, 2))
@@ -975,14 +977,16 @@
         for index in indices:
             saves[index].start()
 
+    for index, source in enumerate((small.segment_row, small.answers, small.counted)):
+        ids[index : index + 1] = source[...]
     greet([near, far] + [(flip(block, mask), place) for mask in range(1, total)])
     moved = table_copies((4, 5, 6, 7, 1, 2, 3, 0), False, table[0], kept.words, move_sems)
-    ids_copies = [pltpu.make_async_copy(small.ids, ids_all.at[block], ids_local)]
+    ids_copies = [pltpu.make_async_copy(ids, ids_all.at[block], ids_local)]
     ids_copies[0].start()
     for mask in range(1, total):
         ids_copies.append(
             remote(
-                small.ids, ids_all.at[block], ids_sems.at[0, mask], ids_sems.at[1, mask],
+                ids, ids_all.at[block], ids_sems.at[0, mask], ids_sems.at[1, mask],
                 (flip(block, mask), place),
             )
         )
@@ -1250,7 +1254,7 @@
     out_shape = list(kept) + [
         full(total, words, rows),
         full(3, total, rows),
-        jax.ShapeDtypeStruct((total,) + small.ids.shape, small.ids.dtype),
+        jax.ShapeDtypeStruct((total, 3, rows), jnp.int32),
     ]
     outcome = pl.pallas_call(
         functools.partial(layer_kernel, total),
@@ -1269,6 +1273,7 @@
             pltpu.VMEM((stages, 3, total, rows), jnp.float32),
             DMA((2,)),
             DMA((2, stages)),
+            pltpu.VMEM((3, rows), jnp.int32),
         ],
         compiler_params=pltpu.CompilerParams(
             collective_id=number, has_side_effects=True, vmem_limit_bytes=62 * 2**20
@@ -1867,7 +1872,6 @@
     vocab_local = embedding.shape[0]
     part = vocab_local // total
     offset = lax.axis_index("mp") * vocab_local + lax.axis_index("dp") * part
-    ids = jnp.concatenate([segment_ids, answer_ids, loss_mask], axis=0)
     norms = (gain_self, shift_self, gain_cross, shift_cross, gain_feed, shift_feed)
     if direct:
         kept, logits, totals, ids_all = layer_forward(
@@ -1876,7 +1880,8 @@
                 cross_value, cross_query, cross_out, feed_up, feed_down,
             ),
             Small(
-                ids, segment_ids.reshape(1, -1), segment_ids.reshape(-1, 1),
+                answer_ids.reshape(1, -1), loss_mask.reshape(1, -1),
+                segment_ids.reshape(1, -1), segment_ids.reshape(-1, 1),
                 *(vector.reshape(1, -1) for vector in norms),
             ),
             embedding,
@@ -1886,14 +1891,14 @@
     else:
         words = spread_rows(embedding)
         kept, logits, totals, ids_all = layer_apart(
-            tokens, memory, segment_ids, ids, offset, words, self_query, self_key, self_value,
+            tokens, memory, segment_ids,
+            jnp.concatenate([segment_ids, answer_ids, loss_mask], axis=0), offset, words, self_query, self_key, self_value,
             self_out, cross_query, cross_key, cross_value, cross_out, feed_up, feed_down, *norms,
         )
     segments_all, answers_all, kept_all = (
         ids_all[:, kind * row_count : (kind + 1) * row_count].reshape(-1, row_len)
         for kind in range(3)
     )
-    targets = (answers_all - offset)[:, None, :]
     log_total = totals[0] + jnp.log(totals[1])
     picked = totals[2]
     keeper = kept_all.astype(jnp.float32)
@@ -1917,13 +1922,15 @@
     loss, pullback = jax.vjp(marginal, doc_scores, likely_all)
     grad_scores, grad_likely = pullback(jnp.ones_like(loss))
     per_segment = grad_likely.reshape(counts.shape) / jnp.maximum(counts, 1.0)
-    grad_logp = (jnp.sum(seg_hot * per_segment[:, None, :], axis=2) * keeper)[:, None, :]
-    log_total = log_total[:, None, :]
+    grad_logp = jnp.sum(seg_hot * per_segment[:, None, :], axis=2) * keeper
     if direct:
-        head_values = (logits, words, kept.states, log_total, grad_logp, targets)
+        head_values = (logits, words, kept.states, log_total, grad_logp, ids_all)
     else:
+        targets = (answers_all - offset)[:, None, :]
         hot = (targets == jnp.arange(part, dtype=jnp.int32)[None, :, None]).astype(jnp.float32)
-        grad_logits = (grad_logp * (hot - jnp.exp(logits - log_total))).astype(jnp.bfloat16)
+        grad_logits = (
+            grad_logp[:, None, :] * (hot - jnp.exp(logits - log_total[:, None, :]))
+        ).astype(jnp.bfloat16)
         parts = jnp.einsum(
             "rvt,vd->rtd", grad_logits, words, preferred_element_type=jnp.float32
         ).astype(jnp.bfloat16)

time: 487 us -> 485 us (level)
  no operation moved by 1% of the time
where the time goes in v7:
time: 485 us; the launch traced here: 478 us
  Pallas kernels  445 us (92%)
  other arithmetic  20.2 us (4%)
  local copies, waits for them, and re-layouts  9.57 us (2%)
    pallas_call x1, Pallas kernels, layer_back(): pl.pallas_call(functools.partial(layer_back_kernel, total, orders, plans_...  222 us
    pallas_call x1, Pallas kernels, layer_forward(): pl.pallas_call(functools.partial(layer_kernel, total), out_shape=out_shap...  143 us
    pallas_call x1, Pallas kernels, head_back(): pl.pallas_call(functools.partial(head_back_kernel, total, tuple(masks), i...  80.2 us

profile of v7, /device:TPU:0, one launch (start us, length us, event | category | flops | bytes accessed | tf_op | source)
XLA Modules:
  0.0 478.4 jit_solution(13176131672978228126)
XLA Ops:
  0.7 0.7 reduce_max.19
  1.4 0.7 exponential_reduce_fusion
  2.1 0.7 eq.68
  2.9 1.5 copy.54.refs_15_.refs_34_
  4.4 143.2 %shard_map.391 = (bf16[512,256]{1,0:T(8,128)(2,1)}, bf16[512,256]{1,0:T(8,128)(2,1)}, bf16[512,256]{1,0:T(8,128)(2,1)}, f32[4,512]{1,0:T(4,128)}, bf16[512,256]{...) custom-call(bf16[512,1024]{1,0:T(8,128)(2,1)} %refs_23_.1, ...), custom_call_target="tpu_custom_call" | custom-call | tf_op jit(solution)/shard_map/pallas_call | solution.py:1259
  147.6 0.9 slice.63
  148.5 0.9 copy.55
  149.3 1.4 fusion.6
  151.3 0.6 fusion.12
  152.6 0.6 multiply_add_fusion.1
  153.4 0.4 fusion.3
  153.9 0.6 fusion.14.refs_6_
  154.5 80.2 %shard_map.392 = (bf16[4,128,1024]{2,1,0:T(8,128)(2,1)}, f32[128,1024]{1,0:T(8,128)}, f32[2,1024]{1,0:T(2,128)}, bf16[1600,1024]{1,0:T(8,128)(2,1)}, bf16[12800,128]{1,0:T(8,128)(2,1)}) custom-call(f32[8,1600,512]{2,1,0:T(8,128)} %get-tuple-element.55.refs_0_, f32[128,1024]{1,0:T(8,128)} %get-tuple-element.56.refs_1_, f32[1,1024]{1,0:T(1,128)} %bitcast.96, ...), custom_call_target="tpu_custom_call" | custom-call | tf_op jit(solution)/shard_map/pallas_call | solution.py:806
  234.7 221.6 %shard_map.393 = (bf16[16,1024,256]{2,1,0:T(8,128)(2,1)}, f32[6,1024]{1,0:T(8,128)}, f32[512,256]{1,0:T(8,128)}, f32[1024,256]{1,0:T(8,128)}, bf16[12800,128]{1,0:T(8,128)(2,1)}) custom-call(bf16[512,1024]{1,0:T(8,128)(2,1)} %bitcast.93, bf16[1024,1024]{1,0:T(8,128)(2,1)} %refs_1_.3, ...), custom_call_target="tpu_custom_call", output_to_operand_aliasing={{4}: (36, {})} | custom-call | tf_op jit(solution)/shard_map/pallas_call | solution.py:1741
  456.4 1.7 fusion.18
  458.1 5.1 %convert_element_type.118 = f32[12800,128]{1,0:T(8,128)} convert(bf16[12800,128]{1,0:T(8,128)(2,1)} %get-tuple-element.84) | non-fusion elementwise | flops 1638400 | bytes 9830400 | tf_op jit(solution)/shard_map/convert_element_type | solution.py:1992
  463.2 1.6 copy-done
  464.8 2.8 slice_bitcast_fusion.3
  467.7 1.1 pad_maximum_fusion.1
  468.8 1.1 pad_maximum_fusion
  469.9 2.6 maximum_convert_fusion.1
  472.5 2.6 maximum_convert_fusion
  475.1 0.8 copy.65
  475.9 1.0 copy.66
  (28 shorter events, 1.2 us)
Async XLA Ops:
  4.4 146.7 %copy-start.3 = (f32[16,4]{0,1:T(4,128)S(1)}, f32[16,4]{0,1:T(4,128)}, u32[]{:S(2)}) copy-start(f32[16,4]{0,1:T(4,128)} %param.29) | copy-start | bytes 772
  4.4 148.9 %copy-start.4 = (s32[64]{0:T(128)S(1)}, s32[64]{0:T(128)}, u32[]{:S(2)}) copy-start(s32[64]{0:T(128)} %param.30) | copy-start | bytes 772
  458.1 6.7 %copy-start = (bf16[16,1024,256]{2,1,0:T(8,128)(2,1)S(1)}, bf16[16,1024,256]{2,1,0:T(8,128)(2,1)}, u32[]{:S(2)}) copy-start(bf16[16,1024,256]{2,1,0:T(8,128)(2,1)} %get-tuple-element.82) | copy-start | bytes 25165828
  472.5 2.6 copy-start.2
  472.5 3.4 copy-start.1

commit v8 on v7

--- a/solution.py
+++ b/solution.py
@@ -1160,7 +1160,7 @@
 
     spread([2])
     nearest = len(sent) - 1
-    lag = 3
+    lag = 2
     for step in range(total + lag):
         if step < total:
             arrive(step)

time: 485 us -> 490 us (1.010)
  Pallas kernels: 445 us -> 451 us
    pallas_call x1, Pallas kernels: 143 us -> 151 us  [layer_forward(): pl.pallas_call(functools.partial(layer_kernel, total), out_shape=out_shap...]
where the time goes in v8:
time: 490 us; the launch traced here: 484 us
  Pallas kernels  451 us (92%)
  other arithmetic  20.2 us (4%)
  local copies, waits for them, and re-layouts  9.57 us (2%)
    pallas_call x1, Pallas kernels, layer_back(): pl.pallas_call(functools.partial(layer_back_kernel, total, orders, plans_...  222 us
    pallas_call x1, Pallas kernels, layer_forward(): pl.pallas_call(functools.partial(layer_kernel, total), out_shape=out_shap...  151 us
    pallas_call x1, Pallas kernels, head_back(): pl.pallas_call(functools.partial(head_back_kernel, total, tuple(masks), i...  78.1 us

profile of v8, /device:TPU:0, one launch (start us, length us, event | category | flops | bytes accessed | tf_op | source)
XLA Modules:
  0.0 484.1 jit_solution(16675964780818075248)
XLA Ops:
  0.7 0.7 reduce_max.19
  1.4 0.7 exponential_reduce_fusion
  2.1 0.7 eq.68
  2.9 1.5 copy.54.refs_15_.refs_34_
  4.4 150.5 %shard_map.391 = (bf16[512,256]{1,0:T(8,128)(2,1)}, bf16[512,256]{1,0:T(8,128)(2,1)}, bf16[512,256]{1,0:T(8,128)(2,1)}, f32[4,512]{1,0:T(4,128)}, bf16[512,256]{...) custom-call(bf16[512,1024]{1,0:T(8,128)(2,1)} %refs_23_.1, ...), custom_call_target="tpu_custom_call" | custom-call | tf_op jit(solution)/shard_map/pallas_call | solution.py:1259
  155.0 0.9 slice.63
  155.8 0.9 copy.55
  156.7 1.4 fusion.6
  158.6 0.6 fusion.12
  159.9 0.6 multiply_add_fusion.1
  160.7 0.4 fusion.3
  161.3 0.6 fusion.14.refs_6_
  161.9 78.1 %shard_map.392 = (bf16[4,128,1024]{2,1,0:T(8,128)(2,1)}, f32[128,1024]{1,0:T(8,128)}, f32[2,1024]{1,0:T(2,128)}, bf16[1600,1024]{1,0:T(8,128)(2,1)}, bf16[12800,128]{1,0:T(8,128)(2,1)}) custom-call(f32[8,1600,512]{2,1,0:T(8,128)} %get-tuple-element.55.refs_0_, f32[128,1024]{1,0:T(8,128)} %get-tuple-element.56.refs_1_, f32[1,1024]{1,0:T(1,128)} %bitcast.96, ...), custom_call_target="tpu_custom_call" | custom-call | tf_op jit(solution)/shard_map/pallas_call | solution.py:806
  240.0 222.0 %shard_map.393 = (bf16[16,1024,256]{2,1,0:T(8,128)(2,1)}, f32[6,1024]{1,0:T(8,128)}, f32[512,256]{1,0:T(8,128)}, f32[1024,256]{1,0:T(8,128)}, bf16[12800,128]{1,0:T(8,128)(2,1)}) custom-call(bf16[512,1024]{1,0:T(8,128)(2,1)} %bitcast.93, bf16[1024,1024]{1,0:T(8,128)(2,1)} %refs_1_.3, ...), custom_call_target="tpu_custom_call", output_to_operand_aliasing={{4}: (36, {})} | custom-call | tf_op jit(solution)/shard_map/pallas_call | solution.py:1741
  462.0 1.7 fusion.18
  463.7 5.1 %convert_element_type.118 = f32[12800,128]{1,0:T(8,128)} convert(bf16[12800,128]{1,0:T(8,128)(2,1)} %get-tuple-element.84) | non-fusion elementwise | flops 1638400 | bytes 9830400 | tf_op jit(solution)/shard_map/convert_element_type | solution.py:1992
  468.8 1.6 copy-done
  470.4 2.8 slice_bitcast_fusion.3
  473.3 1.1 pad_maximum_fusion.1
  474.5 1.1 pad_maximum_fusion
  475.6 2.6 maximum_convert_fusion.1
  478.2 2.6 maximum_convert_fusion
  480.7 0.8 copy.65
  481.5 1.0 copy.66
  (28 shorter events, 1.2 us)
Async XLA Ops:
  4.4 154.1 %copy-start.3 = (f32[16,4]{0,1:T(4,128)S(1)}, f32[16,4]{0,1:T(4,128)}, u32[]{:S(2)}) copy-start(f32[16,4]{0,1:T(4,128)} %param.29) | copy-start | bytes 772
  4.4 156.3 %copy-start.4 = (s32[64]{0:T(128)S(1)}, s32[64]{0:T(128)}, u32[]{:S(2)}) copy-start(s32[64]{0:T(128)} %param.30) | copy-start | bytes 772
  463.7 6.7 %copy-start = (bf16[16,1024,256]{2,1,0:T(8,128)(2,1)S(1)}, bf16[16,1024,256]{2,1,0:T(8,128)(2,1)}, u32[]{:S(2)}) copy-start(bf16[16,1024,256]{2,1,0:T(8,128)(2,1)} %get-tuple-element.82) | copy-start | bytes 25165828
  478.1 2.6 copy-start.2
  478.2 3.4 copy-start.1
